TPU v7x, 32 devices: a whole 2x2x4 slice. The times are simulated.
32 devices in a mesh: dp: 16 (over z, y, core), tensor: 2 (over x).
Axes of the slice: x: 2, y: 2, z: 4, core: 2. Of those that a mesh axis runs over, the one named last changes fastest.
Arguments:
- tokens: bfloat16 [32768, 1024], P(('dp', 'tensor')), may hold values from -6 to 6
- segment_ids: int32 [16, 2048], P('dp'), may hold values from 0 to 7, never falling along the last dimension, each value on 1 to 800 neighbouring positions
- key_mask: int32 [16, 2048], P('dp'), may hold values 0 or 1
- owners: int32 [48, 1], replicated, may hold values from 0 to 15; in each aligned block of 48 rows (0 to 47, 48 to 95, ...) at most 6 rows name the same one
- master_slots: float32 [2, 96, 128, 1024], P('tensor', 'dp'), may hold values from -0.25 to 0.25
- slot_first: float32 [2, 96, 128, 1024], P('tensor', 'dp'), may hold values from -384 to 384
- slot_second: float32 [2, 96, 128, 1024], P('tensor', 'dp'), may hold values from 2048 to 16384
- vectors: float32 [12, 1024], replicated, may hold values from -0.8 to 1.65, as said below
- vector_first: float32 [12, 1024], replicated, may hold values from -384 to 384
- vector_second: float32 [12, 1024], replicated, may hold values from 2048 to 16384
- out_grad: bfloat16 [32768, 1024], P(('dp', 'tensor')), may hold values from -6 to 6
Outputs:
- layer_out: bfloat16 [32768, 1024], P(('dp', 'tensor'))
- input_grad: bfloat16 [32768, 1024], P(('dp', 'tensor'))
- slot_new: float32 [2, 96, 128, 1024], P('tensor', 'dp')
- slot_first_new: float32 [2, 96, 128, 1024], P('tensor', 'dp')
- slot_second_new: float32 [2, 96, 128, 1024], P('tensor', 'dp')
- vector_new: float32 [12, 1024], replicated
- vector_first_new: float32 [12, 1024], replicated
- vector_second_new: float32 [12, 1024], replicated
Inputs may be any that keep to these rules, and one draw needn't show every extreme that they name: `owners`: no owner holds more than 6 pieces, and some owner holds exactly 6. `segment_ids`: within a sequence the numbers never fall; a document has 1 to 800 tokens, one exactly 800. `vectors`: rows 8 and 10 are positive.
All inputs are finite; a program needn't handle non-finite values. No bound on the sum of `key_mask` on one device may be relied on, other than what follows from the above.
Results may differ from a plain program's by a relative error of at most 0.025.
Values may be sent and summed in bfloat16 or wider, within the bound.
A program may use at most 384 MiB of HBM per device.

v0:
```python
import jax
import jax.numpy as jnp
from jax import lax
from jax.sharding import PartitionSpec as P

D = 1024
HD = 64
FF = 4096
QBLK = 512
STEP = 10
CAP = 6


norm_eps = 1e-05
mask_fill = -1000000000.0
beta_one = 0.5
beta_two = 0.5
rate_matrix = 0.03
rate_vector = 0.1
weight_decay = 0.01
adam_eps = 1e-08


def slot_index(owners):
    owner_of = owners[:, 0]
    positions = jnp.arange(owner_of.shape[0], dtype=jnp.int32)
    earlier = (positions[None, :] < positions[:, None]) & (owner_of[None, :] == owner_of[:, None])
    within = jnp.sum(earlier.astype(jnp.int32), axis=1)
    return owner_of * CAP + within


def layer_stats(residual):
    center = residual - jnp.mean(residual, axis=-1, keepdims=True)
    spread = jnp.mean(center * center, axis=-1, keepdims=True)
    inverse = lax.rsqrt(spread + norm_eps)
    return (center * inverse, inverse)


def norm_back(grads, normal, inverse, gains):
    scaled = grads * gains
    return inverse * (
        scaled
        - jnp.mean(scaled, axis=-1, keepdims=True)
        - normal * jnp.mean(scaled * normal, axis=-1, keepdims=True)
    )


def gelu_exact(values):
    return jax.nn.gelu(values, approximate=False)


def block_mask(segment, valid, start):
    length = segment.shape[0]
    query_pos = start + jnp.arange(QBLK, dtype=jnp.int32)
    key_pos = jnp.arange(length, dtype=jnp.int32)
    query_seg = lax.dynamic_slice_in_dim(segment, start, QBLK, 0)
    same = query_seg[:, None] == segment[None, :]
    return same & ((valid[None, :] == 1) | (query_pos[:, None] == key_pos[None, :]))


def block_scores(block_q, key_rows, segment, valid, start):
    scores = jnp.einsum("qhd,khd->hqk", block_q, key_rows, preferred_element_type=jnp.float32)
    return jnp.where(block_mask(segment, valid, start)[None], scores, mask_fill)


def attend_forward(queries, key_rows, value_rows, segment, valid):
    length = queries.shape[0]

    def one_block(index):
        start = index * QBLK
        block_q = lax.dynamic_slice_in_dim(queries, start, QBLK, 0)
        scores = block_scores(block_q, key_rows, segment, valid, start)
        row_max = jnp.max(scores, axis=2, keepdims=True)
        raised = jnp.exp(scores - row_max)
        totals = jnp.sum(raised, axis=2, keepdims=True)
        weights = (raised / totals).astype(jnp.bfloat16)
        context = jnp.einsum(
            "hqk,khd->qhd", weights, value_rows, preferred_element_type=jnp.float32
        )
        return (context, (row_max + jnp.log(totals))[:, :, 0])

    context, log_sums = lax.map(one_block, jnp.arange(length // QBLK, dtype=jnp.int32))
    return (context.reshape(length, -1), log_sums)


def attend_backward(queries, key_rows, value_rows, segment, valid, log_sums, grad_context):
    length = queries.shape[0]

    def one_block(carry, index):
        key_acc, value_acc = carry
        start = index * QBLK
        block_q = lax.dynamic_slice_in_dim(queries, start, QBLK, 0)
        block_g = lax.dynamic_slice_in_dim(grad_context, start, QBLK, 0)
        scores = block_scores(block_q, key_rows, segment, valid, start)
        weights = jnp.exp(scores - log_sums[index][:, :, None])
        value_acc = value_acc + jnp.einsum(
            "hqk,qhd->khd",
            weights.astype(jnp.bfloat16),
            block_g,
            preferred_element_type=jnp.float32,
        )
        grad_weights = jnp.einsum(
            "qhd,khd->hqk", block_g, value_rows, preferred_element_type=jnp.float32
        )
        inner = jnp.sum(weights * grad_weights, axis=2, keepdims=True)
        grad_scores = (weights * (grad_weights - inner)).astype(jnp.bfloat16)
        grad_q = jnp.einsum(
            "hqk,khd->qhd", grad_scores, key_rows, preferred_element_type=jnp.float32
        )
        key_acc = key_acc + jnp.einsum(
            "hqk,qhd->khd", grad_scores, block_q, preferred_element_type=jnp.float32
        )
        return ((key_acc, value_acc), grad_q)

    zeros_kv = jnp.zeros(key_rows.shape, jnp.float32)
    (grad_keys, grad_values), grad_queries = lax.scan(
        one_block, (zeros_kv, zeros_kv), jnp.arange(length // QBLK, dtype=jnp.int32)
    )
    return (
        grad_queries.reshape(length, -1),
        grad_keys.reshape(length, -1),
        grad_values.reshape(length, -1),
    )


def adam_update(weights, first, second, grads, rate, decay):
    first_new = beta_one * first + (1.0 - beta_one) * grads
    second_new = beta_two * second + (1.0 - beta_two) * grads * grads
    first_hat = first_new / (1.0 - beta_one**STEP)
    second_hat = second_new / (1.0 - beta_two**STEP)
    updated = weights - rate * (first_hat / (jnp.sqrt(second_hat) + adam_eps) + decay * weights)
    return (updated, first_new, second_new)


def on_device(
    tokens,
    segment_ids,
    key_mask,
    owners,
    master_slots,
    slot_first,
    slot_second,
    vectors,
    vector_first,
    vector_second,
    out_grad,
):
    n_tensor = lax.axis_size("tensor")
    group = lax.axis_index("tensor")
    head_cols = D // n_tensor
    unit_cols = FF // n_tensor
    heads_here = head_cols // HD
    seq_count = segment_ids.shape[0]
    length = segment_ids.shape[1]
    query_scale = HD ** (-0.5)
    slots = slot_index(owners)
    gathered_slots = lax.all_gather(master_slots[0].astype(jnp.bfloat16), "dp", axis=0, tiled=True)
    stack = jnp.take(gathered_slots, slots, axis=0).reshape(-1, D)
    w_mix = stack[0 : 3 * head_cols]
    w_out = stack[3 * head_cols : 4 * head_cols]
    w_up = stack[4 * head_cols : 4 * head_cols + unit_cols]
    w_down = stack[4 * head_cols + unit_cols :]
    bias_query = lax.dynamic_slice_in_dim(vectors[0], group * head_cols, head_cols, 0)
    bias_value = lax.dynamic_slice_in_dim(vectors[1], group * head_cols, head_cols, 0)
    bias_up = lax.dynamic_slice_in_dim(vectors[2:6].reshape(FF), group * unit_cols, unit_cols, 0)
    gathered = lax.all_gather(tokens, "tensor", axis=0, tiled=True)
    mixed = jnp.einsum("ld,kd->lk", gathered, w_mix, preferred_element_type=jnp.float32)
    queries = ((mixed[:, :head_cols] + bias_query) * query_scale).astype(jnp.bfloat16)
    key_rows = mixed[:, head_cols : 2 * head_cols].astype(jnp.bfloat16)
    value_rows = (mixed[:, 2 * head_cols :] + bias_value).astype(jnp.bfloat16)
    head_shape = (seq_count, length, heads_here, HD)
    queries_h = queries.reshape(head_shape)
    keys_h = key_rows.reshape(head_shape)
    values_h = value_rows.reshape(head_shape)

    def forward_seq(element):
        return attend_forward(element[0], element[1], element[2], element[3], element[4])

    context, log_sums = lax.map(forward_seq, (queries_h, keys_h, values_h, segment_ids, key_mask))
    context = context.reshape(-1, head_cols).astype(jnp.bfloat16)
    attn_sum = lax.psum_scatter(
        jnp.einsum("lk,kd->ld", context, w_out, preferred_element_type=jnp.float32).astype(
            jnp.bfloat16
        ),
        "tensor",
        scatter_dimension=0,
        tiled=True,
    ).astype(jnp.float32)
    residual_one = tokens.astype(jnp.float32) + (attn_sum + vectors[6])
    normal_one, inverse_one = layer_stats(residual_one)
    normed = normal_one * vectors[8] + vectors[9]
    normed_low = normed.astype(jnp.bfloat16)
    norm_rows = lax.all_gather(normed_low, "tensor", axis=0, tiled=True)
    hidden_pre = (
        jnp.einsum("ld,kd->lk", norm_rows, w_up, preferred_element_type=jnp.float32) + bias_up
    )
    hidden_full, gelu_pull = jax.vjp(gelu_exact, hidden_pre)
    hidden = hidden_full.astype(jnp.bfloat16)
    mlp_sum = lax.psum_scatter(
        jnp.einsum("lk,kd->ld", hidden, w_down, preferred_element_type=jnp.float32).astype(
            jnp.bfloat16
        ),
        "tensor",
        scatter_dimension=0,
        tiled=True,
    ).astype(jnp.float32)
    residual_two = normed + (mlp_sum + vectors[7])
    normal_two, inverse_two = layer_stats(residual_two)
    layer_out = (normal_two * vectors[10] + vectors[11]).astype(jnp.bfloat16)
    grad_out = out_grad.astype(jnp.float32)
    grad_two = norm_back(grad_out, normal_two, inverse_two, vectors[10])
    grad_down_in = lax.all_gather(grad_two.astype(jnp.bfloat16), "tensor", axis=0, tiled=True)
    grad_hidden = jnp.einsum("ld,kd->lk", grad_down_in, w_down, preferred_element_type=jnp.float32)
    grad_w_down = jnp.einsum("lk,ld->kd", hidden, grad_down_in, preferred_element_type=jnp.float32)
    grad_pre = gelu_pull(grad_hidden)[0].astype(jnp.bfloat16)
    norm_back_rows = lax.all_gather(normed_low, "tensor", axis=0, tiled=True)
    grad_w_up = jnp.einsum(
        "lk,ld->kd", grad_pre, norm_back_rows, preferred_element_type=jnp.float32
    )
    grad_norm = grad_two + lax.psum_scatter(
        jnp.einsum("lk,kd->ld", grad_pre, w_up, preferred_element_type=jnp.float32).astype(
            jnp.bfloat16
        ),
        "tensor",
        scatter_dimension=0,
        tiled=True,
    ).astype(jnp.float32)
    grad_one = norm_back(grad_norm, normal_one, inverse_one, vectors[8])
    grad_attn_in = lax.all_gather(grad_one.astype(jnp.bfloat16), "tensor", axis=0, tiled=True)
    grad_context = jnp.einsum(
        "ld,kd->lk", grad_attn_in, w_out, preferred_element_type=jnp.float32
    ).astype(jnp.bfloat16)
    grad_w_out = jnp.einsum("lk,ld->kd", context, grad_attn_in, preferred_element_type=jnp.float32)

    def backward_seq(element):
        return attend_backward(
            element[0], element[1], element[2], element[3], element[4], element[5], element[6]
        )

    grad_q, grad_k, grad_v = lax.map(
        backward_seq,
        (
            queries_h,
            keys_h,
            values_h,
            segment_ids,
            key_mask,
            log_sums,
            grad_context.reshape(head_shape),
        ),
    )
    grad_queries = grad_q.reshape(-1, head_cols).astype(jnp.bfloat16) * query_scale
    grad_keys = grad_k.reshape(-1, head_cols).astype(jnp.bfloat16)
    grad_values = grad_v.reshape(-1, head_cols).astype(jnp.bfloat16)
    grad_mix = jnp.concatenate([grad_queries, grad_keys, grad_values], axis=1)
    mix_back_rows = lax.all_gather(tokens, "tensor", axis=0, tiled=True)
    grad_w_mix = jnp.einsum(
        "lk,ld->kd", grad_mix, mix_back_rows, preferred_element_type=jnp.float32
    )
    input_grad = (
        grad_one
        + lax.psum_scatter(
            jnp.einsum("lk,kd->ld", grad_mix, w_mix, preferred_element_type=jnp.float32).astype(
                jnp.bfloat16
            ),
            "tensor",
            scatter_dimension=0,
            tiled=True,
        ).astype(jnp.float32)
    ).astype(jnp.bfloat16)
    query_full = lax.dynamic_update_slice_in_dim(
        jnp.zeros((D,), jnp.float32),
        jnp.sum(grad_queries.astype(jnp.float32), axis=0),
        group * head_cols,
        0,
    )
    value_full = lax.dynamic_update_slice_in_dim(
        jnp.zeros((D,), jnp.float32),
        jnp.sum(grad_values.astype(jnp.float32), axis=0),
        group * head_cols,
        0,
    )
    up_full = lax.dynamic_update_slice_in_dim(
        jnp.zeros((FF,), jnp.float32),
        jnp.sum(grad_pre.astype(jnp.float32), axis=0),
        group * unit_cols,
        0,
    )
    tail_rows = jnp.stack(
        [
            jnp.sum(grad_one, axis=0),
            jnp.sum(grad_two, axis=0),
            jnp.sum(grad_norm * normal_one, axis=0),
            jnp.sum(grad_norm, axis=0),
            jnp.sum(grad_out * normal_two, axis=0),
            jnp.sum(grad_out, axis=0),
        ]
    )
    vector_terms = jnp.concatenate(
        [jnp.stack([query_full, value_full]), up_full.reshape(FF // D, D), tail_rows], axis=0
    )
    vector_grads = lax.psum(vector_terms, ("dp", "tensor"))
    grad_stack = jnp.concatenate([grad_w_mix, grad_w_out, grad_w_up, grad_w_down], axis=0)
    grad_pieces = grad_stack.reshape(slots.shape[0], -1, D)
    spread_slots = (
        jnp.zeros((lax.axis_size("dp") * CAP,) + grad_pieces.shape[1:], jnp.float32)
        .at[slots]
        .set(grad_pieces)
    )
    own_grads = lax.psum_scatter(
        spread_slots.astype(jnp.bfloat16), "dp", scatter_dimension=0, tiled=True
    ).astype(jnp.float32)
    slot_new, slot_first_new, slot_second_new = adam_update(
        master_slots[0], slot_first[0], slot_second[0], own_grads, rate_matrix, weight_decay
    )
    vector_new, vector_first_new, vector_second_new = adam_update(
        vectors, vector_first, vector_second, vector_grads, rate_vector, 0.0
    )
    return (
        layer_out,
        input_grad,
        slot_new[None],
        slot_first_new[None],
        slot_second_new[None],
        vector_new,
        vector_first_new,
        vector_second_new,
    )


def solution(mesh):
    placed = (
        P(("dp", "tensor"), None),
        P("dp", None),
        P("dp", None),
        P(),
        P("tensor", "dp", None, None),
        P("tensor", "dp", None, None),
        P("tensor", "dp", None, None),
        P(),
        P(),
        P(),
        P(("dp", "tensor"), None),
    )
    return jax.shard_map(
        on_device,
        mesh=mesh,
        in_specs=placed,
        out_specs=(
            P(("dp", "tensor"), None),
            P(("dp", "tensor"), None),
            P("tensor", "dp", None, None),
            P("tensor", "dp", None, None),
            P("tensor", "dp", None, None),
            P(),
            P(),
            P(),
        ),
        check_vma=False,
    )
```

profile of v0, /device:TPU:13, one launch (start us, length us, event | category | flops | bytes accessed | tf_op | source)
XLA Modules:
  0.0 1745.1 jit_solution(772397140472765420)
XLA Ops:
  12.8 127.8 %all-gather.6.cloned.1.call-done = bf16[96,128,1024]{2,1,0:T(8,128)(2,1)} async-done(((bf16[6,128,1024]{2,1,0:T(8,128)(2,1)}), bf16[96,128,1024]{2,1,0:T(8,128)(2,1)}) %all-gather.6.cloned.1.call-update) | async-done | bytes 25165840 | tf_op jit(solution)/shard_map/all_gather | solution.py:157
  140.6 15.1 gather_fusion
  167.6 31.2 %all-gather.8.cloned.1.call-done = bf16[2048,1024]{1,0:T(8,128)(2,1)} async-done(((bf16[1024,1024]{1,0:T(8,128)(2,1)}), bf16[2048,1024]{1,0:T(8,128)(2,1)}) %all-gather.8.cloned.1.call-update) | async-done | bytes 4194320 | tf_op jit(solution)/shard_map/all_gather | solution.py:166
  211.8 194.0 %while.47 = (s32[]{:T(128)}, bf16[4,512,8,64]{1,3,2,0:T(8,128)(2,1)}, f32[4,8,512]{2,1,0:T(8,128)}, s32[4]{0:T(128)S(1)}, s32[2048]{0:T(1024)S(1)}, /*index=5*/s...) while((s32[]{:T(128)}, ...), condition=%wide.region_4.5_spmd, body=%wide.region_1.4_spmd.sunk | while | flops 2227173888 | bytes 110786768 | solution.py:82
  214.8 14.5 select_reduce_fusion.2
  229.3 14.6 fusion.122
  243.9 15.8 fusion.123
  263.2 14.5 select_reduce_fusion.2
  277.7 14.6 fusion.122
  292.3 15.8 fusion.123
  311.7 14.5 select_reduce_fusion.2
  326.2 14.6 fusion.122
  340.8 15.8 fusion.123
  360.1 14.5 select_reduce_fusion.2
  374.6 14.6 fusion.122
  389.2 15.8 fusion.123
  416.3 54.4 %reduce-scatter.6.cloned.1.call-done = bf16[1024,1024]{1,0:T(8,128)(2,1)} async-done(((bf16[2048,1024]{1,0:T(8,128)(2,1)}), bf16[1024,1024]{1,0:T(8,128)(2,1)}) %reduce-scatter.6.cloned.1.call-update) | async-done | bytes 2097168 | tf_op jit(solution)/shard_map/reduce_scatter | solution.py:181
  484.7 49.5 %all-gather.10.cloned.1.call-done = bf16[2048,1024]{1,0:T(8,128)(2,1)} async-done(((bf16[1024,1024]{1,0:T(8,128)(2,1)}), bf16[2048,1024]{1,0:T(8,128)(2,1)}) %all-gather.10.cloned.1.call-update) | async-done | bytes 4194320 | tf_op jit(solution)/shard_map/all_gather | solution.py:193
  534.2 49.3 %multiply_convert_fusion.1 = (bf16[2048,2048]{1,0:T(8,128)(2,1)S(1)}, f32[2048,2048]{1,0:T(8,128)}, f32[2048,2048]{1,0:T(8,128)}) fusion(f32[2048]{0:T(1024)S(1)} %dynamic_slice.63, bf16[2048,1024]{1,0:T(8,128)(2,1)} %all-gather.10.cloned.1.call-done, bf16[2048,1024]{1,0:T(8,128)(2,1)} %bitcast.172), kind=kOutput, calls=%fused_computation.53 | convolution fusion | flops 8866758656 | bytes 50339840 | tf_op jit(solution)/shard_map/ld,kd->lk/dot_general | solution.py:195
  597.2 54.4 %reduce-scatter.8.cloned.1.call-done = bf16[1024,1024]{1,0:T(8,128)(2,1)} async-done(((bf16[2048,1024]{1,0:T(8,128)(2,1)}), bf16[1024,1024]{1,0:T(8,128)(2,1)}) %reduce-scatter.8.cloned.1.call-update) | async-done | bytes 2097168 | tf_op jit(solution)/shard_map/reduce_scatter | solution.py:199
  664.4 56.9 %all-gather.12.cloned.1.call-done = bf16[2048,1024]{1,0:T(8,128)(2,1)} async-done(((bf16[1024,1024]{1,0:T(8,128)(2,1)}), bf16[2048,1024]{1,0:T(8,128)(2,1)}) %all-gather.12.cloned.1.call-update) | async-done | bytes 4194320 | tf_op jit(solution)/shard_map/all_gather | solution.py:212
  721.2 23.4 %convert_reduce_fusion = (f32[2048]{0:T(1024)}, bf16[2048,2048]{1,0:T(8,128)(2,1)}) fusion(f32[2048,2048]{1,0:T(8,128)} %get-tuple-element.286, bf16[2048,1024]{1,0:T(8,128)(2,1)} %all-gather.12.cloned.1.call-done, bf16[2048,1024]{1,0:T(8,128)(2,1)} %bitcast.174, f32[2048,2048]{1,0:T(8,128)} %get-tuple-element.309, f32[2048]{0:T(1024)S(1)} %dynamic_slice.63), kind=kOutput, calls=%fused_computation.51 | convolution fusion | flops 8661235712 | bytes 50348032 | tf_op jit(solution)/shard_map/ld,kd->lk/dot_general | solution.py:213
  744.6 13.8 convolution_convert_fusion.1
  758.5 54.4 %reduce-scatter.10.cloned.1.call-done = bf16[1024,1024]{1,0:T(8,128)(2,1)} async-done(((bf16[2048,1024]{1,0:T(8,128)(2,1)}), bf16[1024,1024]{1,0:T(8,128)(2,1)}) %reduce-scatter.10.cloned.1.call-update) | async-done | bytes 2097168 | tf_op jit(solution)/shard_map/reduce_scatter | solution.py:220
  826.3 56.8 %all-gather.14.cloned.1.call-done = bf16[2048,1024]{1,0:T(8,128)(2,1)} async-done(((bf16[1024,1024]{1,0:T(8,128)(2,1)}), bf16[2048,1024]{1,0:T(8,128)(2,1)}) %all-gather.14.cloned.1.call-update) | async-done | bytes 4194320 | tf_op jit(solution)/shard_map/all_gather | solution.py:229
  890.8 439.9 %while.48 = (s32[]{:T(128)}, f32[2048,8,64]{0,2,1:T(8,128)}, f32[2048,8,64]{0,2,1:T(8,128)}, bf16[4,512,8,64]{1,3,2,0:T(8,128)(2,1)}, s32[4]{0:T(128)S(1)}, /*in...) while((s32[]{:T(128)}, f32[2048,8,64]{0,2,1:T(8,128)}, ...), condition=%wide.region_18.19_spmd.clone, body=%wide.region_16.18_spmd.clone.sunk | while | flops 5477759488 | bytes 349321536 | solution.py:116
  897.7 14.3 fusion.133
  911.9 16.5 bitcast_add_fusion.6
  928.5 25.2 %multiply_reduce_fusion.7 = (f32[8,512]{1,0:T(8,128)S(1)}, f32[8,512,2048]{2,1,0:T(8,128)}) fusion(f32[8,512,2048]{2,1,0:T(8,128)} %fusion.133, f32[8,512]{1,0:T(8,128)S(1)} %dynamic-slice_bitcast_fusion.2, pred[512,2048]{1,0:T(8,128)(4,1)} %fusion.134, bf16[2048,8,64]{0,2,1:T(8,128)(2,1)} %get-tuple-element.534, ...), kind=kOutput, calls=%fused_computation.20.clone.1 | convolution fusion | flops 1107292160 | bytes 70811648 | tf_op jit(solution)/shard_map/while/body/eval_jaxpr/while/body/eval_jaxpr/qhd,khd->hqk/dot_general | solution.py:102
  953.7 28.1 %multiply_convert_fusion.3 = bf16[8,512,2048]{2,1,0:T(8,128)(2,1)} fusion(f32[8,512,2048]{2,1,0:T(8,128)} %get-tuple-element.448, f32[8,512,2048]{2,1,0:T(8,128)} %fusion.133, f32[8,512]{1,0:T(8,128)S(1)} %get-tuple-element.449, f32[8,512]{1,0:T(8,128)S(1)} %dynamic-slice_bitcast_fusion.2, pred[512,2048]{1,0:T(8,128)(4,1)} %fusion.134), kind=kLoop, calls=%fused_computation.19.clone.1 | loop fusion | flops 41943040 | bytes 84967424 | tf_op jit(solution)/shard_map/while/body/eval_jaxpr/while/body/eval_jaxpr/convert_element_type | solution.py:106
  1005.2 14.3 fusion.133
  1019.5 18.3 %bitcast_add_fusion.6 = f32[2048,8,64]{0,2,1:T(8,128)} fusion(f32[2048,8,64]{0,2,1:T(8,128)} %get-tuple-element.508, f32[8,512,2048]{2,1,0:T(8,128)} %fusion.133, f32[8,512]{1,0:T(8,128)S(1)} %dynamic-slice_bitcast_fusion.2, pred[512,2048]{1,0:T(8,128)(4,1)} %fusion.134, pred[]{:T(512)S(6)} %compare.3, bf16[2048,8,64]{0,2,1:T(8,128)(2,1)} %get-tuple-element.533, ...), kind=kOutput, calls=%fused_computation.27.clone.1 | convolution fusion | flops 1101004800 | bytes 43532292 | tf_op jit(solution)/shard_map/while/body/eval_jaxpr/while/body/eval_jaxpr/hqk,qhd->khd/dot_general | solution.py:96
  1037.8 25.2 %multiply_reduce_fusion.7 = (f32[8,512]{1,0:T(8,128)S(1)}, f32[8,512,2048]{2,1,0:T(8,128)}) fusion(f32[8,512,2048]{2,1,0:T(8,128)} %fusion.133, f32[8,512]{1,0:T(8,128)S(1)} %dynamic-slice_bitcast_fusion.2, pred[512,2048]{1,0:T(8,128)(4,1)} %fusion.134, bf16[2048,8,64]{0,2,1:T(8,128)(2,1)} %get-tuple-element.534, ...), kind=kOutput, calls=%fused_computation.20.clone.1 | convolution fusion | flops 1107292160 | bytes 70811648 | tf_op jit(solution)/shard_map/while/body/eval_jaxpr/while/body/eval_jaxpr/qhd,khd->hqk/dot_general | solution.py:102
  1063.0 28.1 %multiply_convert_fusion.3 = bf16[8,512,2048]{2,1,0:T(8,128)(2,1)} fusion(f32[8,512,2048]{2,1,0:T(8,128)} %get-tuple-element.448, f32[8,512,2048]{2,1,0:T(8,128)} %fusion.133, f32[8,512]{1,0:T(8,128)S(1)} %get-tuple-element.449, f32[8,512]{1,0:T(8,128)S(1)} %dynamic-slice_bitcast_fusion.2, pred[512,2048]{1,0:T(8,128)(4,1)} %fusion.134), kind=kLoop, calls=%fused_computation.19.clone.1 | loop fusion | flops 41943040 | bytes 84967424 | tf_op jit(solution)/shard_map/while/body/eval_jaxpr/while/body/eval_jaxpr/convert_element_type | solution.py:106
  1115.8 14.3 fusion.133
  1130.1 18.3 %bitcast_add_fusion.6 = f32[2048,8,64]{0,2,1:T(8,128)} fusion(f32[2048,8,64]{0,2,1:T(8,128)} %get-tuple-element.508, f32[8,512,2048]{2,1,0:T(8,128)} %fusion.133, f32[8,512]{1,0:T(8,128)S(1)} %dynamic-slice_bitcast_fusion.2, pred[512,2048]{1,0:T(8,128)(4,1)} %fusion.134, pred[]{:T(512)S(6)} %compare.3, bf16[2048,8,64]{0,2,1:T(8,128)(2,1)} %get-tuple-element.533, ...), kind=kOutput, calls=%fused_computation.27.clone.1 | convolution fusion | flops 1101004800 | bytes 43532292 | tf_op jit(solution)/shard_map/while/body/eval_jaxpr/while/body/eval_jaxpr/hqk,qhd->khd/dot_general | solution.py:96
  1148.4 25.2 %multiply_reduce_fusion.7 = (f32[8,512]{1,0:T(8,128)S(1)}, f32[8,512,2048]{2,1,0:T(8,128)}) fusion(f32[8,512,2048]{2,1,0:T(8,128)} %fusion.133, f32[8,512]{1,0:T(8,128)S(1)} %dynamic-slice_bitcast_fusion.2, pred[512,2048]{1,0:T(8,128)(4,1)} %fusion.134, bf16[2048,8,64]{0,2,1:T(8,128)(2,1)} %get-tuple-element.534, ...), kind=kOutput, calls=%fused_computation.20.clone.1 | convolution fusion | flops 1107292160 | bytes 70811648 | tf_op jit(solution)/shard_map/while/body/eval_jaxpr/while/body/eval_jaxpr/qhd,khd->hqk/dot_general | solution.py:102
  1173.6 28.1 %multiply_convert_fusion.3 = bf16[8,512,2048]{2,1,0:T(8,128)(2,1)} fusion(f32[8,512,2048]{2,1,0:T(8,128)} %get-tuple-element.448, f32[8,512,2048]{2,1,0:T(8,128)} %fusion.133, f32[8,512]{1,0:T(8,128)S(1)} %get-tuple-element.449, f32[8,512]{1,0:T(8,128)S(1)} %dynamic-slice_bitcast_fusion.2, pred[512,2048]{1,0:T(8,128)(4,1)} %fusion.134), kind=kLoop, calls=%fused_computation.19.clone.1 | loop fusion | flops 41943040 | bytes 84967424 | tf_op jit(solution)/shard_map/while/body/eval_jaxpr/while/body/eval_jaxpr/convert_element_type | solution.py:106
  1226.4 14.3 fusion.133
  1240.7 18.3 %bitcast_add_fusion.6 = f32[2048,8,64]{0,2,1:T(8,128)} fusion(f32[2048,8,64]{0,2,1:T(8,128)} %get-tuple-element.508, f32[8,512,2048]{2,1,0:T(8,128)} %fusion.133, f32[8,512]{1,0:T(8,128)S(1)} %dynamic-slice_bitcast_fusion.2, pred[512,2048]{1,0:T(8,128)(4,1)} %fusion.134, pred[]{:T(512)S(6)} %compare.3, bf16[2048,8,64]{0,2,1:T(8,128)(2,1)} %get-tuple-element.533, ...), kind=kOutput, calls=%fused_computation.27.clone.1 | convolution fusion | flops 1101004800 | bytes 43532292 | tf_op jit(solution)/shard_map/while/body/eval_jaxpr/while/body/eval_jaxpr/hqk,qhd->khd/dot_general | solution.py:96
  1259.0 25.2 %multiply_reduce_fusion.7 = (f32[8,512]{1,0:T(8,128)S(1)}, f32[8,512,2048]{2,1,0:T(8,128)}) fusion(f32[8,512,2048]{2,1,0:T(8,128)} %fusion.133, f32[8,512]{1,0:T(8,128)S(1)} %dynamic-slice_bitcast_fusion.2, pred[512,2048]{1,0:T(8,128)(4,1)} %fusion.134, bf16[2048,8,64]{0,2,1:T(8,128)(2,1)} %get-tuple-element.534, ...), kind=kOutput, calls=%fused_computation.20.clone.1 | convolution fusion | flops 1107292160 | bytes 70811648 | tf_op jit(solution)/shard_map/while/body/eval_jaxpr/while/body/eval_jaxpr/qhd,khd->hqk/dot_general | solution.py:102
  1284.2 28.1 %multiply_convert_fusion.3 = bf16[8,512,2048]{2,1,0:T(8,128)(2,1)} fusion(f32[8,512,2048]{2,1,0:T(8,128)} %get-tuple-element.448, f32[8,512,2048]{2,1,0:T(8,128)} %fusion.133, f32[8,512]{1,0:T(8,128)S(1)} %get-tuple-element.449, f32[8,512]{1,0:T(8,128)S(1)} %dynamic-slice_bitcast_fusion.2, pred[512,2048]{1,0:T(8,128)(4,1)} %fusion.134), kind=kLoop, calls=%fused_computation.19.clone.1 | loop fusion | flops 41943040 | bytes 84967424 | tf_op jit(solution)/shard_map/while/body/eval_jaxpr/while/body/eval_jaxpr/convert_element_type | solution.py:106
  1348.4 12.8 fusion.72
  1399.0 16.3 broadcast_in_dim.98
  1415.3 45.1 %scatter_fusion = f32[96,128,1024]{2,1,0:T(8,128)} fusion(f32[96,128,1024]{2,1,0:T(8,128)} %broadcast_in_dim.98, s32[48]{0:T(128)S(1)} %bitcast.218, f32[48,128,1024]{2,1,0:T(8,128)} %bitcast.166), kind=kCustom, calls=%fused_computation.1 | custom fusion | bytes 75497664 | tf_op jit(solution)/shard_map/scatter | solution.py:308
  1460.4 26.0 %convert_element_type.147 = bf16[96,128,1024]{2,1,0:T(8,128)(2,1)} convert(f32[96,128,1024]{2,1,0:T(8,128)} %scatter_fusion) | non-fusion elementwise | flops 12582912 | bytes 75497472 | tf_op jit(solution)/shard_map/convert_element_type | solution.py:311
  1487.6 39.7 %psum.7 = f32[12,1024]{1,0:T(8,128)S(1)} all-reduce(f32[12,1024]{1,0:T(8,128)S(1)} %concatenate.11), channel_id=1, replica_groups=mesh['dp'=16,'tensor'=2] {'dp','tensor'}, use_global_device_ids=true, to_apply=%region_31.32 | all-reduce | flops 12288 | bytes 98304 | tf_op jit(solution)/shard_map/psum | solution.py:302
  1533.5 195.2 %reduce-scatter.14.cloned.1.call-done = bf16[6,128,1024]{2,1,0:T(8,128)(2,1)} async-done(((bf16[96,128,1024]{2,1,0:T(8,128)(2,1)}), bf16[6,128,1024]{2,1,0:T(8,128)(2,1)}) %reduce-scatter.14.cloned.1.call-update) | async-done | bytes 1572880 | tf_op jit(solution)/shard_map/reduce_scatter | solution.py:310
  (266 shorter events, 272.7 us)
Async XLA Ops:
  7.2 4.2 copy-start.53
  7.2 5.0 copy-start.27
  7.2 133.4 %all-gather.6.cloned.1.call-start = ((), (), s32[]{:S(2)}) async-start(), calls=%async_computation.5 | async-start | bytes 26738688 | tf_op jit(solution)/shard_map/all_gather | solution.py:157
  10.5 188.2 %all-gather.8.cloned.1.call-start = ((), (), s32[]{:S(2)}) async-start(), calls=%async_computation.6 | async-start | bytes 6291456 | tf_op jit(solution)/shard_map/all_gather | solution.py:166
  11.3 459.4 %reduce-scatter.6.cloned.1.call-start = ((), (), s32[]{:S(2)}) async-start(), calls=%async_computation.7 | async-start | bytes 6291456 | tf_op jit(solution)/shard_map/reduce_scatter | solution.py:181
  162.2 4.8 copy-start.9
  167.5 31.2 %copy-start.16 = (bf16[12,128,1024]{2,1,0:T(8,128)(2,1)}, bf16[12,128,1024]{2,1,0:T(8,128)(2,1)S(1)}, u32[]{:S(2)}) copy-start(bf16[12,128,1024]{2,1,0:T(8,128)(2,1)S(1)} %slice.85) | copy-start | bytes 9437188
  207.6 4.2 copy-start.22
  405.8 4.6 copy-start.1
  405.8 6.0 copy-start.24
  416.2 54.5 %copy-start.5 = (bf16[1024,1024]{1,0:T(8,128)(2,1)S(1)}, bf16[1024,1024]{1,0:T(8,128)(2,1)}, u32[]{:S(2)}) copy-start(bf16[1024,1024]{1,0:T(8,128)(2,1)} %param.15) | copy-start | bytes 6291460
  416.2 54.5 %copy-start.29 = (f32[1,1024]{1,0:T(1,128)S(1)}, f32[1,1024]{1,0:T(1,128)}, u32[]{:S(2)}) copy-start(f32[1,1024]{1,0:T(1,128)} %get-tuple-element.305) | copy-start | bytes 12292
  416.2 118.0 %all-gather.10.cloned.1.call-start = ((), (), s32[]{:S(2)}) async-start(), calls=%async_computation.8 | async-start | bytes 6291456 | tf_op jit(solution)/shard_map/all_gather | solution.py:193
  470.7 4.2 copy-start.33
  470.7 4.2 copy-start.39
  477.3 174.3 %reduce-scatter.8.cloned.1.call-start = ((), (), s32[]{:S(2)}) async-start(), calls=%async_computation.9 | async-start | bytes 6291456 | tf_op jit(solution)/shard_map/reduce_scatter | solution.py:199
  534.2 52.5 %copy-start.15 = (bf16[16,128,1024]{2,1,0:T(8,128)(2,1)S(1)}, bf16[16,128,1024]{2,1,0:T(8,128)(2,1)}, u32[]{:S(2)}) copy-start(bf16[16,128,1024]{2,1,0:T(8,128)(2,1)} %get-tuple-element.293) | copy-start | bytes 12582916
  597.1 54.5 %copy-start.6 = (bf16[1024,1024]{1,0:T(8,128)(2,1)S(1)}, bf16[1024,1024]{1,0:T(8,128)(2,1)}, u32[]{:S(2)}) copy-start(bf16[1024,1024]{1,0:T(8,128)(2,1)} %param.15) | copy-start | bytes 6291460
  597.1 54.5 %copy-start.30 = (f32[1,1024]{1,0:T(1,128)S(1)}, f32[1,1024]{1,0:T(1,128)}, u32[]{:S(2)}) copy-start(f32[1,1024]{1,0:T(1,128)} %get-tuple-element.305) | copy-start | bytes 12292
  597.1 54.5 %copy-start.32 = (f32[1024]{0:T(1024)S(1)}, f32[1024]{0:T(1024)}, u32[]{:S(2)}) copy-start(f32[1024]{0:T(1024)} %copy-done.31) | copy-start | bytes 12292
  597.1 54.5 %copy-start.34 = (f32[1,1024]{1,0:T(1,128)S(1)}, f32[1,1024]{1,0:T(1,128)}, u32[]{:S(2)}) copy-start(f32[1,1024]{1,0:T(1,128)} %get-tuple-element.304) | copy-start | bytes 12292
  597.1 54.5 %copy-start.36 = (f32[1024]{0:T(1024)S(1)}, f32[1024]{0:T(1024)}, u32[]{:S(2)}) copy-start(f32[1024]{0:T(1024)} %copy-done.35) | copy-start | bytes 12292
  597.1 54.5 %copy-start.40 = (f32[1,1024]{1,0:T(1,128)S(1)}, f32[1,1024]{1,0:T(1,128)}, u32[]{:S(2)}) copy-start(f32[1,1024]{1,0:T(1,128)} %get-tuple-element.303) | copy-start | bytes 12292
  597.2 54.5 %copy-start.46 = (f32[1,1024]{1,0:T(1,128)S(1)}, f32[1,1024]{1,0:T(1,128)}, u32[]{:S(2)}) copy-start(f32[1,1024]{1,0:T(1,128)} %get-tuple-element.302) | copy-start | bytes 12292
  597.2 124.0 %all-gather.12.cloned.1.call-start = ((), (), s32[]{:S(2)}) async-start(), calls=%async_computation.10 | async-start | bytes 6291456 | tf_op jit(solution)/shard_map/all_gather | solution.py:212
  664.3 148.6 %reduce-scatter.10.cloned.1.call-start = ((), (), s32[]{:S(2)}) async-start(), calls=%async_computation.11 | async-start | bytes 6291456 | tf_op jit(solution)/shard_map/reduce_scatter | solution.py:220
  758.4 124.6 %all-gather.14.cloned.1.call-start = ((), (), s32[]{:S(2)}) async-start(), calls=%async_computation.12 | async-start | bytes 6291456 | tf_op jit(solution)/shard_map/all_gather | solution.py:229
  812.9 6.8 copy-start.8
  812.9 6.8 copy-start.11
  812.9 6.8 copy-start.13
  826.2 701.8 %reduce-scatter.12.cloned.1.call-start = ((), (), s32[]{:S(2)}) async-start(), calls=%async_computation.13 | async-start | bytes 6291456 | tf_op jit(solution)/shard_map/reduce_scatter | solution.py:262
  826.2 64.6 %copy-start.2 = (bf16[2048,8,64]{0,2,1:T(8,128)(2,1)S(1)}, bf16[2048,8,64]{0,2,1:T(8,128)(2,1)}, u32[]{:S(2)}) copy-start(bf16[2048,8,64]{0,2,1:T(8,128)(2,1)} %copy-done.1) | copy-start | bytes 6291460
  826.2 64.6 %copy-start.23 = (s32[1,2048]{1,0:T(1,128)S(1)}, s32[1,2048]{1,0:T(1,128)}, u32[]{:S(2)}) copy-start(s32[1,2048]{1,0:T(1,128)} %param.16) | copy-start | bytes 24580
  826.2 64.6 %copy-start.26 = (s32[1,2048]{1,0:T(1,128)S(1)}, s32[1,2048]{1,0:T(1,128)}, u32[]{:S(2)}) copy-start(s32[1,2048]{1,0:T(1,128)} %param.17) | copy-start | bytes 24580
  981.8 10.7 copy-start
  1091.1 10.7 copy-start
  1201.7 10.7 copy-start
  1312.3 10.7 copy-start
  1335.5 4.2 copy-start.17
  1348.3 380.4 %reduce-scatter.14.cloned.1.call-start = ((), (), s32[]{:S(2)}) async-start(), calls=%async_computation.14 | async-start | bytes 26738688 | tf_op jit(solution)/shard_map/reduce_scatter | solution.py:310
  1348.4 12.8 copy-start.54
  1361.2 11.6 copy-start.19
  1361.2 11.6 copy-start.55
  1399.0 16.3 copy-start.52
  1486.4 40.9 %copy-start.28 = (f32[12,1024]{1,0:T(8,128)S(1)}, f32[12,1024]{1,0:T(8,128)}, u32[]{:S(2)}) copy-start(f32[12,1024]{1,0:T(8,128)} %param.22) | copy-start | bytes 147460
  1486.4 40.9 %copy-start.37 = (f32[12,1024]{1,0:T(8,128)S(1)}, f32[12,1024]{1,0:T(8,128)}, u32[]{:S(2)}) copy-start(f32[12,1024]{1,0:T(8,128)} %param.23) | copy-start | bytes 147460
  1486.4 40.9 %copy-start.38 = (f32[12,1024]{1,0:T(8,128)S(1)}, f32[12,1024]{1,0:T(8,128)}, u32[]{:S(2)}) copy-start(f32[12,1024]{1,0:T(8,128)} %param.24) | copy-start | bytes 147460
  1528.0 200.7 %copy-start.12 = (f32[1,6,128,1024]{3,2,1,0:T(8,128)S(1)}, f32[1,6,128,1024]{3,2,1,0:T(8,128)}, u32[]{:S(2)}) copy-start(f32[1,6,128,1024]{3,2,1,0:T(8,128)} %param.19) | copy-start | bytes 9437188
  (22 other events, 39.5 us)
Sparse Core Ops, SparseCore 0:
  10.7 129.8 all-gather.5
  142.1 56.5 all-gather.7
  416.3 54.2 reduce-scatter.5
  477.5 56.7 all-gather.9
  597.3 54.3 reduce-scatter.7
  664.4 56.7 all-gather.11
  758.6 54.2 reduce-scatter.9
  826.3 56.7 all-gather.13
  1348.4 54.2 reduce-scatter.11
  1486.6 242.0 reduce-scatter.13
where the time goes:
time: 1760 us; the launch traced here: 1750 us
  waiting for transfers between devices  681 us (39%)
  matrix products  582 us (33%)
  other arithmetic  286 us (16%)
  local copies, waits for them, and re-layouts  127 us (7%)
  blocking collectives  39.7 us (2%)
    reduce_scatter x1, waiting for transfers between devices, on_device(): lax.psum_scatter(spread_slots.astype(jnp.bfloat16), 'dp', scatter_dimensi...  195 us
    all_gather x1, waiting for transfers between devices, on_device(): lax.all_gather(master_slots[0].astype(jnp.bfloat16), 'dp', axis=0, tiled=...  128 us
    dot_general x8, matrix products, block_scores(): jnp.einsum('qhd,khd->hqk', block_q, key_rows, preferred_element_type=jnp....  115 us
    convert_element_type x4, other arithmetic, one_block(): grad_scores = (weights * (grad_weights - inner)).astype(jnp.bfloat16)  113 us
    dot_general x4, matrix products, one_block(): jnp.einsum('qhd,khd->hqk', block_g, value_rows, preferred_element_type=jn...  101 us
    dot_general x4, matrix products, one_block(): jnp.einsum('hqk,qhd->khd', weights.astype(jnp.bfloat16), block_g, preferr...  71.4 us
    dot_general x4, matrix products, one_block(): jnp.einsum('hqk,khd->qhd', weights, value_rows, preferred_element_type=jn...  63.3 us
    reduce_sum x4, other arithmetic, one_block(): totals = jnp.sum(raised, axis=2, keepdims=True)  58.4 us
  transfers between devices with their start and end apart: 10, of which 9 were waited for; matrix products, arithmetic and copies ran while one was open for 10% of the time, Pallas kernels for 0%

commit v1 on v0

--- a/solution.py
+++ b/solution.py
@@ -1,6 +1,10 @@
+import functools
+
 import jax
 import jax.numpy as jnp
 from jax import lax
+from jax.experimental import pallas as pl
+from jax.experimental.pallas import tpu as pltpu
 from jax.sharding import PartitionSpec as P
 
 D = 1024
@@ -132,7 +136,7 @@
     return (updated, first_new, second_new)
 
 
-def on_device(
+def on_device_generic(
     tokens,
     segment_ids,
     key_mask,
@@ -328,6 +332,473 @@
     )
 
 
+DOC_MAX = 800
+EXT_PAD = 512
+ABLK = 256
+HPG = 4
+AUG = 16
+neg_big = -1000000000.0
+NN = (((1,), (0,)), ((), ()))
+NT = (((1,), (1,)), ((), ()))
+TN = (((0,), (0,)), ((), ()))
+
+
+def mm(a, b, dims):
+    return lax.dot_general(a, b, dims, preferred_element_type=jnp.float32)
+
+
+def attn_fwd_kernel(lo_ref, hi_ref, q_ref, k_ref, v_ref, qaug_ref, kaug_ref, hid_ref, o_ref, lse_ref, kn_ref, m_ref, acc_ref):
+    ext = q_ref.shape[1]
+    ones = jnp.concatenate(
+        [jnp.ones((1, ABLK), jnp.float32), jnp.zeros((AUG - 1, ABLK), jnp.float32)], axis=0
+    ).astype(jnp.bfloat16)
+    for h in range(HPG):
+        rows = slice(h * HD, (h + 1) * HD)
+        kn_ref[h] = jnp.concatenate([k_ref[rows, :], kaug_ref[...]], axis=0).T
+
+    def query_block(qb, _):
+        lo = lo_ref[qb]
+        hi = hi_ref[qb]
+        qs = pl.ds(pl.multiple_of(qb * ABLK, ABLK), ABLK)
+
+        @pl.when(hi > lo)
+        def _work():
+            hidden = hid_ref[0:1, qs]
+            for h in range(HPG):
+                rows = slice(h * HD, (h + 1) * HD)
+                q32 = q_ref[rows, qs].astype(jnp.float32)
+                k32 = k_ref[rows, qs].astype(jnp.float32)
+                own = jnp.sum(q32 * k32, axis=0, keepdims=True)
+                m_ref[h] = jnp.where(hidden > 0.0, own, -1e30)
+                acc_ref[h, 0:HD, :] = v_ref[rows, qs].astype(jnp.float32) * hidden
+                acc_ref[h, HD:, :] = jnp.broadcast_to(hidden, (AUG, ABLK))
+
+            def key_block(kb, _):
+                ks = pl.ds(pl.multiple_of(kb * ABLK, ABLK), ABLK)
+                for h in range(HPG):
+                    rows = slice(h * HD, (h + 1) * HD)
+                    qa = jnp.concatenate([q_ref[rows, qs], qaug_ref[:, qs]], axis=0)
+                    s = mm(kn_ref[h, ks, :], qa, NN)
+                    old = m_ref[h]
+                    new = jnp.maximum(old, jnp.max(s, axis=0, keepdims=True))
+                    m_ref[h] = new
+                    p = jnp.exp(s - new).astype(jnp.bfloat16)
+                    va = jnp.concatenate([v_ref[rows, ks], ones], axis=0)
+                    acc_ref[h] = acc_ref[h] * jnp.exp(old - new) + mm(va, p, NN)
+                return 0
+
+            lax.fori_loop(lo, hi, key_block, 0)
+            for h in range(HPG):
+                rows = slice(h * HD, (h + 1) * HD)
+                total = acc_ref[h, HD : HD + 1, :]
+                o_ref[rows, qs] = (acc_ref[h, 0:HD, :] * (1.0 / total)).astype(jnp.bfloat16)
+                lse_ref[0, h : h + 1, qs] = m_ref[h] + jnp.log(total)
+
+        @pl.when(hi <= lo)
+        def _skip():
+            o_ref[:, qs] = jnp.zeros((HPG * HD, ABLK), jnp.bfloat16)
+            lse_ref[0, :, qs] = jnp.zeros((8, ABLK), jnp.float32)
+
+        return 0
+
+    lax.fori_loop(0, ext // ABLK, query_block, 0)
+
+
+def attn_bwd_kernel(
+    lo_ref, hi_ref, q_ref, k_ref, v_ref, g_ref, c_ref, lse_ref, qaug_ref, kaug_ref, hid_ref,
+    dq_ref, dk_ref, dv_ref, kn_ref, vn_ref, acc_ref, dk_acc, dv_acc,
+):
+    ext = q_ref.shape[1]
+    for h in range(HPG):
+        rows = slice(h * HD, (h + 1) * HD)
+        kn_ref[h] = jnp.concatenate([k_ref[rows, :], kaug_ref[...]], axis=0).T
+        vn_ref[h] = v_ref[rows, :].T
+    dk_acc[...] = jnp.zeros_like(dk_acc)
+    dv_acc[...] = jnp.zeros_like(dv_acc)
+
+    def query_block(qb, _):
+        lo = lo_ref[qb]
+        hi = hi_ref[qb]
+        qs = pl.ds(pl.multiple_of(qb * ABLK, ABLK), ABLK)
+
+        @pl.when(hi > lo)
+        def _work():
+            hidden = hid_ref[0:1, qs]
+            deltas = []
+            logs = []
+            for h in range(HPG):
+                rows = slice(h * HD, (h + 1) * HD)
+                q32 = q_ref[rows, qs].astype(jnp.float32)
+                k32 = k_ref[rows, qs].astype(jnp.float32)
+                v32 = v_ref[rows, qs].astype(jnp.float32)
+                g32 = g_ref[rows, qs].astype(jnp.float32)
+                c32 = c_ref[rows, qs].astype(jnp.float32)
+                delta = jnp.sum(g32 * c32, axis=0, keepdims=True)
+                log = lse_ref[0, h : h + 1, qs]
+                own = jnp.sum(q32 * k32, axis=0, keepdims=True)
+                p_own = jnp.where(hidden > 0.0, jnp.exp(own - log), 0.0)
+                d_own = p_own * (jnp.sum(g32 * v32, axis=0, keepdims=True) - delta)
+                acc_ref[h] = d_own * k32
+                dk_acc[rows, qs] += d_own * q32
+                dv_acc[rows, qs] += p_own * g32
+                deltas.append(delta)
+                logs.append(log)
+
+            def key_block(kb, _):
+                ks = pl.ds(pl.multiple_of(kb * ABLK, ABLK), ABLK)
+                for h in range(HPG):
+                    rows = slice(h * HD, (h + 1) * HD)
+                    q = q_ref[rows, qs]
+                    g = g_ref[rows, qs]
+                    qa = jnp.concatenate([q, qaug_ref[:, qs]], axis=0)
+                    s = mm(kn_ref[h, ks, :], qa, NN)
+                    p = jnp.exp(s - logs[h])
+                    dp = mm(vn_ref[h, ks, :], g, NN)
+                    ds = (p * (dp - deltas[h])).astype(jnp.bfloat16)
+                    pb = p.astype(jnp.bfloat16)
+                    dv_acc[rows, ks] += mm(g, pb, NT)
+                    dk_acc[rows, ks] += mm(q, ds, NT)
+                    acc_ref[h] += mm(k_ref[rows, ks], ds, NN)
+                return 0
+
+            lax.fori_loop(lo, hi, key_block, 0)
+            for h in range(HPG):
+                rows = slice(h * HD, (h + 1) * HD)
+                dq_ref[rows, qs] = acc_ref[h].astype(jnp.bfloat16) * (HD ** (-0.5))
+
+        @pl.when(hi <= lo)
+        def _skip():
+            dq_ref[:, qs] = jnp.zeros((HPG * HD, ABLK), jnp.bfloat16)
+
+        return 0
+
+    lax.fori_loop(0, ext // ABLK, query_block, 0)
+    dk_ref[...] = dk_acc[...].astype(jnp.bfloat16)
+    dv_ref[...] = dv_acc[...].astype(jnp.bfloat16)
+
+
+def group_block(offset, rows, ext):
+    return pl.BlockSpec((rows, ext), lambda g, lo, hi: (offset + g, 0))
+
+
+def fixed_block(rows, ext):
+    return pl.BlockSpec((rows, ext), lambda g, lo, hi: (0, 0))
+
+
+def attend(lo, hi, qkv, qaug, kaug, hidden):
+    ext = qkv.shape[1]
+    groups = D // HD // HPG
+    rows = HPG * HD
+    return pl.pallas_call(
+        attn_fwd_kernel,
+        out_shape=(
+            jax.ShapeDtypeStruct((D, ext), jnp.bfloat16),
+            jax.ShapeDtypeStruct((groups, 8, ext), jnp.float32),
+        ),
+        grid_spec=pltpu.PrefetchScalarGridSpec(
+            num_scalar_prefetch=2,
+            grid=(groups,),
+            in_specs=[
+                group_block(0, rows, ext),
+                group_block(groups, rows, ext),
+                group_block(2 * groups, rows, ext),
+                fixed_block(AUG, ext),
+                fixed_block(AUG, ext),
+                fixed_block(8, ext),
+            ],
+            out_specs=[
+                group_block(0, rows, ext),
+                pl.BlockSpec((1, 8, ext), lambda g, lo, hi: (g, 0, 0)),
+            ],
+            scratch_shapes=[
+                pltpu.VMEM((HPG, ext, HD + AUG), jnp.bfloat16),
+                pltpu.VMEM((HPG, 1, ABLK), jnp.float32),
+                pltpu.VMEM((HPG, HD + AUG, ABLK), jnp.float32),
+            ],
+        ),
+        compiler_params=pltpu.CompilerParams(vmem_limit_bytes=40 * 2**20),
+        cost_estimate=pl.CostEstimate(flops=20 * 10**9, bytes_accessed=14 * 10**6, transcendentals=0),
+        name="attend",
+    )(lo, hi, qkv, qkv, qkv, qaug, kaug, hidden)
+
+
+def attend_back(lo, hi, qkv, grads, context, logs, qaug, kaug, hidden):
+    ext = qkv.shape[1]
+    groups = D // HD // HPG
+    rows = HPG * HD
+    out = jax.ShapeDtypeStruct((D, ext), jnp.bfloat16)
+    return pl.pallas_call(
+        attn_bwd_kernel,
+        out_shape=(out, out, out),
+        grid_spec=pltpu.PrefetchScalarGridSpec(
+            num_scalar_prefetch=2,
+            grid=(groups,),
+            in_specs=[
+                group_block(0, rows, ext),
+                group_block(groups, rows, ext),
+                group_block(2 * groups, rows, ext),
+                group_block(0, rows, ext),
+                group_block(0, rows, ext),
+                pl.BlockSpec((1, 8, ext), lambda g, lo, hi: (g, 0, 0)),
+                fixed_block(AUG, ext),
+                fixed_block(AUG, ext),
+                fixed_block(8, ext),
+            ],
+            out_specs=[group_block(0, rows, ext)] * 3,
+            scratch_shapes=[
+                pltpu.VMEM((HPG, ext, HD + AUG), jnp.bfloat16),
+                pltpu.VMEM((HPG, ext, HD), jnp.bfloat16),
+                pltpu.VMEM((HPG, HD, ABLK), jnp.float32),
+                pltpu.VMEM((rows, ext), jnp.float32),
+                pltpu.VMEM((rows, ext), jnp.float32),
+            ],
+        ),
+        compiler_params=pltpu.CompilerParams(vmem_limit_bytes=48 * 2**20),
+        cost_estimate=pl.CostEstimate(flops=50 * 10**9, bytes_accessed=30 * 10**6, transcendentals=0),
+        name="attend_back",
+    )(lo, hi, qkv, qkv, qkv, grads, context, logs, qaug, kaug, hidden)
+
+
+def document_plan(segment, valid, half, rows):
+    length = segment.shape[0]
+    ext = rows + EXT_PAD
+    base = half * EXT_PAD
+    position = jnp.arange(length, dtype=jnp.int32)
+    documents = jnp.arange(8, dtype=jnp.int32)[:, None]
+    one_hot = segment[None, :] == documents
+    counts = jnp.sum(one_hot.astype(jnp.int32), axis=1, keepdims=True)
+    starts = jnp.sum((segment[None, :] < documents).astype(jnp.int32), axis=1, keepdims=True)
+    start = jnp.sum(jnp.where(one_hot, starts, 0), axis=0)
+    end = jnp.sum(jnp.where(one_hot, starts + counts, 0), axis=0)
+    crossing = (start < rows) & (end > rows)
+    left = jnp.max(jnp.where(crossing, rows - start, 0))
+    right = jnp.max(jnp.where(crossing, end - rows, 0))
+    worker = jnp.where(left <= right, half == 1, half == 0)
+    own = (position >= half * rows) & (position < (half + 1) * rows)
+    handled = jnp.where(crossing, worker, own)
+    cut = lambda values: lax.dynamic_slice_in_dim(values, base, ext, 0)
+    handled_ext = cut(handled)
+    begins = jnp.where(handled_ext, cut(start) - base, ext).reshape(-1, ABLK)
+    ends = jnp.where(handled_ext, cut(end) - base, 0).reshape(-1, ABLK)
+    lo = jnp.min(begins, axis=1) // ABLK
+    hi = (jnp.max(ends, axis=1) + (ABLK - 1)) // ABLK
+    blank = jnp.max(ends, axis=1) == 0
+    lo = jnp.where(blank, 0, lo)
+    hi = jnp.where(blank, 0, hi)
+    hot = cut(one_hot.T).T
+    masked = cut(valid) == 0
+    ones = jnp.ones((1, ext), jnp.bfloat16)
+    fill = jnp.zeros((AUG - 9, ext), jnp.bfloat16)
+    qaug = jnp.concatenate([hot.astype(jnp.bfloat16), ones, fill], axis=0)
+    kaug = jnp.concatenate(
+        [
+            jnp.where(hot, 0.0, neg_big).astype(jnp.bfloat16),
+            jnp.where(masked[None, :], neg_big, 0.0).astype(jnp.bfloat16),
+            fill,
+        ],
+        axis=0,
+    )
+    hidden = jnp.broadcast_to(masked.astype(jnp.float32)[None, :], (8, ext))
+    foreign = lax.dynamic_slice_in_dim(crossing & ~worker, half * rows, rows, 0)
+    return lo, hi, qaug, kaug, hidden, handled_ext, foreign
+
+
+def gelu_pair(values):
+    cdf = 0.5 * lax.erfc(values * (-(0.5**0.5)))
+    density = jnp.exp(values * values * -0.5) * (0.5 / jnp.pi) ** 0.5
+    return (values * cdf, cdf + values * density)
+
+
+def on_device_rows(
+    tokens,
+    segment_ids,
+    key_mask,
+    owners,
+    master_slots,
+    slot_first,
+    slot_second,
+    vectors,
+    vector_first,
+    vector_second,
+    out_grad,
+):
+    n_dp = lax.axis_size("dp")
+    n_tensor = lax.axis_size("tensor")
+    half = lax.axis_index("tensor")
+    every = ("tensor", "dp")
+    rows = tokens.shape[0]
+    ext = rows + EXT_PAD
+    halo = DOC_MAX // 2
+    swap = [(0, 1), (1, 0)]
+    edge = jnp.where(half == 0, rows - halo, 0)
+    halo_at = jnp.where(half == 0, rows, EXT_PAD - halo)
+    own_at = half * EXT_PAD
+
+    def extend(own_rows, halo_rows):
+        whole = jnp.zeros((ext,) + own_rows.shape[1:], own_rows.dtype)
+        whole = lax.dynamic_update_slice_in_dim(whole, halo_rows, halo_at, 0)
+        return lax.dynamic_update_slice_in_dim(whole, own_rows, own_at, 0)
+
+    def own_part(values):
+        return lax.dynamic_slice_in_dim(values, own_at, rows, 0)
+
+    def halo_part(values):
+        return lax.dynamic_slice_in_dim(values, halo_at, halo, 0)
+
+    lo, hi, qaug, kaug, hidden_keys, handled, foreign = document_plan(
+        segment_ids[0], key_mask[0], half, rows
+    )
+    halo_tokens = lax.ppermute(lax.dynamic_slice_in_dim(tokens, edge, halo, 0), "tensor", swap)
+    tokens_ext = extend(tokens, halo_tokens)
+
+    slots = slot_index(owners)
+    pieces = slots.shape[0]
+    piece_rows = master_slots.shape[2]
+    chunk = piece_rows // n_dp
+    low_slots = master_slots[0].astype(jnp.bfloat16).reshape(CAP, n_dp, chunk, D)
+    spread = lax.all_to_all(low_slots.transpose(1, 0, 2, 3), "dp", 0, 0, tiled=False)
+    dense = jnp.take(spread.reshape(n_dp * CAP, chunk, D), slots, axis=0)
+    mix_pieces = 4 * (D // n_tensor) // piece_rows
+    up_pieces = (FF // n_tensor) // piece_rows
+
+    def gather(part):
+        return lax.all_gather(part.reshape(-1, D), every, axis=0, tiled=True)
+
+    w_mix = gather(dense[:mix_pieces])
+    w_up = gather(dense[mix_pieces : mix_pieces + up_pieces])
+    w_down = gather(dense[mix_pieces + up_pieces :])
+    per = mix_pieces // 4
+    w_mix = (
+        w_mix.reshape(n_tensor, n_dp, 4, per, chunk, D).transpose(2, 0, 3, 1, 4, 5).reshape(4 * D, D)
+    )
+    w_qkv = w_mix[: 3 * D]
+    w_out = w_mix[3 * D :]
+    bias_up = (
+        vectors[2:6].reshape(n_tensor, up_pieces, n_dp, chunk).transpose(0, 2, 1, 3).reshape(FF)
+    )
+
+    bias_qkv = jnp.concatenate([vectors[0], jnp.zeros((D,), jnp.float32), vectors[1]])
+    scale_qkv = jnp.concatenate([jnp.full((D,), HD ** (-0.5)), jnp.ones((2 * D,))])
+    qkv = (
+        (mm(w_qkv, tokens_ext, NT) + bias_qkv[:, None]) * scale_qkv.astype(jnp.float32)[:, None]
+    ).astype(jnp.bfloat16)
+    context, logs = attend(lo, hi, qkv, qaug, kaug, hidden_keys)
+    attn_ext = mm(context, w_out, TN).astype(jnp.bfloat16)
+    halo_attn = lax.ppermute(halo_part(attn_ext), "tensor", swap)
+    attn_back = lax.dynamic_update_slice_in_dim(
+        jnp.zeros((rows, D), jnp.bfloat16), halo_attn, edge, 0
+    )
+    attn_sum = jnp.where(foreign[:, None], attn_back, own_part(attn_ext)).astype(jnp.float32)
+    residual_one = tokens.astype(jnp.float32) + (attn_sum + vectors[6])
+    normal_one, inverse_one = layer_stats(residual_one)
+    normed = normal_one * vectors[8] + vectors[9]
+    normed_low = normed.astype(jnp.bfloat16)
+
+    gelu, slope = gelu_pair(mm(normed_low, w_up, NT) + bias_up)
+    hidden = gelu.astype(jnp.bfloat16)
+    slope = slope.astype(jnp.bfloat16)
+    residual_two = normed + (mm(hidden, w_down, NN) + vectors[7])
+    normal_two, inverse_two = layer_stats(residual_two)
+    layer_out = (normal_two * vectors[10] + vectors[11]).astype(jnp.bfloat16)
+    grad_out = out_grad.astype(jnp.float32)
+    grad_two = norm_back(grad_out, normal_two, inverse_two, vectors[10])
+    grad_two_low = grad_two.astype(jnp.bfloat16)
+
+    def scatter(part):
+        return lax.psum_scatter(part, every, scatter_dimension=0, tiled=True)
+
+    grad_w_down = scatter(mm(hidden, grad_two_low, TN).astype(jnp.bfloat16))
+    grad_pre32 = mm(grad_two_low, w_down, NT) * slope.astype(jnp.float32)
+    grad_pre = grad_pre32.astype(jnp.bfloat16)
+    grad_w_up = scatter(mm(grad_pre, normed_low, TN).astype(jnp.bfloat16))
+    grad_norm = grad_two + mm(grad_pre, w_up, NN)
+    grad_one = norm_back(grad_norm, normal_one, inverse_one, vectors[8])
+    grad_one_low = grad_one.astype(jnp.bfloat16)
+
+    halo_grad = lax.ppermute(
+        lax.dynamic_slice_in_dim(grad_one_low, edge, halo, 0), "tensor", swap
+    )
+    grad_ext = jnp.where(handled[:, None], extend(grad_one_low, halo_grad), 0)
+    grad_context = mm(w_out, grad_ext, NT).astype(jnp.bfloat16)
+    grad_w_out = mm(context, grad_ext, NN)
+    grad_q, grad_k, grad_v = attend_back(
+        lo, hi, qkv, grad_context, context, logs, qaug, kaug, hidden_keys
+    )
+    grad_qkv = jnp.concatenate([grad_q, grad_k, grad_v], axis=0)
+    grad_w_qkv = mm(grad_qkv, tokens_ext, NN)
+    grad_w_mix = jnp.concatenate([grad_w_qkv, grad_w_out], axis=0).astype(jnp.bfloat16)
+    grad_w_mix = scatter(
+        grad_w_mix.reshape(4, n_tensor, per, n_dp, chunk, D)
+        .transpose(1, 3, 0, 2, 4, 5)
+        .reshape(4 * D, D)
+    )
+    input_ext = mm(grad_qkv, w_qkv, TN)
+    halo_input = lax.ppermute(halo_part(input_ext).astype(jnp.bfloat16), "tensor", swap)
+    input_back = lax.dynamic_update_slice_in_dim(
+        jnp.zeros((rows, D), jnp.bfloat16), halo_input, edge, 0
+    )
+    input_grad = (grad_one + own_part(input_ext) + input_back.astype(jnp.float32)).astype(
+        jnp.bfloat16
+    )
+
+    up_sum = (
+        jnp.sum(grad_pre.astype(jnp.float32), axis=0)
+        .reshape(n_tensor, n_dp, up_pieces, chunk)
+        .transpose(0, 2, 1, 3)
+        .reshape(FF // D, D)
+    )
+    vector_terms = jnp.concatenate(
+        [
+            jnp.stack(
+                [
+                    jnp.sum(grad_q.astype(jnp.float32), axis=1),
+                    jnp.sum(grad_v.astype(jnp.float32), axis=1),
+                ]
+            ),
+            up_sum,
+            jnp.stack(
+                [
+                    jnp.sum(grad_one, axis=0),
+                    jnp.sum(grad_two, axis=0),
+                    jnp.sum(grad_norm * normal_one, axis=0),
+                    jnp.sum(grad_norm, axis=0),
+                    jnp.sum(grad_out * normal_two, axis=0),
+                    jnp.sum(grad_out, axis=0),
+                ]
+            ),
+        ],
+        axis=0,
+    )
+    vector_grads = lax.psum(vector_terms, ("dp", "tensor"))
+
+    grad_chunks = jnp.concatenate([grad_w_mix, grad_w_up, grad_w_down], axis=0).reshape(
+        pieces, chunk, D
+    )
+    piece_of = jnp.full((n_dp * CAP,), pieces, jnp.int32).at[slots].set(
+        jnp.arange(pieces, dtype=jnp.int32)
+    )
+    padded = jnp.concatenate([grad_chunks, jnp.zeros((1, chunk, D), jnp.bfloat16)], axis=0)
+    outgoing = jnp.take(padded, piece_of, axis=0).reshape(n_dp, CAP, chunk, D)
+    incoming = lax.all_to_all(outgoing, "dp", 0, 0, tiled=False)
+    own_grads = incoming.transpose(1, 0, 2, 3).reshape(CAP, piece_rows, D).astype(jnp.float32)
+    slot_new, slot_first_new, slot_second_new = adam_update(
+        master_slots[0], slot_first[0], slot_second[0], own_grads, rate_matrix, weight_decay
+    )
+    vector_new, vector_first_new, vector_second_new = adam_update(
+        vectors, vector_first, vector_second, vector_grads, rate_vector, 0.0
+    )
+    return (
+        layer_out,
+        input_grad,
+        slot_new[None],
+        slot_first_new[None],
+        slot_second_new[None],
+        vector_new,
+        vector_first_new,
+        vector_second_new,
+    )
+
+
 def solution(mesh):
     placed = (
         P(("dp", "tensor"), None),
@@ -342,8 +813,9 @@
         P(),
         P(("dp", "tensor"), None),
     )
+    two_halves = mesh.shape["tensor"] == 2
     return jax.shard_map(
-        on_device,
+        on_device_rows if two_halves else on_device_generic,
         mesh=mesh,
         in_specs=placed,
         out_specs=(

time: 1760 us -> 984 us (0.56)
  matrix products: 582 us -> 199 us
  waiting for transfers between devices: 681 us -> 427 us
  other arithmetic: 286 us -> 45.6 us
  Pallas kernels: 0 us -> 125 us
  local copies, waits for them, and re-layouts: 127 us -> 56.1 us
  starting transfers between devices: 0.41 us -> 68.7 us
    dot_general x40 -> x12, matrix products: 582 us -> 199 us  [mm(): return lax.dot_general(a, b, dims, preferred_element_type=jnp.float32)]
    all_gather x5 -> x3, waiting for transfers between devices: 322 us -> 50.5 us  [gather(): return lax.all_gather(part.reshape(-1, D), every, axis=0, tiled=True)]
    convert_element_type x12 -> x4, other arithmetic: 159 us -> 5.28 us  [the longest x1 4.94 us: on_device_rows(): (grad_one + own_part(input_ext) + input_back.astype(jnp.float32)).astype(...]
    pallas_call x0 -> x2, Pallas kernels: none -> 125 us  [the longest x1 64.4 us: attend_back(): pl.pallas_call(attn_bwd_kernel, out_shape=(out, out, out), grid_spec=pltp...]
    reduce_scatter x5 -> x3, waiting for transfers between devices: 358 us -> 274 us  [scatter(): return lax.psum_scatter(part, every, scatter_dimension=0, tiled=True)]
    ppermute x0 -> x4, waiting for transfers between devices: none -> 66.5 us  [the longest x1 32.5 us: on_device_rows(): halo_attn = lax.ppermute(halo_part(attn_ext), 'tensor', swap)]
    reduce_sum x9 -> x7, other arithmetic: 73.2 us -> 11.4 us  [the longest x1 4.24 us: on_device_rows(): jnp.sum(grad_two, axis=0)]
    scatter x1, local copies, waits for them, and re-layouts: 45.1 us -> 0.85 us  [on_device_rows(): jnp.full((n_dp * CAP,), pieces, jnp.int32).at[slots]]
  transfers between devices with their start and end apart: 10 -> 12, of which waited for: 9 -> 7; matrix products, arithmetic and copies ran while one was open for 10% -> 20% of each run, Pallas kernels for 0% -> 13%
where the time goes in v1:
time: 984 us; the launch traced here: 985 us
  waiting for transfers between devices  427 us (43%)
  matrix products  199 us (20%)
  Pallas kernels  125 us (13%)
  starting transfers between devices  68.7 us (7%)
  local copies, waits for them, and re-layouts  56.1 us (6%)
  blocking collectives  46.8 us (5%)
  other arithmetic  45.6 us (5%)
  between operations  16.5 us (2%)
    reduce_scatter x3, waiting for transfers between devices, scatter(): return lax.psum_scatter(part, every, scatter_dimension=0, tiled=True)  274 us
    dot_general x12, matrix products, mm(): return lax.dot_general(a, b, dims, preferred_element_type=jnp.float32)  199 us
    pallas_call x1, Pallas kernels, attend_back(): pl.pallas_call(attn_bwd_kernel, out_shape=(out, out, out), grid_spec=pltp...  64.4 us
    pallas_call x1, Pallas kernels, attend(): pl.pallas_call(attn_fwd_kernel, out_shape=(jax.ShapeDtypeStruct((D, ext),...  60.6 us
    all_gather x3, waiting for transfers between devices, gather(): return lax.all_gather(part.reshape(-1, D), every, axis=0, tiled=True)  50.5 us
    psum x1, blocking collectives, on_device_rows(): vector_grads = lax.psum(vector_terms, ('dp', 'tensor'))  46.8 us
    all_to_all x1, waiting for transfers between devices, on_device_rows(): lax.all_to_all(low_slots.transpose(1, 0, 2, 3), 'dp', 0, 0, tiled=False)  36 us
    ppermute x1, starting transfers between devices, on_device_rows(): halo_attn = lax.ppermute(halo_part(attn_ext), 'tensor', swap)  33.4 us
  transfers between devices with their start and end apart: 12, of which 7 were waited for; matrix products, arithmetic and copies ran while one was open for 20% of the time, Pallas kernels for 13%

profile of v1, /device:TPU:13, one launch (start us, length us, event | category | flops | bytes accessed | tf_op | source)
XLA Modules:
  0.0 984.9 jit_solution(9167457805303496930)
XLA Ops:
  7.2 2.1 convert_bitcast_fusion
  10.6 6.7 all-to-all-start
  17.6 36.0 %all-to-all-done = bf16[16,6,8,1024]{3,2,1,0:T(8,128)(2,1)} async-done(((bf16[16,6,8,1024]{3,2,1,0:T(8,128)(2,1)}), bf16[16,6,8,1024]{3,2,1,0:T(8,128)(2,1)}, u32[]{:S(2)}, u32[]{:S(2)}) %all-to-all-start) | async-done | bytes 1572896 | tf_op jit(solution)/shard_map/all_to_all | solution.py:659
  53.6 2.0 gather_fusion
  63.6 16.6 %collective-permute-done = bf16[400,1024]{1,0:T(8,128)(2,1)S(1)} collective-permute-done((bf16[400,1024]{1,0:T(8,128)(2,1)}, bf16[400,1024]{1,0:T(8,128)(2,1)S(1)}, u32[]{:S(2)}, u32[]{:S(2)}) %collective-permute-start) | collective-permute-done | bytes 819232 | tf_op jit(solution)/shard_map/ppermute | solution.py:651
  80.2 2.1 broadcast.169.clone
  83.2 1.5 constant_dynamic-update-slice_fusion.7
  85.2 50.4 %all-gather.4.cloned.1.call-done = bf16[4096,1024]{1,0:T(8,128)(2,1)} async-done(((bf16[128,1024]{1,0:T(8,128)(2,1)}), bf16[4096,1024]{1,0:T(8,128)(2,1)}) %all-gather.4.cloned.1.call-update) | async-done | bytes 8388624 | tf_op jit(solution)/shard_map/all_gather | solution.py:665
  135.7 3.5 slice.71
  140.2 16.2 %multiply_convert_fusion.q_ref.k_ref.v_ref = bf16[3072,1536]{1,0:T(8,128)(2,1)} fusion(bf16[3072,1024]{1,0:T(8,128)(2,1)S(1)} %bitcast.86, bf16[1536,1024]{1,0:T(8,128)(2,1)} %constant_dynamic-update-slice_fusion.7, f32[3072]{0:T(1024)S(1)} %copy-done.46, f32[3072]{0:T(1024)S(1)} %pad_maximum_fusion.1), kind=kOutput, calls=%fused_computation.4 | convolution fusion | flops 9677832192 | bytes 18898944 | tf_op jit(solution)/shard_map/dot_general | solution.py:347
  156.5 3.7 copy-done.12
  160.2 60.6 %attend.1 = (bf16[1024,1536]{1,0:T(8,128)(2,1)S(1)}, f32[4,8,1536]{2,1,0:T(8,128)S(1)}) custom-call(s32[6]{0:T(128)S(1)} %get-tuple-element.68.lo_ref, s32[6]{0:T(128)S(1)} %get-tuple-element.67.hi_ref, bf16[3072,1536]{1,0:T(8,128)(2,1)S(1)} %copy-done.12, bf16[3072,1536]{1,0:T(8,128)(2,1)S(1)} %copy-done.12, bf16[3072,1536]{1,0:T(8,128)(2,1)S(1)} %copy-done.12, ...), custom_call_target="tpu_custom_call" | custom-call | flops 20000000000 | bytes 14000000 | tf_op jit(solution)/shard_map/attend/pallas_call | solution.py:492
  220.8 2.9 slice.72
  224.0 3.7 convolution_convert_fusion.4
  227.8 1.7 copy-done.23
  230.4 33.4 %collective-permute-start.1 = (bf16[400,1024]{1,0:T(8,128)(2,1)}, bf16[400,1024]{1,0:T(8,128)(2,1)}, u32[]{:S(2)}, u32[]{:S(2)}) collective-permute-start(bf16[400,1024]{1,0:T(8,128)(2,1)} %constant_dynamic-slice_fusion.1), channel_id=1, source_target_pairs={{0,1},{1,0},{2,3},{3,2},{4,5},{5,4},{6,7},{7,6},{8,9},{9,8},{10,11... | collective-permute-start | bytes 2457608 | tf_op jit(solution)/shard_map/ppermute | solution.py:687
  264.2 32.5 %collective-permute-done.1 = bf16[400,1024]{1,0:T(8,128)(2,1)} collective-permute-done((bf16[400,1024]{1,0:T(8,128)(2,1)}, bf16[400,1024]{1,0:T(8,128)(2,1)}, u32[]{:S(2)}, u32[]{:S(2)}) %collective-permute-start.1) | collective-permute-done | bytes 819232 | tf_op jit(solution)/shard_map/ppermute | solution.py:687
  298.1 2.7 fusion.16
  300.8 2.6 multiply_reduce_fusion.3
  303.4 52.0 %multiply_convert_fusion.2 = (bf16[1024,4096]{1,0:T(8,128)(2,1)}, f32[1024,4096]{1,0:T(8,128)}, f32[1024,4096]{1,0:T(8,128)}) fusion(f32[4096]{0:T(1024)S(1)} %add.223, bf16[4096,1024]{1,0:T(8,128)(2,1)} %all-gather.6.cloned.1.call-done, f32[1024]{0:T(1024)S(1)} %bitcast.119, f32[1024]{0:T(1024)S(1)} %bitcast.105, f32[1024]{0:T(1024)S(1)} %add_rsqrt_fusion.1, ...), kind=kOutput, calls=%fused_computation.10 | convolution fusion | flops 8872001536 | bytes 54562816 | tf_op jit(solution)/shard_map/dot_general | solution.py:347
  355.4 15.3 %fusion.43 = (f32[1024]{0:T(1024)S(1)}, f32[1024,1024]{1,0:T(8,128)S(1)}) fusion(f32[1024]{0:T(1024)S(1)} %bitcast.122, bf16[1024,4096]{1,0:T(8,128)(2,1)} %get-tuple-element.42, bf16[4096,1024]{1,0:T(8,128)(2,1)} %all-gather.8.cloned.1.call-done, f32[1024]{0:T(1024)S(1)} %bitcast.120, f32[1024]{0:T(1024)S(1)} %bitcast.106, f32[1024]{0:T(1024)S(1)} %add_rsqrt_fusion.1, ...), kind=kOutput, calls=%fused_computation.154 | convolution fusion | flops 8601467904 | bytes 25194496 | tf_op jit(solution)/shard_map/dot_general | solution.py:347
  372.3 2.8 fusion.14
  375.1 4.2 fusion.36
  379.4 23.9 %convert_reduce_fusion = (f32[4096]{0:T(1024)}, bf16[1024,4096]{1,0:T(8,128)(2,1)}) fusion(f32[1024,4096]{1,0:T(8,128)} %get-tuple-element.43, f32[1024,4096]{1,0:T(8,128)} %get-tuple-element.69, f32[4096]{0:T(1024)S(1)} %add.223, bf16[4096,1024]{1,0:T(8,128)(2,1)} %all-gather.8.cloned.1.call-done, f32[1024,1024]{1,0:T(8,128)} %get-tuple-element.36), kind=kOutput, calls=%fused_computation.7 | convolution fusion | flops 8641310720 | bytes 54558720 | tf_op jit(solution)/shard_map/dot_general | solution.py:347
  403.3 15.8 %convolution_convert_fusion.1 = bf16[4096,1024]{1,0:T(8,128)(2,1)} fusion(bf16[1024,4096]{1,0:T(8,128)(2,1)} %get-tuple-element.74, f32[1024]{0:T(1024)S(1)} %bitcast.121, f32[1024]{0:T(1024)S(1)} %bitcast.107, bf16[1024,1024]{1,0:T(8,128)(2,1)} %get-tuple-element.45, bf16[1024,1024]{1,0:T(8,128)(2,1)S(1)} %copy-done.15, f32[1024]{0:T(1024)S(1)} %add_rsqrt_fusion.1, ...), kind=kOutput, calls=%fused_computation.26 | convolution fusion | flops 8603566080 | bytes 20992000 | tf_op jit(solution)/shard_map/dot_general | solution.py:347
  419.2 15.3 %convolution_convert_fusion = bf16[4096,1024]{1,0:T(8,128)(2,1)} fusion(bf16[1024,4096]{1,0:T(8,128)(2,1)} %get-tuple-element.42, f32[1024,1024]{1,0:T(8,128)} %get-tuple-element.36), kind=kOutput, calls=%fused_computation.25 | convolution fusion | flops 8595177472 | bytes 20971520 | tf_op jit(solution)/shard_map/dot_general | solution.py:347
  434.6 18.5 %multiply_reduce_fusion = (f32[1024]{0:T(1024)}, f32[1024]{0:T(1024)S(1)}, f32[1024]{0:T(1024)S(1)}, f32[1024]{0:T(1024)}, f32[1024,1024]{1,0:T(8,128)S(1)}) fusion(f32[1024]{0:T(1024)S(1)} %add_rsqrt_fusion.1, f32[1024]{0:T(1024)S(1)} %broadcast_multiply_fusion.5, f32[1024]{0:T(1024)S(1)} %bitcast.101, bf16[1024,1024]{1,0:T(8,128)(2,1)} %get-tuple-element.45, ...), kind=kOutput, calls=%fused_computation.42 | convolution fusion | flops 8604610560 | bytes 29392896 | tf_op jit(solution)/shard_map/dot_general | solution.py:347
  453.1 3.1 fusion.38
  456.7 2.2 collective-permute-start.2
  458.8 17.4 %collective-permute-done.2 = bf16[400,1024]{1,0:T(8,128)(2,1)S(1)} collective-permute-done((bf16[400,1024]{1,0:T(8,128)(2,1)S(1)}, bf16[400,1024]{1,0:T(8,128)(2,1)S(1)}, u32[]{:S(2)}, u32[]{:S(2)}) %collective-permute-start.2) | collective-permute-done | bytes 819232 | tf_op jit(solution)/shard_map/ppermute | solution.py:718
  478.3 5.1 convolution_convert_fusion.3.g_ref
  483.5 64.4 %attend_back.1 = (bf16[1024,1536]{1,0:T(8,128)(2,1)S(1)}, bf16[1024,1536]{1,0:T(8,128)(2,1)}, bf16[1024,1536]{1,0:T(8,128)(2,1)}) custom-call(s32[6]{0:T(128)S(1)} %copy-done.9, s32[6]{0:T(128)S(1)} %copy-done.7, bf16[3072,1536]{1,0:T(8,128)(2,1)} %multiply_convert_fusion.q_ref.k_ref.v_ref, bf16[3072,1536]{1,0:T(8,128)(2,1)} %multiply_convert_fusion.q_ref.k_ref.v_ref, ...), custom_call_target="tpu_custom_call" | custom-call | flops 49999998976 | bytes 30000000 | tf_op jit(solution)/shard_map/attend_back/pallas_call | solution.py:530
  548.1 1.7 copy-done.22
  552.1 4.7 convolution_convert_fusion.5
  556.8 13.5 %convolution_convert_fusion.2 = bf16[3072,1024]{1,0:T(8,128)(2,1)} fusion(bf16[3072,1536]{1,0:T(8,128)(2,1)S(1)} %constant_dynamic-update-slice_fusion, bf16[1536,1024]{1,0:T(8,128)(2,1)} %constant_dynamic-update-slice_fusion.7), kind=kOutput, calls=%fused_computation.35 | convolution fusion | flops 9666822144 | bytes 18874368 | tf_op jit(solution)/shard_map/dot_general | solution.py:347
  570.3 7.7 pad_maximum_fusion
  578.0 8.1 copy.52
  587.1 127.0 %reduce-scatter.8.cloned.1.call-done = bf16[128,1024]{1,0:T(8,128)(2,1)} async-done(((bf16[4096,1024]{1,0:T(8,128)(2,1)}), bf16[128,1024]{1,0:T(8,128)(2,1)}) %reduce-scatter.8.cloned.1.call-update) | async-done | bytes 262160 | tf_op jit(solution)/shard_map/reduce_scatter | solution.py:708
  714.1 146.6 %reduce-scatter.4.cloned.1.call-done = bf16[128,1024]{1,0:T(8,128)(2,1)} async-done(((bf16[4096,1024]{1,0:T(8,128)(2,1)}), bf16[128,1024]{1,0:T(8,128)(2,1)}) %reduce-scatter.4.cloned.1.call-update) | async-done | bytes 262160 | tf_op jit(solution)/shard_map/reduce_scatter | solution.py:708
  862.8 3.0 gather_fusion.1
  865.9 2.8 broadcast_select_fusion.1
  868.6 24.0 %all-to-all-start.1 = ((bf16[16,6,8,1024]{3,2,1,0:T(8,128)(2,1)}), bf16[16,6,8,1024]{3,2,1,0:T(8,128)(2,1)}, u32[]{:S(2)}, u32[]{:S(2)}) async-start(bf16[16,6,8,1024]{3,2,1,0:T(8,128)(2,1)} %broadcast_select_fusion.1), calls=%async_computation.4 | async-start | bytes 3145728 | tf_op jit(solution)/shard_map/all_to_all | solution.py:782
  892.7 14.7 %fusion.44 = f32[1536,1024]{1,0:T(8,128)S(1)} fusion(bf16[3072,1536]{1,0:T(8,128)(2,1)} %copy-done.27, bf16[3072,1024]{1,0:T(8,128)(2,1)} %bitcast.87), kind=kOutput, calls=%fused_computation.155 | convolution fusion | flops 9663676416 | bytes 22020096 | tf_op jit(solution)/shard_map/dot_general | solution.py:347
  907.4 2.6 copy-done.21
  916.8 46.8 %psum.7 = f32[12,1024]{1,0:T(8,128)S(1)} all-reduce(f32[12,1024]{1,0:T(8,128)S(1)} %concatenate.32), channel_id=1, replica_groups=mesh['dp'=16,'tensor'=2] {'dp','tensor'}, use_global_device_ids=true, to_apply=%region_30.31 | all-reduce | flops 12288 | bytes 98304 | tf_op jit(solution)/shard_map/psum | solution.py:772
  964.7 1.6 constant_dynamic-update-slice_fusion.3
  966.3 4.9 add_convert_fusion.1
  971.2 6.6 multiply_subtract_fusion
  (183 shorter events, 31.1 us)
Async XLA Ops:
  9.3 8.0 copy-start.45
  10.6 46.9 %copy-start.15 = (bf16[1024,1024]{1,0:T(8,128)(2,1)S(1)}, bf16[1024,1024]{1,0:T(8,128)(2,1)}, u32[]{:S(2)}) copy-start(bf16[1024,1024]{1,0:T(8,128)(2,1)} %param.11) | copy-start | bytes 6291460
  10.6 43.0 %all-to-all-start = ((bf16[16,6,8,1024]{3,2,1,0:T(8,128)(2,1)}), bf16[16,6,8,1024]{3,2,1,0:T(8,128)(2,1)}, u32[]{:S(2)}, u32[]{:S(2)}) async-start(bf16[16,6,8,1024]{3,2,1,0:T(8,128)(2,1)} %copy.48), calls=%async_computation | async-start | bytes 3145728 | tf_op jit(solution)/shard_map/all_to_all | solution.py:659
  17.3 42.4 %copy-start.30 = (s32[1,2048]{1,0:T(1,128)S(1)}, s32[1,2048]{1,0:T(1,128)}, u32[]{:S(2)}) copy-start(s32[1,2048]{1,0:T(1,128)} %param.12) | copy-start | bytes 24580
  17.3 45.3 %copy-start.28 = (f32[12,1024]{1,0:T(8,128)S(1)}, f32[12,1024]{1,0:T(8,128)}, u32[]{:S(2)}) copy-start(f32[12,1024]{1,0:T(8,128)} %param.18) | copy-start | bytes 147460
  17.3 45.9 %copy-start.40 = (s32[1,2048]{1,0:T(1,128)S(1)}, s32[1,2048]{1,0:T(1,128)}, u32[]{:S(2)}) copy-start(s32[1,2048]{1,0:T(1,128)} %param.13) | copy-start | bytes 24580
  17.3 118.4 %all-gather.4.cloned.1.call-start = ((), (), s32[]{:S(2)}) async-start(), calls=%async_computation.5 | async-start | bytes 8650752 | tf_op jit(solution)/shard_map/all_gather | solution.py:665
  17.5 42.2 %copy-start.44 = (s32[48,1]{0,1:T(1,128)}, s32[48,1]{0,1:T(1,128)S(1)}, u32[]{:S(2)}) copy-start(s32[48,1]{0,1:T(1,128)S(1)} %get-tuple-element.50) | copy-start | bytes 580
  56.6 246.8 %all-gather.6.cloned.1.call-start = ((), (), s32[]{:S(2)}) async-start(), calls=%async_computation.6 | async-start | bytes 8650752 | tf_op jit(solution)/shard_map/all_gather | solution.py:665
  57.4 298.0 %all-gather.8.cloned.1.call-start = ((), (), s32[]{:S(2)}) async-start(), calls=%async_computation.7 | async-start | bytes 8650752 | tf_op jit(solution)/shard_map/all_gather | solution.py:665
  58.4 21.7 %collective-permute-start = (bf16[400,1024]{1,0:T(8,128)(2,1)}, bf16[400,1024]{1,0:T(8,128)(2,1)S(1)}, u32[]{:S(2)}, u32[]{:S(2)}) collective-permute-start(bf16[400,1024]{1,0:T(8,128)(2,1)} %constant_dynamic-slice_fusion.3), channel_id=1, source_target_pairs={{0,1},{1,0},{2,3},{3,2},{4,5},{5,4},{6,7},{7,6},{8,9},{9,8},{10,11... | collective-permute-start | bytes 2457608 | tf_op jit(solution)/shard_map/ppermute | solution.py:651
  62.5 93.9 %copy-start.6 = (s32[6]{0:T(128)}, s32[6]{0:T(128)S(1)}, u32[]{:S(2)}) copy-start(s32[6]{0:T(128)S(1)} %get-tuple-element.67.hi_ref) | copy-start | bytes 76
  62.5 93.9 %copy-start.8 = (s32[6]{0:T(128)}, s32[6]{0:T(128)S(1)}, u32[]{:S(2)}) copy-start(s32[6]{0:T(128)S(1)} %get-tuple-element.68.lo_ref) | copy-start | bytes 76
  63.5 93.0 %copy-start.2 = (bf16[16,1536]{1,0:T(8,128)(2,1)}, bf16[16,1536]{1,0:T(8,128)(2,1)S(1)}, u32[]{:S(2)}) copy-start(bf16[16,1536]{1,0:T(8,128)(2,1)S(1)} %get-tuple-element.65.kaug_ref) | copy-start | bytes 147460
  63.5 93.0 %copy-start.4 = (bf16[16,1536]{1,0:T(8,128)(2,1)}, bf16[16,1536]{1,0:T(8,128)(2,1)S(1)}, u32[]{:S(2)}) copy-start(bf16[16,1536]{1,0:T(8,128)(2,1)S(1)} %get-tuple-element.66.qaug_ref) | copy-start | bytes 147460
  84.7 502.4 %reduce-scatter.6.cloned.1.call-start = ((), (), s32[]{:S(2)}) async-start(), calls=%async_computation.9 | async-start | bytes 8650752 | tf_op jit(solution)/shard_map/reduce_scatter | solution.py:708
  140.2 16.2 %copy-start.20 = (bf16[3,2,4,16,8,1024]{5,4,3,2,1,0:T(8,128)(2,1)}, bf16[3,2,4,16,8,1024]{5,4,3,2,1,0:T(8,128)(2,1)S(1)}, u32[]{:S(2)}) copy-start(bf16[3,2,4,16,8,1024]{5,4,3,2,1,0:T(8,128)(2,1)S(1)} %copy.49) | copy-start | bytes 18874372
  156.5 3.7 copy-start.12
  160.2 60.6 %copy-start = (f32[8,1536]{1,0:T(8,128)}, f32[8,1536]{1,0:T(8,128)S(1)}, u32[]{:S(2)}) copy-start(f32[8,1536]{1,0:T(8,128)S(1)} %broadcast_in_dim.162.hid_ref) | copy-start | bytes 147460
  220.8 3.2 copy-start.10
  224.0 3.8 copy-start.25
  230.4 66.3 %collective-permute-start.1 = (bf16[400,1024]{1,0:T(8,128)(2,1)}, bf16[400,1024]{1,0:T(8,128)(2,1)}, u32[]{:S(2)}, u32[]{:S(2)}) collective-permute-start(bf16[400,1024]{1,0:T(8,128)(2,1)} %constant_dynamic-slice_fusion.1), channel_id=1, source_target_pairs={{0,1},{1,0},{2,3},{3,2},{4,5},{5,4},{6,7},{7,6},{8,9},{9,8},{10,11... | collective-permute-start | bytes 2457608 | tf_op jit(solution)/shard_map/ppermute | solution.py:687
  264.1 34.0 %copy-start.24 = (bf16[1536,1024]{1,0:T(8,128)(2,1)S(1)}, bf16[1536,1024]{1,0:T(8,128)(2,1)}, u32[]{:S(2)}) copy-start(bf16[1536,1024]{1,0:T(8,128)(2,1)} %copy-done.23) | copy-start | bytes 9437188
  303.4 52.0 %copy-start.41 = (f32[1,1024]{1,0:T(1,128)S(1)}, f32[1,1024]{1,0:T(1,128)}, u32[]{:S(2)}) copy-start(f32[1,1024]{1,0:T(1,128)} %get-tuple-element.56) | copy-start | bytes 12292
  371.3 3.9 copy-start.35
  419.2 295.0 %reduce-scatter.8.cloned.1.call-start = ((), (), s32[]{:S(2)}) async-start(), calls=%async_computation.10 | async-start | bytes 8650752 | tf_op jit(solution)/shard_map/reduce_scatter | solution.py:708
  434.5 426.2 %reduce-scatter.4.cloned.1.call-start = ((), (), s32[]{:S(2)}) async-start(), calls=%async_computation.8 | async-start | bytes 8650752 | tf_op jit(solution)/shard_map/reduce_scatter | solution.py:708
  456.2 20.5 %copy-start.13 = (f32[1024,1024]{1,0:T(8,128)}, f32[1024,1024]{1,0:T(8,128)S(1)}, u32[]{:S(2)}) copy-start(f32[1024,1024]{1,0:T(8,128)S(1)} %get-tuple-element.38) | copy-start | bytes 12582916
  456.7 19.6 %collective-permute-start.2 = (bf16[400,1024]{1,0:T(8,128)(2,1)S(1)}, bf16[400,1024]{1,0:T(8,128)(2,1)S(1)}, u32[]{:S(2)}, u32[]{:S(2)}) collective-permute-start(bf16[400,1024]{1,0:T(8,128)(2,1)S(1)} %constant_dynamic-slice_fusion), channel_id=1, source_target_pairs={{0,1},{1,0},{2,3},{3,2},{4,5},{5,4},{6,7},{7,6},{8,9},{9,8},{10,11... | collective-permute-start | bytes 2457608 | tf_op jit(solution)/shard_map/ppermute | solution.py:718
  478.3 5.1 copy-start.1
  478.3 5.1 copy-start.3
  478.3 5.1 copy-start.5
  478.3 5.1 copy-start.7
  478.3 5.1 copy-start.9
  548.1 2.7 copy-start.17
  552.0 4.7 copy-start.27
  868.6 102.6 %all-to-all-start.1 = ((bf16[16,6,8,1024]{3,2,1,0:T(8,128)(2,1)}), bf16[16,6,8,1024]{3,2,1,0:T(8,128)(2,1)}, u32[]{:S(2)}, u32[]{:S(2)}) async-start(bf16[16,6,8,1024]{3,2,1,0:T(8,128)(2,1)} %broadcast_select_fusion.1), calls=%async_computation.4 | async-start | bytes 3145728 | tf_op jit(solution)/shard_map/all_to_all | solution.py:782
  907.4 2.7 copy-start.21
  910.1 6.6 copy-start.34
  910.1 6.6 copy-start.36
  910.1 6.7 copy-start.37
  911.1 52.6 %copy-start.29 = (f32[12,1024]{1,0:T(8,128)S(1)}, f32[12,1024]{1,0:T(8,128)}, u32[]{:S(2)}) copy-start(f32[12,1024]{1,0:T(8,128)} %param.18) | copy-start | bytes 147460
  911.1 52.6 %copy-start.31 = (f32[12,1024]{1,0:T(8,128)S(1)}, f32[12,1024]{1,0:T(8,128)}, u32[]{:S(2)}) copy-start(f32[12,1024]{1,0:T(8,128)} %param.19) | copy-start | bytes 147460
  911.1 53.3 %collective-permute-start.3 = (bf16[400,1024]{1,0:T(8,128)(2,1)}, bf16[400,1024]{1,0:T(8,128)(2,1)}, u32[]{:S(2)}, u32[]{:S(2)}) collective-permute-start(bf16[400,1024]{1,0:T(8,128)(2,1)} %dynamic-slice_convert_fusion), channel_id=1, source_target_pairs={{0,1},{1,0},{2,3},{3,2},{4,5},{5,4},{6,7},{7,6},{8,9},{9,8},{10,11... | collective-permute-start | bytes 2457608 | tf_op jit(solution)/shard_map/ppermute | solution.py:736
  913.2 3.6 copy-start.42
  913.2 3.6 copy-start.43
  913.2 50.5 %copy-start.32 = (f32[12,1024]{1,0:T(8,128)S(1)}, f32[12,1024]{1,0:T(8,128)}, u32[]{:S(2)}) copy-start(f32[12,1024]{1,0:T(8,128)} %param.20) | copy-start | bytes 147460
  966.2 5.0 copy-start.16
  (11 other events, 18.2 us)
Sparse Core Ops, SparseCore 0:
  56.8 78.8 all-gather.3
  138.6 76.4 all-gather.5
  218.6 90.9 all-gather.7
  419.3 146.7 reduce-scatter.5
  568.2 145.8 reduce-scatter.7
  716.3 144.4 reduce-scatter.3

commit v2 on v1

--- a/solution.py
+++ b/solution.py
@@ -522,24 +522,29 @@
     )(lo, hi, qkv, qkv, qkv, qaug, kaug, hidden)
 
 
-def attend_back(lo, hi, qkv, grads, context, logs, qaug, kaug, hidden):
+def attend_back(lo, hi, qkv, grads, context, logs, qaug, kaug, hidden, first, step):
     ext = qkv.shape[1]
     groups = D // HD // HPG
     rows = HPG * HD
-    out = jax.ShapeDtypeStruct((D, ext), jnp.bfloat16)
+    count = len(range(first, groups, step))
+    out = jax.ShapeDtypeStruct((count * rows, ext), jnp.bfloat16)
+
+    def taken(offset):
+        return pl.BlockSpec((rows, ext), lambda g, lo, hi: (offset + first + step * g, 0))
+
     return pl.pallas_call(
         attn_bwd_kernel,
         out_shape=(out, out, out),
         grid_spec=pltpu.PrefetchScalarGridSpec(
             num_scalar_prefetch=2,
-            grid=(groups,),
+            grid=(count,),
             in_specs=[
-                group_block(0, rows, ext),
-                group_block(groups, rows, ext),
-                group_block(2 * groups, rows, ext),
-                group_block(0, rows, ext),
-                group_block(0, rows, ext),
-                pl.BlockSpec((1, 8, ext), lambda g, lo, hi: (g, 0, 0)),
+                taken(0),
+                taken(groups),
+                taken(2 * groups),
+                taken(0),
+                taken(0),
+                pl.BlockSpec((1, 8, ext), lambda g, lo, hi: (first + step * g, 0, 0)),
                 fixed_block(AUG, ext),
                 fixed_block(AUG, ext),
                 fixed_block(8, ext),
@@ -603,10 +608,354 @@
     return lo, hi, qaug, kaug, hidden, handled_ext, foreign
 
 
+MESH = pl.DeviceIdType.MESH
+CHUNKS = 3
+
+
+def neighbours(z, y, core, x):
+    def at(z, y, core, x):
+        return {"dp": (z * 2 + y) * 2 + core, "tensor": x}
+
+    return {
+        "x": at(z, y, core, 1 - x),
+        "y": at(z, 1 - y, core, x),
+        "core": at(z, y, 1 - core, x),
+        "up": at(jnp.minimum(z + 1, 3), y, core, x),
+        "down": at(jnp.maximum(z - 1, 0), y, core, x),
+    }
+
+
+def greet(near, z):
+    barrier = pltpu.get_barrier_semaphore()
+    for name in ("x", "y", "core"):
+        pl.semaphore_signal(barrier, inc=1, device_id=near[name], device_id_type=MESH)
+
+    @pl.when(z < 3)
+    def _up():
+        pl.semaphore_signal(barrier, inc=1, device_id=near["up"], device_id_type=MESH)
+
+    @pl.when(z > 0)
+    def _down():
+        pl.semaphore_signal(barrier, inc=1, device_id=near["down"], device_id_type=MESH)
+
+    at_end = jnp.where((z == 0) | (z == 3), 1, 0)
+    pl.semaphore_wait(barrier, 5 - at_end)
+
+
+def greet_all(near, me, n_dp):
+    barrier = pltpu.get_barrier_semaphore()
+    pl.semaphore_signal(barrier, inc=1, device_id=near["x"], device_id_type=MESH)
+
+    def one(i, _):
+        other = {"dp": lax.rem(me + i, n_dp), "tensor": lax.axis_index("tensor")}
+        pl.semaphore_signal(barrier, inc=1, device_id=other, device_id_type=MESH)
+        return 0
+
+    lax.fori_loop(1, n_dp, one, 0)
+    pl.semaphore_wait(barrier, n_dp)
+
+
+def gather_kernel(
+    slots_ref, low_ref, mix_ref, up_ref, down_ref,
+    spread_ref, dense_ref, local_sem, own_sem, post, mail, send, recv,
+):
+    z, y, core, x = coordinates()
+    near = neighbours(z, y, core, x)
+    width = D // 2
+    outs = (mix_ref, up_ref, down_ref)
+    me = lax.axis_index("dp")
+    n_dp = low_ref.shape[0]
+    greet_all(near, me, n_dp)
+
+    def letter(to):
+        return pltpu.make_async_remote_copy(
+            src_ref=low_ref.at[to],
+            dst_ref=spread_ref.at[pl.ds(me * CAP, CAP)],
+            send_sem=post.at[to],
+            recv_sem=mail.at[me],
+            device_id={"dp": to, "tensor": x},
+            device_id_type=MESH,
+        )
+
+    def answer(of):
+        return pltpu.make_async_remote_copy(
+            src_ref=low_ref.at[of],
+            dst_ref=spread_ref.at[pl.ds(of * CAP, CAP)],
+            send_sem=post.at[of],
+            recv_sem=mail.at[of],
+            device_id={"dp": of, "tensor": x},
+            device_id_type=MESH,
+        )
+
+    def peer(i):
+        return lax.rem(me + i, n_dp)
+
+    def post_one(i, _):
+        letter(peer(i)).start()
+        return 0
+
+    lax.fori_loop(1, n_dp, post_one, 0)
+    mine = pltpu.make_async_copy(low_ref.at[me], spread_ref.at[pl.ds(me * CAP, CAP)], local_sem)
+    mine.start()
+    mine.wait()
+
+    def mail_one(i, _):
+        answer(peer(i)).wait_recv()
+        letter(peer(i)).wait_send()
+        return 0
+
+    lax.fori_loop(1, n_dp, mail_one, 0)
+
+    def place(p, _):
+        dense_ref[p // 16, (p // 4) % 4, p % 4] = spread_ref[slots_ref[p]]
+        return 0
+
+    lax.fori_loop(0, slots_ref.shape[0], place, 0)
+
+    def block(k, t, zz, yy, cc, part=None):
+        groups = slice(None) if part is None else pl.ds(2 * part, 2)
+        return outs[k].at[
+            groups,
+            t,
+            :,
+            pl.ds(pl.multiple_of((zz * 2 + yy) * 16, 16), 16),
+            pl.ds(pl.multiple_of(cc * width, width), width),
+        ]
+
+    own = [
+        pltpu.make_async_copy(dense_ref.at[k], block(k, x, z, y, core), own_sem.at[k])
+        for k in range(CHUNKS)
+    ]
+    for one in own:
+        one.start()
+
+    def copy(kind, link, k, zz, t, yy, cc, part=None, fresh=False):
+        view = block(k, t, zz, yy, cc, part)
+        return pltpu.make_async_remote_copy(
+            src_ref=dense_ref.at[k] if fresh else view,
+            dst_ref=view,
+            send_sem=send.at[kind, k, zz],
+            recv_sem=recv.at[kind, k, zz],
+            device_id=near[link],
+            device_id_type=MESH,
+        )
+
+    def up(k, zz, fresh=False):
+        return copy(0, "up", k, zz, x, y, core, fresh=fresh)
+
+    def down(k, zz, fresh=False):
+        return copy(1, "down", k, zz, x, y, core, fresh=fresh)
+
+    def spread(k, zz, fresh):
+        copy(2, "x", k, zz, x, y, core, fresh=fresh).start()
+        copy(3, "y", k, zz, x, y, core, fresh=fresh).start()
+        copy(4, "core", k, zz, x, y, core, fresh=fresh).start()
+
+    def each(d, body):
+        @pl.when((d > 0) & (z - d >= 0))
+        def _below():
+            for k in range(CHUNKS):
+                body(k, z - d, 0)
+
+        @pl.when((d > 0) & (z + d <= 3))
+        def _above():
+            for k in range(CHUNKS):
+                body(k, z + d, 1)
+
+    def each_or_own(d, body):
+        each(d, body)
+
+        @pl.when(d == 0)
+        def _own():
+            for k in range(CHUNKS):
+                body(k, z, None)
+
+    def begin(k):
+        @pl.when(z < 3)
+        def _up():
+            up(k, z, True).start()
+
+        @pl.when(z > 0)
+        def _down():
+            down(k, z, True).start()
+
+        spread(k, z, True)
+
+    def first(k, zz, side):
+        if side == 0:
+            up(k, zz).wait_recv()
+
+            @pl.when(z < 3)
+            def _up():
+                up(k, zz).start()
+
+        else:
+            down(k, zz).wait_recv()
+
+            @pl.when(z > 0)
+            def _on():
+                down(k, zz).start()
+
+        spread(k, zz, False)
+
+    def second(k, zz, side):
+        copy(2, "x", k, zz, 1 - x, y, core).wait_recv()
+        copy(5, "y", k, zz, 1 - x, y, core, 0).start()
+        copy(7, "core", k, zz, 1 - x, y, core).start()
+        copy(3, "y", k, zz, x, 1 - y, core).wait_recv()
+        copy(6, "x", k, zz, x, 1 - y, core, 1).start()
+        copy(8, "core", k, zz, x, 1 - y, core).start()
+
+    def third(k, zz, side):
+        copy(5, "y", k, zz, 1 - x, 1 - y, core, 0).wait_recv()
+        copy(9, "core", k, zz, 1 - x, 1 - y, core, 0).start()
+        copy(6, "x", k, zz, 1 - x, 1 - y, core, 1).wait_recv()
+        copy(10, "core", k, zz, 1 - x, 1 - y, core, 1).start()
+
+    def finish(k, zz, side):
+        if side != 1:
+
+            @pl.when(z < 3)
+            def _up():
+                up(k, zz).wait_send()
+
+        if side != 0:
+
+            @pl.when(z > 0)
+            def _down():
+                down(k, zz).wait_send()
+
+        copy(2, "x", k, zz, x, y, core).wait_send()
+        copy(3, "y", k, zz, x, y, core).wait_send()
+        copy(5, "y", k, zz, 1 - x, y, core, 0).wait_send()
+        copy(6, "x", k, zz, x, 1 - y, core, 1).wait_send()
+        copy(4, "core", k, zz, x, y, core).wait_send()
+        copy(7, "core", k, zz, 1 - x, y, core).wait_send()
+        copy(8, "core", k, zz, x, 1 - y, core).wait_send()
+        copy(9, "core", k, zz, 1 - x, 1 - y, core, 0).wait_send()
+        copy(10, "core", k, zz, 1 - x, 1 - y, core, 1).wait_send()
+        copy(4, "core", k, zz, x, y, 1 - core).wait_recv()
+        copy(7, "core", k, zz, 1 - x, y, 1 - core).wait_recv()
+        copy(8, "core", k, zz, x, 1 - y, 1 - core).wait_recv()
+        copy(9, "core", k, zz, 1 - x, 1 - y, 1 - core, 0).wait_recv()
+        copy(10, "core", k, zz, 1 - x, 1 - y, 1 - core, 1).wait_recv()
+
+    for k in range(CHUNKS):
+        begin(k)
+
+    def step(d, _):
+        @pl.when(d < 4)
+        def _one():
+            each(d, first)
+
+        @pl.when((d >= 1) & (d < 5))
+        def _two():
+            each_or_own(d - 1, second)
+
+        @pl.when(d >= 2)
+        def _three():
+            each_or_own(d - 2, third)
+
+        return 0
+
+    lax.fori_loop(1, 6, step, 0)
+
+    def end(d, _):
+        each_or_own(d, finish)
+        return 0
+
+    lax.fori_loop(0, 4, end, 0)
+    for one in own:
+        one.wait()
+
+
+def gather_weights(slots, low):
+    n_dp = low.shape[0]
+    stack = jax.ShapeDtypeStruct((4, 2, 4, 128, D), low.dtype)
+    return pl.pallas_call(
+        gather_kernel,
+        out_shape=(stack,) * 3,
+        in_specs=[
+            pl.BlockSpec(memory_space=pltpu.SMEM),
+            pl.BlockSpec(memory_space=pl.ANY),
+        ],
+        out_specs=(pl.BlockSpec(memory_space=pl.ANY),) * 3,
+        scratch_shapes=[
+            pltpu.VMEM((n_dp * CAP, 16, D // 2), low.dtype),
+            pltpu.VMEM((CHUNKS, 4, 4, 16, D // 2), low.dtype),
+            pltpu.SemaphoreType.DMA,
+            pltpu.SemaphoreType.DMA((CHUNKS,)),
+            pltpu.SemaphoreType.DMA((n_dp,)),
+            pltpu.SemaphoreType.DMA((n_dp,)),
+            pltpu.SemaphoreType.DMA((11, CHUNKS, 4)),
+            pltpu.SemaphoreType.DMA((11, CHUNKS, 4)),
+        ],
+        compiler_params=pltpu.CompilerParams(
+            collective_id=1, has_side_effects=True, vmem_limit_bytes=32 * 2**20
+        ),
+        cost_estimate=pl.CostEstimate(flops=0, bytes_accessed=50 * 10**6, transcendentals=0),
+        name="gather_weights",
+    )(slots, low)
+
+
 def gelu_pair(values):
     cdf = 0.5 * lax.erfc(values * (-(0.5**0.5)))
     density = jnp.exp(values * values * -0.5) * (0.5 / jnp.pi) ** 0.5
     return (values * cdf, cdf + values * density)
+
+
+def coordinates():
+    dp = lax.axis_index("dp")
+    return dp // 4, (dp // 2) % 2, dp % 2, lax.axis_index("tensor")
+
+
+def exchange(values, axis):
+    if axis == "x":
+        return lax.ppermute(values, "tensor", [(0, 1), (1, 0)])
+    flip = {"core": 1, "y": 2, "z_near": 4, "z_far": 8}[axis]
+    return lax.ppermute(values, "dp", [(i, i ^ flip) for i in range(lax.axis_size("dp"))])
+
+
+def pick(values, index, axis):
+    return lax.dynamic_index_in_dim(values, index, axis, keepdims=False)
+
+
+def add_low(one, two):
+    return (one.astype(jnp.float32) + two.astype(jnp.float32)).astype(jnp.bfloat16)
+
+
+def sum_all(values):
+    for axis in ("core", "y", "x", "z_near", "z_far"):
+        values = values + exchange(values, axis)
+    return values
+
+
+def halve(values, index, axis, link):
+    other = exchange(pick(values, 1 - index, axis), link)
+    return pick(values, index, axis), other
+
+
+def scatter_rows(lhs, rhs, dims, shape):
+    z, y, core, x = coordinates()
+    width = D // 2
+    far = lax.dynamic_slice_in_dim(rhs, (1 - core) * width, width, 1)
+    near = lax.dynamic_slice_in_dim(rhs, core * width, width, 1)
+    arrived = exchange(mm(lhs, far, dims).astype(jnp.bfloat16), "core")
+    product = (mm(lhs, near, dims) + arrived.astype(jnp.float32)).astype(jnp.bfloat16)
+    product = product.reshape(shape + (width,))
+    middle = shape[2] // 2
+    one, one_in = halve(product[:, :, :middle], x, 1, "x")
+    two, two_in = halve(product[:, :, middle:], y, 4, "y")
+    one_send = exchange(add_low(pick(one, 1 - y, 3), pick(one_in, 1 - y, 3)), "y")
+    two_send = exchange(add_low(pick(two, 1 - x, 1), pick(two_in, 1 - x, 1)), "x")
+    one = pick(one, y, 3).astype(jnp.float32) + pick(one_in, y, 3).astype(jnp.float32) + one_send.astype(jnp.float32)
+    two = pick(two, x, 1).astype(jnp.float32) + pick(two_in, x, 1).astype(jnp.float32) + two_send.astype(jnp.float32)
+    line = jnp.concatenate([one, two], axis=1).astype(jnp.bfloat16)
+    line = line.reshape(shape[0], shape[2], 2, 2, 16, width)
+    line, line_in = halve(line, z // 2, 2, "z_far")
+    last_in = exchange(add_low(pick(line, 1 - z % 2, 2), pick(line_in, 1 - z % 2, 2)), "z_near")
+    last = pick(line, z % 2, 2).astype(jnp.float32) + pick(line_in, z % 2, 2).astype(jnp.float32)
+    return (last + last_in.astype(jnp.float32)).astype(jnp.bfloat16).reshape(-1, 16, width)
 
 
 def on_device_rows(
@@ -654,28 +1003,17 @@
     slots = slot_index(owners)
     pieces = slots.shape[0]
     piece_rows = master_slots.shape[2]
-    chunk = piece_rows // n_dp
-    low_slots = master_slots[0].astype(jnp.bfloat16).reshape(CAP, n_dp, chunk, D)
-    spread = lax.all_to_all(low_slots.transpose(1, 0, 2, 3), "dp", 0, 0, tiled=False)
-    dense = jnp.take(spread.reshape(n_dp * CAP, chunk, D), slots, axis=0)
+    low_slots = master_slots[0].astype(jnp.bfloat16).reshape(CAP, 8, 16, 2, D // 2)
+    low_slots = low_slots.transpose(1, 3, 0, 2, 4).reshape(n_dp, CAP, 16, D // 2)
     mix_pieces = 4 * (D // n_tensor) // piece_rows
     up_pieces = (FF // n_tensor) // piece_rows
-
-    def gather(part):
-        return lax.all_gather(part.reshape(-1, D), every, axis=0, tiled=True)
-
-    w_mix = gather(dense[:mix_pieces])
-    w_up = gather(dense[mix_pieces : mix_pieces + up_pieces])
-    w_down = gather(dense[mix_pieces + up_pieces :])
     per = mix_pieces // 4
-    w_mix = (
-        w_mix.reshape(n_tensor, n_dp, 4, per, chunk, D).transpose(2, 0, 3, 1, 4, 5).reshape(4 * D, D)
-    )
-    w_qkv = w_mix[: 3 * D]
-    w_out = w_mix[3 * D :]
-    bias_up = (
-        vectors[2:6].reshape(n_tensor, up_pieces, n_dp, chunk).transpose(0, 2, 1, 3).reshape(FF)
-    )
+    mix, up, down = gather_weights(slots, low_slots)
+    w_qkv = mix[:3].reshape(3 * D, D)
+    w_out = mix[3].reshape(D, D)
+    w_up = up.reshape(FF, D)
+    w_down = down.reshape(FF, D)
+    bias_up = vectors[2:6].reshape(n_tensor, 4, -1).transpose(1, 0, 2).reshape(FF)
 
     bias_qkv = jnp.concatenate([vectors[0], jnp.zeros((D,), jnp.float32), vectors[1]])
     scale_qkv = jnp.concatenate([jnp.full((D,), HD ** (-0.5)), jnp.ones((2 * D,))])
@@ -704,13 +1042,11 @@
     grad_two = norm_back(grad_out, normal_two, inverse_two, vectors[10])
     grad_two_low = grad_two.astype(jnp.bfloat16)
 
-    def scatter(part):
-        return lax.psum_scatter(part, every, scatter_dimension=0, tiled=True)
-
-    grad_w_down = scatter(mm(hidden, grad_two_low, TN).astype(jnp.bfloat16))
+    wide = (4, n_tensor, up_pieces // 4, 4, 2, 16)
+    grad_w_down = scatter_rows(hidden, grad_two_low, TN, wide)
     grad_pre32 = mm(grad_two_low, w_down, NT) * slope.astype(jnp.float32)
     grad_pre = grad_pre32.astype(jnp.bfloat16)
-    grad_w_up = scatter(mm(grad_pre, normed_low, TN).astype(jnp.bfloat16))
+    grad_w_up = scatter_rows(grad_pre, normed_low, TN, wide)
     grad_norm = grad_two + mm(grad_pre, w_up, NN)
     grad_one = norm_back(grad_norm, normal_one, inverse_one, vectors[8])
     grad_one_low = grad_one.astype(jnp.bfloat16)
@@ -720,18 +1056,28 @@
     )
     grad_ext = jnp.where(handled[:, None], extend(grad_one_low, halo_grad), 0)
     grad_context = mm(w_out, grad_ext, NT).astype(jnp.bfloat16)
-    grad_w_out = mm(context, grad_ext, NN)
-    grad_q, grad_k, grad_v = attend_back(
-        lo, hi, qkv, grad_context, context, logs, qaug, kaug, hidden_keys
-    )
+    grad_w_out = scatter_rows(context, grad_ext, NN, (1, n_tensor, per, 4, 2, 16))
+    half_heads = (3, n_tensor, per // 2, 4, 2, 16)
+    parts = []
+    grad_w_qkv = []
+    for first in range(2):
+        part = attend_back(
+            lo, hi, qkv, grad_context, context, logs, qaug, kaug, hidden_keys, first, 2
+        )
+        parts.append(part)
+        grad_w_qkv.append(
+            scatter_rows(jnp.concatenate(part, axis=0), tokens_ext, NN, half_heads)
+        )
+    grad_w_qkv = jnp.concatenate(
+        [g.reshape(3, per // 2, 16, D // 2) for g in grad_w_qkv], axis=1
+    ).reshape(3 * per, 16, D // 2)
+
+    def whole(index):
+        pair = [part[index].reshape(n_tensor, -1, ext) for part in parts]
+        return jnp.concatenate(pair, axis=1).reshape(D, ext)
+
+    grad_q, grad_k, grad_v = whole(0), whole(1), whole(2)
     grad_qkv = jnp.concatenate([grad_q, grad_k, grad_v], axis=0)
-    grad_w_qkv = mm(grad_qkv, tokens_ext, NN)
-    grad_w_mix = jnp.concatenate([grad_w_qkv, grad_w_out], axis=0).astype(jnp.bfloat16)
-    grad_w_mix = scatter(
-        grad_w_mix.reshape(4, n_tensor, per, n_dp, chunk, D)
-        .transpose(1, 3, 0, 2, 4, 5)
-        .reshape(4 * D, D)
-    )
     input_ext = mm(grad_qkv, w_qkv, TN)
     halo_input = lax.ppermute(halo_part(input_ext).astype(jnp.bfloat16), "tensor", swap)
     input_back = lax.dynamic_update_slice_in_dim(
@@ -741,21 +1087,12 @@
         jnp.bfloat16
     )
 
-    up_sum = (
-        jnp.sum(grad_pre.astype(jnp.float32), axis=0)
-        .reshape(n_tensor, n_dp, up_pieces, chunk)
-        .transpose(0, 2, 1, 3)
-        .reshape(FF // D, D)
-    )
-    vector_terms = jnp.concatenate(
+    early_terms = jnp.concatenate(
         [
-            jnp.stack(
-                [
-                    jnp.sum(grad_q.astype(jnp.float32), axis=1),
-                    jnp.sum(grad_v.astype(jnp.float32), axis=1),
-                ]
-            ),
-            up_sum,
+            jnp.sum(grad_pre.astype(jnp.float32), axis=0)
+            .reshape(4, n_tensor, -1)
+            .transpose(1, 0, 2)
+            .reshape(FF // D, D),
             jnp.stack(
                 [
                     jnp.sum(grad_one, axis=0),
@@ -769,18 +1106,23 @@
         ],
         axis=0,
     )
-    vector_grads = lax.psum(vector_terms, ("dp", "tensor"))
-
-    grad_chunks = jnp.concatenate([grad_w_mix, grad_w_up, grad_w_down], axis=0).reshape(
-        pieces, chunk, D
-    )
+    late_terms = jnp.stack(
+        [
+            jnp.sum(grad_q.astype(jnp.float32), axis=1),
+            jnp.sum(grad_v.astype(jnp.float32), axis=1),
+        ]
+    )
+    vector_grads = jnp.concatenate([sum_all(late_terms), sum_all(early_terms)], axis=0)
+
+    grad_chunks = jnp.concatenate([grad_w_qkv, grad_w_out, grad_w_up, grad_w_down], axis=0)
     piece_of = jnp.full((n_dp * CAP,), pieces, jnp.int32).at[slots].set(
         jnp.arange(pieces, dtype=jnp.int32)
     )
-    padded = jnp.concatenate([grad_chunks, jnp.zeros((1, chunk, D), jnp.bfloat16)], axis=0)
-    outgoing = jnp.take(padded, piece_of, axis=0).reshape(n_dp, CAP, chunk, D)
+    padded = jnp.concatenate([grad_chunks, jnp.zeros((1, 16, D // 2), jnp.bfloat16)], axis=0)
+    outgoing = jnp.take(padded, piece_of, axis=0).reshape(n_dp, CAP, 16, D // 2)
     incoming = lax.all_to_all(outgoing, "dp", 0, 0, tiled=False)
-    own_grads = incoming.transpose(1, 0, 2, 3).reshape(CAP, piece_rows, D).astype(jnp.float32)
+    own_grads = incoming.reshape(8, 2, CAP, 16, D // 2).transpose(2, 0, 3, 1, 4)
+    own_grads = own_grads.reshape(CAP, piece_rows, D).astype(jnp.float32)
     slot_new, slot_first_new, slot_second_new = adam_update(
         master_slots[0], slot_first[0], slot_second[0], own_grads, rate_matrix, weight_decay
     )
@@ -813,9 +1155,9 @@
         P(),
         P(("dp", "tensor"), None),
     )
-    two_halves = mesh.shape["tensor"] == 2
+    by_rows = mesh.shape["tensor"] == 2 and mesh.shape["dp"] == 16
     return jax.shard_map(
-        on_device_rows if two_halves else on_device_generic,
+        on_device_rows if by_rows else on_device_generic,
         mesh=mesh,
         in_specs=placed,
         out_specs=(

time: 984 us -> 876 us (0.89)
  waiting for transfers between devices: 427 us -> 131 us
  starting transfers between devices: 68.7 us -> 213 us
  Pallas kernels: 125 us -> 256 us
  blocking collectives: 46.8 us -> 0 us
  matrix products: 199 us -> 183 us
  local copies, waits for them, and re-layouts: 56.1 us -> 42.7 us
  between operations: 16.5 us -> 4.07 us
    reduce_scatter x3 -> x0, waiting for transfers between devices: 274 us -> none  [scatter(): return lax.psum_scatter(part, every, scatter_dimension=0, tiled=True)]
    ppermute x0 -> x45, starting transfers between devices: none -> 153 us  [the longest x33 144 us: exchange(): lax.ppermute(values, 'dp', [(i, i ^ flip) for i in range(lax.axis_size('d...]
    pallas_call x0 -> x1, Pallas kernels: none -> 147 us  [gather_weights(): pl.pallas_call(gather_kernel, out_shape=(stack,) * 3, in_specs=[pl.BlockS...]
    ppermute x0 -> x45, waiting for transfers between devices: none -> 124 us  [the longest x33 93.2 us: exchange(): lax.ppermute(values, 'dp', [(i, i ^ flip) for i in range(lax.axis_size('d...]
    all_gather x3 -> x0, waiting for transfers between devices: 50.5 us -> none  [gather(): return lax.all_gather(part.reshape(-1, D), every, axis=0, tiled=True)]
    psum x1 -> x0, blocking collectives: 46.8 us -> none  [on_device_rows(): vector_grads = lax.psum(vector_terms, ('dp', 'tensor'))]
    all_to_all x1 -> x0, waiting for transfers between devices: 36 us -> none  [on_device_rows(): lax.all_to_all(low_slots.transpose(1, 0, 2, 3), 'dp', 0, 0, tiled=False)]
    ppermute x1, waiting for transfers between devices: 32.5 us -> 7.53 us  [on_device_rows(): halo_attn = lax.ppermute(halo_part(attn_ext), 'tensor', swap)]
  transfers between devices with their start and end apart: 12 -> 50, of which waited for: 7 -> 26; matrix products, arithmetic and copies ran while one was open for 20% -> 13% of each run, Pallas kernels for 13% -> 23%
where the time goes in v2:
time: 876 us; the launch traced here: 879 us
  Pallas kernels  256 us (29%)
  starting transfers between devices  213 us (24%)
  matrix products  183 us (21%)
  waiting for transfers between devices  131 us (15%)
  other arithmetic  48.6 us (6%)
  local copies, waits for them, and re-layouts  42.7 us (5%)
    dot_general x18, matrix products, mm(): return lax.dot_general(a, b, dims, preferred_element_type=jnp.float32)  183 us
    pallas_call x1, Pallas kernels, gather_weights(): pl.pallas_call(gather_kernel, out_shape=(stack,) * 3, in_specs=[pl.BlockS...  147 us
    ppermute x33, starting transfers between devices, exchange(): lax.ppermute(values, 'dp', [(i, i ^ flip) for i in range(lax.axis_size('d...  144 us
    ppermute x33, waiting for transfers between devices, exchange(): lax.ppermute(values, 'dp', [(i, i ^ flip) for i in range(lax.axis_size('d...  93.2 us
    pallas_call x2, Pallas kernels, attend_back(): pl.pallas_call(attn_bwd_kernel, out_shape=(out, out, out), grid_spec=pltp...  57.9 us
    pallas_call x1, Pallas kernels, attend(): pl.pallas_call(attn_fwd_kernel, out_shape=(jax.ShapeDtypeStruct((D, ext),...  51.2 us
    ppermute x1, starting transfers between devices, on_device_rows(): halo_attn = lax.ppermute(halo_part(attn_ext), 'tensor', swap)  43.3 us
    ppermute x12, waiting for transfers between devices, exchange(): return lax.ppermute(values, 'tensor', [(0, 1), (1, 0)])  30.3 us
  transfers between devices with their start and end apart: 50, of which 26 were waited for; matrix products, arithmetic and copies ran while one was open for 13% of the time, Pallas kernels for 23%

profile of v2, /device:TPU:13, one launch (start us, length us, event | category | flops | bytes accessed | tf_op | source)
XLA Modules:
  0.0 878.5 jit_solution(17631649338656983707)
XLA Ops:
  16.3 146.6 %gather_weights.1 = (bf16[4,2,4,128,1024]{4,3,2,1,0:T(8,128)(2,1)S(1)}, bf16[4,2,4,128,1024]{4,3,2,1,0:T(8,128)(2,1)S(1)}, bf16[4,2,4,128,1024]{4,3,2,1,0:T(8,128)(2,1)}) custom-call(s32[48]{0:T(128)S(1)} %multiply_add_fusion.3.slots_ref, bf16[16,6,16,512]{3,2,1,0:T(8,128)(2,1)S(1)} %bitcast.370), custom_call_target="tpu_custom_call" | custom-call | bytes 50000000 | tf_op jit(solution)/shard_map/gather_weights/pallas_call | solution.py:875
  162.9 3.3 copy-done.6
  166.3 3.4 slice.65
  176.2 12.0 %multiply_convert_fusion.q_ref.k_ref.v_ref = bf16[3072,1536]{1,0:T(8,128)(2,1)S(1)} fusion(bf16[3072,1024]{1,0:T(8,128)(2,1)S(1)} %bitcast.390, bf16[1536,1024]{1,0:T(8,128)(2,1)} %copy-done.21, f32[3072]{0:T(1024)S(1)} %copy-done.42, f32[3072]{0:T(1024)S(1)} %pad_maximum_fusion.5), kind=kOutput, calls=%fused_computation.3 | convolution fusion | flops 9677832192 | bytes 18898944 | tf_op jit(solution)/shard_map/dot_general | solution.py:347
  188.2 51.2 %attend.1 = (bf16[1024,1536]{1,0:T(8,128)(2,1)S(1)}, f32[4,8,1536]{2,1,0:T(8,128)S(1)}) custom-call(s32[6]{0:T(128)S(1)} %get-tuple-element.85.lo_ref, s32[6]{0:T(128)S(1)} %get-tuple-element.84.hi_ref, bf16[3072,1536]{1,0:T(8,128)(2,1)S(1)} %multiply_convert_fusion.q_ref.k_ref.v_ref, bf16[3072,1536]{1,0:T(8,128)(2,1)S(1)} %multiply_convert_fusion.q_ref.k_ref.v_ref, ...), custom_call_target="tpu_custom_call" | custom-call | flops 20000000000 | bytes 14000000 | tf_op jit(solution)/shard_map/attend/pallas_call | solution.py:492
  239.5 3.7 convolution_convert_fusion.3
  245.2 43.3 %collective-permute-start.1 = (bf16[400,1024]{1,0:T(8,128)(2,1)}, bf16[400,1024]{1,0:T(8,128)(2,1)S(1)}, u32[]{:S(2)}, u32[]{:S(2)}) collective-permute-start(bf16[400,1024]{1,0:T(8,128)(2,1)} %constant_dynamic-slice_fusion.10), channel_id=1, source_target_pairs={{0,1},{1,0},{2,3},{3,2},{4,5},{5,4},{6,7},{7,6},{8,9},{9,8},{10,11... | collective-permute-start | bytes 2457608 | tf_op jit(solution)/shard_map/ppermute | solution.py:1025
  290.9 7.5 collective-permute-done.1
  303.6 46.2 %multiply_convert_fusion.2 = (bf16[1024,4096]{1,0:T(8,128)(2,1)S(1)}, f32[1024,4096]{1,0:T(8,128)}, f32[1024,4096]{1,0:T(8,128)}) fusion(f32[4096]{0:T(1024)S(1)} %bitcast.452, bf16[1024,1024]{1,0:T(8,128)(2,1)S(1)} %fusion.21, bf16[4096,1024]{1,0:T(8,128)(2,1)S(1)} %bitcast.376), kind=kOutput, calls=%fused_computation.9 | convolution fusion | flops 8862564352 | bytes 52445184 | tf_op jit(solution)/shard_map/dot_general | solution.py:347
  349.9 9.4 %fusion.159 = (f32[1024]{0:T(1024)S(1)}, f32[1024,1024]{1,0:T(8,128)S(1)}) fusion(f32[1024]{0:T(1024)S(1)} %bitcast.460, bf16[1024,4096]{1,0:T(8,128)(2,1)S(1)} %get-tuple-element.54, bf16[4096,1024]{1,0:T(8,128)(2,1)S(1)} %bitcast.466, f32[1024]{0:T(1024)S(1)} %bitcast.457, f32[1024]{0:T(1024)S(1)} %bitcast.442, f32[1024]{0:T(1024)S(1)} %add_rsqrt_fusion.1, ...), kind=kOutput, calls=%fused_computation.357 | convolution fusion | flops 8601467904 | bytes 25194496 | tf_op jit(solution)/shard_map/dot_general | solution.py:347
  363.2 3.0 fusion.147
  369.7 22.8 %convert_reduce_fusion = (f32[4096]{0:T(1024)S(1)}, bf16[1024,4096]{1,0:T(8,128)(2,1)}) fusion(f32[1024,4096]{1,0:T(8,128)} %get-tuple-element.55, f32[1024,4096]{1,0:T(8,128)} %get-tuple-element.86, f32[4096]{0:T(1024)S(1)} %bitcast.453, bf16[1024,1024]{1,0:T(8,128)(2,1)} %convert_element_type.941, bf16[4096,1024]{1,0:T(8,128)(2,1)} %bitcast.463), kind=kOutput, calls=%fused_computation.6 | convolution fusion | flops 8640262144 | bytes 52461568 | tf_op jit(solution)/shard_map/dot_general | solution.py:347
  392.6 17.8 %multiply_reduce_fusion = (f32[1024]{0:T(1024)S(1)}, f32[1024]{0:T(1024)S(1)}, f32[1024]{0:T(1024)S(1)}, f32[1024]{0:T(1024)S(1)}, f32[1024,1024]{1,0:T(8,128)S(1)}) fusion(f32[1024]{0:T(1024)S(1)} %add_rsqrt_fusion.1, f32[1024]{0:T(1024)S(1)} %broadcast_multiply_fusion.5, f32[1024]{0:T(1024)S(1)} %bitcast.428, bf16[1024,1024]{1,0:T(8,128)(2,1)} %copy-done.14, ...), kind=kOutput, calls=%fused_computation.47 | convolution fusion | flops 8604610560 | bytes 29392896 | tf_op jit(solution)/shard_map/dot_general | solution.py:347
  417.6 14.9 %collective-permute-start.44 = (f32[10,1024]{1,0:T(8,128)S(1)}, f32[10,1024]{1,0:T(8,128)S(1)}, u32[]{:S(2)}, u32[]{:S(2)}) collective-permute-start(f32[10,1024]{1,0:T(8,128)S(1)} %concatenate.118), channel_id=1, source_target_pairs={{0,2},{2,0},{4,6},{6,4},{8,10},{10,8},{12,14},{14,12},{16,18},{18,... | collective-permute-start | bytes 122888 | tf_op jit(solution)/shard_map/ppermute | solution.py:916
  432.5 10.3 %convolution_convert_fusion = bf16[4096,512]{1,0:T(8,128)(2,1)} fusion(bf16[1024,4096]{1,0:T(8,128)(2,1)} %copy-done.43, bf16[1024,1024]{1,0:T(8,128)(2,1)} %convert_element_type.941, s32[]{:T(128)S(6)} %select_n.375), kind=kOutput, calls=%fused_computation.36 | convolution fusion | flops 4297064448 | bytes 13631492 | tf_op jit(solution)/shard_map/dot_general | solution.py:347
  442.9 9.8 %convolution_convert_fusion.1 = bf16[4096,512]{1,0:T(8,128)(2,1)} fusion(bf16[1024,4096]{1,0:T(8,128)(2,1)} %get-tuple-element.91, bf16[1024,1024]{1,0:T(8,128)(2,1)S(1)} %copy-done.29, s32[]{:T(128)S(6)} %select_n.375), kind=kOutput, calls=%fused_computation.37 | convolution fusion | flops 4297064448 | bytes 13631492 | tf_op jit(solution)/shard_map/dot_general | solution.py:347
  457.0 4.8 convolution_convert_fusion.2.g_ref
  461.8 28.6 %attend_back.2 = (bf16[512,1536]{1,0:T(8,128)(2,1)S(1)}, bf16[512,1536]{1,0:T(8,128)(2,1)S(1)}, bf16[512,1536]{1,0:T(8,128)(2,1)S(1)}) custom-call(s32[6]{0:T(128)S(1)} %get-tuple-element.85.lo_ref, s32[6]{0:T(128)S(1)} %get-tuple-element.84.hi_ref, bf16[3072,1536]{1,0:T(8,128)(2,1)} %copy-done.9, bf16[3072,1536]{1,0:T(8,128)(2,1)} %copy-done.9, ...), custom_call_target="tpu_custom_call" | custom-call | flops 49999998976 | bytes 30000000 | tf_op jit(solution)/shard_map/attend_back/pallas_call | solution.py:535
  490.4 29.3 %attend_back.3 = (bf16[512,1536]{1,0:T(8,128)(2,1)S(1)}, bf16[512,1536]{1,0:T(8,128)(2,1)S(1)}, bf16[512,1536]{1,0:T(8,128)(2,1)S(1)}) custom-call(s32[6]{0:T(128)S(1)} %get-tuple-element.85.lo_ref, s32[6]{0:T(128)S(1)} %get-tuple-element.84.hi_ref, bf16[3072,1536]{1,0:T(8,128)(2,1)} %copy-done.9, bf16[3072,1536]{1,0:T(8,128)(2,1)} %copy-done.9, ...), custom_call_target="tpu_custom_call" | custom-call | flops 49999998976 | bytes 30000000 | tf_op jit(solution)/shard_map/attend_back/pallas_call | solution.py:535
  519.8 3.2 fusion.30
  523.0 54.0 %collective-permute-start.18 = (bf16[1024,512]{1,0:T(8,128)(2,1)S(1)}, bf16[1024,512]{1,0:T(8,128)(2,1)S(1)}, u32[]{:S(2)}, u32[]{:S(2)}) collective-permute-start(bf16[1024,512]{1,0:T(8,128)(2,1)S(1)} %fusion.30), channel_id=1, source_target_pairs={{0,2},{2,0},{4,6},{6,4},{8,10},{10,8},{12,14},{14,12},{16,18},{18,... | collective-permute-start | bytes 3145736 | tf_op jit(solution)/shard_map/ppermute | solution.py:916
  578.9 2.7 convolution_convert_fusion.5
  587.6 2.7 convolution_convert_fusion.4
  592.9 6.8 collective-permute-done.21
  604.0 3.4 collective-permute-done.20
  607.5 57.0 %collective-permute-start.23 = (bf16[1,4,2,16,512]{4,3,1,2,0:T(8,128)(2,1)S(1)}, bf16[1,4,2,16,512]{4,3,1,2,0:T(8,128)(2,1)S(1)}, u32[]{:S(2)}, u32[]{:S(2)}) collective-permute-start(bf16[1,4,2,16,512]{4,3,1,2,0:T(8,128)(2,1)S(1)} %copy_bitcast_fusion.11), channel_id=1, source_target_pairs={{0,16},{2,18},{4,20},{6,22},{8,24},{10,26},{12,28},{14,30},{16,0},... | collective-permute-start | bytes 393224 | tf_op jit(solution)/shard_map/ppermute | solution.py:916
  664.5 2.7 fusion.24
  669.0 2.9 fusion.25
  672.7 2.6 collective-permute-done.7
  677.0 6.7 collective-permute-done.14
  686.7 2.5 collective-permute-done.6
  692.5 9.5 %add_convert_fusion.2 = bf16[4096,512]{1,0:T(8,128)(2,1)S(1)} fusion(bf16[4096,512]{1,0:T(8,128)(2,1)} %collective-permute-done.25, bf16[1024,4096]{1,0:T(8,128)(2,1)} %get-tuple-element.91, bf16[1024,1024]{1,0:T(8,128)(2,1)S(1)} %copy-done.30, s32[]{:T(128)S(6)} %select_n.374), kind=kOutput, calls=%fused_computation.30 | convolution fusion | flops 4301258752 | bytes 17825796 | tf_op jit(solution)/shard_map/dot_general | solution.py:347
  704.5 6.4 add_convert_fusion.1
  713.5 3.7 collective-permute-done.10
  724.1 17.4 %collective-permute-done.35 = bf16[4,2,2,4,16,512]{5,4,3,2,0,1:T(8,128)(2,1)S(1)} collective-permute-done((bf16[4,2,2,4,16,512]{5,4,3,2,0,1:T(8,128)(2,1)S(1)}, bf16[4,2,2,4,16,512]{5,4,3,2,0,1:T(8,128)(2,1)S(1)}, u32[]{:S(2)}, u32[]{:S(2)}) %collective-permute-start.35) | collective-permute-done | bytes 1048608 | tf_op jit(solution)/shard_map/ppermute | solution.py:916
  744.2 11.1 %collective-permute-done.29 = bf16[4,2,4,16,512]{4,3,2,1,0:T(8,128)(2,1)S(1)} collective-permute-done((bf16[4,2,4,16,512]{4,3,2,1,0:T(8,128)(2,1)S(1)}, bf16[4,2,4,16,512]{4,3,2,1,0:T(8,128)(2,1)S(1)}, u32[]{:S(2)}, u32[]{:S(2)}) %collective-permute-start.29) | collective-permute-done | bytes 524320 | tf_op jit(solution)/shard_map/ppermute | solution.py:914
  758.0 8.6 collective-permute-done.36
  769.6 13.8 %collective-permute-done.30 = bf16[4,4,2,16,512]{4,3,1,0,2:T(8,128)(2,1)S(1)} collective-permute-done((bf16[4,4,2,16,512]{4,3,1,0,2:T(8,128)(2,1)S(1)}, bf16[4,4,2,16,512]{4,3,1,0,2:T(8,128)(2,1)S(1)}, u32[]{:S(2)}, u32[]{:S(2)}) %collective-permute-start.30) | collective-permute-done | bytes 524320 | tf_op jit(solution)/shard_map/ppermute | solution.py:916
  783.6 11.1 %collective-permute-done.37 = bf16[4,4,2,16,512]{4,3,1,0,2:T(8,128)(2,1)S(1)} collective-permute-done((bf16[4,4,2,16,512]{4,3,1,0,2:T(8,128)(2,1)S(1)}, bf16[4,4,2,16,512]{4,3,1,0,2:T(8,128)(2,1)S(1)}, u32[]{:S(2)}, u32[]{:S(2)}) %collective-permute-start.37) | collective-permute-done | bytes 524320 | tf_op jit(solution)/shard_map/ppermute | solution.py:916
  795.0 7.9 collective-permute-done.38
  805.3 13.5 %all-to-all-start = ((bf16[16,6,16,512]{3,2,1,0:T(8,128)(2,1)}), bf16[16,6,16,512]{3,2,1,0:T(8,128)(2,1)S(1)}, u32[]{:S(2)}, u32[]{:S(2)}) async-start(bf16[16,6,16,512]{3,2,1,0:T(8,128)(2,1)} %broadcast_select_fusion.1), calls=%async_computation | async-start | bytes 3145728 | tf_op jit(solution)/shard_map/all_to_all | solution.py:1123
  818.8 14.1 %fusion.8 = f32[1536,1024]{1,0:T(8,128)S(1)} fusion(bf16[3072,1024]{1,0:T(8,128)(2,1)} %bitcast.389, bf16[1024,1536]{1,0:T(8,128)(2,1)} %bitcast.397, bf16[1024,1536]{1,0:T(8,128)(2,1)} %bitcast.396, bf16[1024,1536]{1,0:T(8,128)(2,1)} %bitcast.395), kind=kOutput, calls=%fused_computation.23 | convolution fusion | flops 9691987968 | bytes 22020096 | tf_op jit(solution)/shard_map/dot_general | solution.py:347
  836.2 10.6 %collective-permute-done.47 = f32[10,1024]{1,0:T(8,128)S(1)} collective-permute-done((f32[10,1024]{1,0:T(8,128)S(1)}, f32[10,1024]{1,0:T(8,128)S(1)}, u32[]{:S(2)}, u32[]{:S(2)}) %collective-permute-start.47) | collective-permute-done | bytes 40992 | tf_op jit(solution)/shard_map/ppermute | solution.py:916
  849.3 3.6 collective-permute-done.41
  860.1 2.7 add_convert_fusion.3
  863.2 2.8 copy.144
  866.0 3.8 reshape.945
  869.8 8.3 multiply_subtract_fusion
  (345 shorter events, 110.3 us)
Async XLA Ops:
  2.7 169.6 %collective-permute-start = (bf16[400,1024]{1,0:T(8,128)(2,1)}, bf16[400,1024]{1,0:T(8,128)(2,1)}, u32[]{:S(2)}, u32[]{:S(2)}) collective-permute-start(bf16[400,1024]{1,0:T(8,128)(2,1)} %constant_dynamic-slice_fusion.12), channel_id=1, source_target_pairs={{0,1},{1,0},{2,3},{3,2},{4,5},{5,4},{6,7},{7,6},{8,9},{9,8},{10,11... | collective-permute-start | bytes 2457608 | tf_op jit(solution)/shard_map/ppermute | solution.py:1000
  245.2 53.2 %collective-permute-start.1 = (bf16[400,1024]{1,0:T(8,128)(2,1)}, bf16[400,1024]{1,0:T(8,128)(2,1)S(1)}, u32[]{:S(2)}, u32[]{:S(2)}) collective-permute-start(bf16[400,1024]{1,0:T(8,128)(2,1)} %constant_dynamic-slice_fusion.10), channel_id=1, source_target_pairs={{0,1},{1,0},{2,3},{3,2},{4,5},{5,4},{6,7},{7,6},{8,9},{9,8},{10,11... | collective-permute-start | bytes 2457608 | tf_op jit(solution)/shard_map/ppermute | solution.py:1025
  416.0 37.9 %collective-permute-start.2 = (bf16[400,1024]{1,0:T(8,128)(2,1)}, bf16[400,1024]{1,0:T(8,128)(2,1)S(1)}, u32[]{:S(2)}, u32[]{:S(2)}) collective-permute-start(bf16[400,1024]{1,0:T(8,128)(2,1)} %constant_dynamic-slice_fusion.9), channel_id=1, source_target_pairs={{0,1},{1,0},{2,3},{3,2},{4,5},{5,4},{6,7},{7,6},{8,9},{9,8},{10,11... | collective-permute-start | bytes 2457608 | tf_op jit(solution)/shard_map/ppermute | solution.py:1054
  417.6 25.2 %collective-permute-start.44 = (f32[10,1024]{1,0:T(8,128)S(1)}, f32[10,1024]{1,0:T(8,128)S(1)}, u32[]{:S(2)}, u32[]{:S(2)}) collective-permute-start(f32[10,1024]{1,0:T(8,128)S(1)} %concatenate.118), channel_id=1, source_target_pairs={{0,2},{2,0},{4,6},{6,4},{8,10},{10,8},{12,14},{14,12},{16,18},{18,... | collective-permute-start | bytes 122888 | tf_op jit(solution)/shard_map/ppermute | solution.py:916
  442.8 10.4 %collective-permute-start.45 = (f32[10,1024]{1,0:T(8,128)S(1)}, f32[10,1024]{1,0:T(8,128)S(1)}, u32[]{:S(2)}, u32[]{:S(2)}) collective-permute-start(f32[10,1024]{1,0:T(8,128)S(1)} %add.973), channel_id=1, source_target_pairs={{0,4},{2,6},{4,0},{6,2},{8,12},{10,14},{12,8},{14,10},{16,20},{18,... | collective-permute-start | bytes 122888 | tf_op jit(solution)/shard_map/ppermute | solution.py:916
  452.7 251.8 %collective-permute-start.32 = (bf16[4096,512]{1,0:T(8,128)(2,1)}, bf16[4096,512]{1,0:T(8,128)(2,1)}, u32[]{:S(2)}, u32[]{:S(2)}) collective-permute-start(bf16[4096,512]{1,0:T(8,128)(2,1)} %convolution_convert_fusion), channel_id=1, source_target_pairs={{0,2},{2,0},{4,6},{6,4},{8,10},{10,8},{12,14},{14,12},{16,18},{18,... | collective-permute-start | bytes 12582920 | tf_op jit(solution)/shard_map/ppermute | solution.py:916
  452.8 239.7 %collective-permute-start.25 = (bf16[4096,512]{1,0:T(8,128)(2,1)}, bf16[4096,512]{1,0:T(8,128)(2,1)}, u32[]{:S(2)}, u32[]{:S(2)}) collective-permute-start(bf16[4096,512]{1,0:T(8,128)(2,1)} %convolution_convert_fusion.1), channel_id=1, source_target_pairs={{0,2},{2,0},{4,6},{6,4},{8,10},{10,8},{12,14},{14,12},{16,18},{18,... | collective-permute-start | bytes 12582920 | tf_op jit(solution)/shard_map/ppermute | solution.py:916
  523.0 67.3 %collective-permute-start.18 = (bf16[1024,512]{1,0:T(8,128)(2,1)S(1)}, bf16[1024,512]{1,0:T(8,128)(2,1)S(1)}, u32[]{:S(2)}, u32[]{:S(2)}) collective-permute-start(bf16[1024,512]{1,0:T(8,128)(2,1)S(1)} %fusion.30), channel_id=1, source_target_pairs={{0,2},{2,0},{4,6},{6,4},{8,10},{10,8},{12,14},{14,12},{16,18},{18,... | collective-permute-start | bytes 3145736 | tf_op jit(solution)/shard_map/ppermute | solution.py:916
  581.6 82.9 %collective-permute-start.4 = (bf16[1536,512]{1,0:T(8,128)(2,1)S(1)}, bf16[1536,512]{1,0:T(8,128)(2,1)S(1)}, u32[]{:S(2)}, u32[]{:S(2)}) collective-permute-start(bf16[1536,512]{1,0:T(8,128)(2,1)S(1)} %convolution_convert_fusion.5), channel_id=1, source_target_pairs={{0,2},{2,0},{4,6},{6,4},{8,10},{10,8},{12,14},{14,12},{16,18},{18,... | collective-permute-start | bytes 4718600 | tf_op jit(solution)/shard_map/ppermute | solution.py:916
  592.2 7.5 collective-permute-start.21
  592.8 7.5 collective-permute-start.19
  599.7 3.9 collective-permute-start.22
  600.3 68.3 %collective-permute-start.11 = (bf16[1536,512]{1,0:T(8,128)(2,1)S(1)}, bf16[1536,512]{1,0:T(8,128)(2,1)S(1)}, u32[]{:S(2)}, u32[]{:S(2)}) collective-permute-start(bf16[1536,512]{1,0:T(8,128)(2,1)S(1)} %convolution_convert_fusion.4), channel_id=1, source_target_pairs={{0,2},{2,0},{4,6},{6,4},{8,10},{10,8},{12,14},{14,12},{16,18},{18,... | collective-permute-start | bytes 4718600 | tf_op jit(solution)/shard_map/ppermute | solution.py:916
  603.6 3.8 collective-permute-start.20
  607.5 64.6 %collective-permute-start.23 = (bf16[1,4,2,16,512]{4,3,1,2,0:T(8,128)(2,1)S(1)}, bf16[1,4,2,16,512]{4,3,1,2,0:T(8,128)(2,1)S(1)}, u32[]{:S(2)}, u32[]{:S(2)}) collective-permute-start(bf16[1,4,2,16,512]{4,3,1,2,0:T(8,128)(2,1)S(1)} %copy_bitcast_fusion.11), channel_id=1, source_target_pairs={{0,16},{2,18},{4,20},{6,22},{8,24},{10,26},{12,28},{14,30},{16,0},... | collective-permute-start | bytes 393224 | tf_op jit(solution)/shard_map/ppermute | solution.py:916
  667.5 7.8 collective-permute-start.7
  668.6 7.4 collective-permute-start.5
  672.1 11.5 %collective-permute-start.14 = (bf16[3,2,1,4,16,512]{5,4,3,0,2,1:T(8,128)(2,1)S(1)}, bf16[3,2,1,4,16,512]{5,4,3,0,2,1:T(8,128)(2,1)S(1)}, u32[]{:S(2)}, u32[]{:S(2)}) collective-permute-start(bf16[3,2,1,4,16,512]{5,4,3,0,2,1:T(8,128)(2,1)S(1)} %copy_bitcast_fusion.6), channel_id=1, source_target_pairs={{0,4},{2,6},{4,0},{6,2},{8,12},{10,14},{12,8},{14,10},{16,20},{18,... | collective-permute-start | bytes 1179656 | tf_op jit(solution)/shard_map/ppermute | solution.py:916
  675.3 9.3 %collective-permute-start.12 = (bf16[3,1,4,2,16,512]{5,4,2,0,3,1:T(8,128)(2,1)S(1)}, bf16[3,1,4,2,16,512]{5,4,2,0,3,1:T(8,128)(2,1)S(1)}, u32[]{:S(2)}, u32[]{:S(2)}) collective-permute-start(bf16[3,1,4,2,16,512]{5,4,2,0,3,1:T(8,128)(2,1)S(1)} %copy_bitcast_fusion.7), channel_id=1, source_target_pairs={{0,1},{1,0},{2,3},{3,2},{4,5},{5,4},{6,7},{7,6},{8,9},{9,8},{10,11... | collective-permute-start | bytes 1179656 | tf_op jit(solution)/shard_map/ppermute | solution.py:914
  676.0 10.5 %collective-permute-start.8 = (bf16[3,1,4,16,512]{4,3,2,0,1:T(8,128)(2,1)S(1)}, bf16[3,1,4,16,512]{4,3,2,0,1:T(8,128)(2,1)S(1)}, u32[]{:S(2)}, u32[]{:S(2)}) collective-permute-start(bf16[3,1,4,16,512]{4,3,2,0,1:T(8,128)(2,1)S(1)} %fusion.75), channel_id=1, source_target_pairs={{0,1},{1,0},{2,3},{3,2},{4,5},{5,4},{6,7},{7,6},{8,9},{9,8},{10,11... | collective-permute-start | bytes 589832 | tf_op jit(solution)/shard_map/ppermute | solution.py:914
  683.7 5.5 collective-permute-start.6
  684.6 7.0 collective-permute-start.15
  686.5 5.2 collective-permute-start.13
  689.4 23.7 %collective-permute-start.9 = (bf16[3,2,2,16,512]{4,3,1,0,2:T(8,128)(2,1)S(1)}, bf16[3,2,2,16,512]{4,3,1,0,2:T(8,128)(2,1)S(1)}, u32[]{:S(2)}, u32[]{:S(2)}) collective-permute-start(bf16[3,2,2,16,512]{4,3,1,0,2:T(8,128)(2,1)S(1)} %fusion.98), channel_id=1, source_target_pairs={{0,16},{2,18},{4,20},{6,22},{8,24},{10,26},{12,28},{14,30},{16,0},... | collective-permute-start | bytes 589832 | tf_op jit(solution)/shard_map/ppermute | solution.py:916
  691.9 21.5 %collective-permute-start.16 = (bf16[3,2,2,16,512]{4,3,1,0,2:T(8,128)(2,1)S(1)}, bf16[3,2,2,16,512]{4,3,1,0,2:T(8,128)(2,1)S(1)}, u32[]{:S(2)}, u32[]{:S(2)}) collective-permute-start(bf16[3,2,2,16,512]{4,3,1,0,2:T(8,128)(2,1)S(1)} %fusion.96), channel_id=1, source_target_pairs={{0,16},{2,18},{4,20},{6,22},{8,24},{10,26},{12,28},{14,30},{16,0},... | collective-permute-start | bytes 589832 | tf_op jit(solution)/shard_map/ppermute | solution.py:916
  703.0 16.1 %collective-permute-start.28 = (bf16[4,2,2,4,16,512]{5,4,3,2,0,1:T(8,128)(2,1)S(1)}, bf16[4,2,2,4,16,512]{5,4,3,2,0,1:T(8,128)(2,1)S(1)}, u32[]{:S(2)}, u32[]{:S(2)}) collective-permute-start(bf16[4,2,2,4,16,512]{5,4,3,2,0,1:T(8,128)(2,1)S(1)} %copy_bitcast_fusion.2), channel_id=1, source_target_pairs={{0,4},{2,6},{4,0},{6,2},{8,12},{10,14},{12,8},{14,10},{16,20},{18,... | collective-permute-start | bytes 3145736 | tf_op jit(solution)/shard_map/ppermute | solution.py:916
  704.0 16.2 %collective-permute-start.26 = (bf16[4,2,4,2,16,512]{5,4,2,1,0,3:T(8,128)(2,1)S(1)}, bf16[4,2,4,2,16,512]{5,4,2,1,0,3:T(8,128)(2,1)S(1)}, u32[]{:S(2)}, u32[]{:S(2)}) collective-permute-start(bf16[4,2,4,2,16,512]{5,4,2,1,0,3:T(8,128)(2,1)S(1)} %copy_bitcast_fusion.3), channel_id=1, source_target_pairs={{0,1},{1,0},{2,3},{3,2},{4,5},{5,4},{6,7},{7,6},{8,9},{9,8},{10,11... | collective-permute-start | bytes 3145736 | tf_op jit(solution)/shard_map/ppermute | solution.py:914
  711.5 30.0 %collective-permute-start.35 = (bf16[4,2,2,4,16,512]{5,4,3,2,0,1:T(8,128)(2,1)S(1)}, bf16[4,2,2,4,16,512]{5,4,3,2,0,1:T(8,128)(2,1)S(1)}, u32[]{:S(2)}, u32[]{:S(2)}) collective-permute-start(bf16[4,2,2,4,16,512]{5,4,3,2,0,1:T(8,128)(2,1)S(1)} %copy_bitcast_fusion), channel_id=1, source_target_pairs={{0,4},{2,6},{4,0},{6,2},{8,12},{10,14},{12,8},{14,10},{16,20},{18,... | collective-permute-start | bytes 3145736 | tf_op jit(solution)/shard_map/ppermute | solution.py:916
  713.1 29.6 %collective-permute-start.33 = (bf16[4,2,4,2,16,512]{5,4,2,1,0,3:T(8,128)(2,1)S(1)}, bf16[4,2,4,2,16,512]{5,4,2,1,0,3:T(8,128)(2,1)S(1)}, u32[]{:S(2)}, u32[]{:S(2)}) collective-permute-start(bf16[4,2,4,2,16,512]{5,4,2,1,0,3:T(8,128)(2,1)S(1)} %copy_bitcast_fusion.1), channel_id=1, source_target_pairs={{0,1},{1,0},{2,3},{3,2},{4,5},{5,4},{6,7},{7,6},{8,9},{9,8},{10,11... | collective-permute-start | bytes 3145736 | tf_op jit(solution)/shard_map/ppermute | solution.py:914
  713.4 3.8 collective-permute-start.10
  717.2 117.8 %collective-permute-start.46 = (f32[10,1024]{1,0:T(8,128)S(1)}, f32[10,1024]{1,0:T(8,128)S(1)}, u32[]{:S(2)}, u32[]{:S(2)}) collective-permute-start(f32[10,1024]{1,0:T(8,128)S(1)} %copy-done.31), channel_id=1, source_target_pairs={{0,1},{1,0},{2,3},{3,2},{4,5},{5,4},{6,7},{7,6},{8,9},{9,8},{10,11... | collective-permute-start | bytes 122888 | tf_op jit(solution)/shard_map/ppermute | solution.py:914
  719.0 3.8 collective-permute-start.17
  720.2 35.1 %collective-permute-start.29 = (bf16[4,2,4,16,512]{4,3,2,1,0:T(8,128)(2,1)S(1)}, bf16[4,2,4,16,512]{4,3,2,1,0:T(8,128)(2,1)S(1)}, u32[]{:S(2)}, u32[]{:S(2)}) collective-permute-start(bf16[4,2,4,16,512]{4,3,2,1,0:T(8,128)(2,1)S(1)} %fusion.45), channel_id=1, source_target_pairs={{0,1},{1,0},{2,3},{3,2},{4,5},{5,4},{6,7},{7,6},{8,9},{9,8},{10,11... | collective-permute-start | bytes 1572872 | tf_op jit(solution)/shard_map/ppermute | solution.py:914
  722.8 33.0 %collective-permute-start.27 = (bf16[4,2,4,16,512]{4,3,2,1,0:T(8,128)(2,1)S(1)}, bf16[4,2,4,16,512]{4,3,2,1,0:T(8,128)(2,1)S(1)}, u32[]{:S(2)}, u32[]{:S(2)}) collective-permute-start(bf16[4,2,4,16,512]{4,3,2,1,0:T(8,128)(2,1)S(1)} %fusion.48), channel_id=1, source_target_pairs={{0,4},{2,6},{4,0},{6,2},{8,12},{10,14},{12,8},{14,10},{16,20},{18,... | collective-permute-start | bytes 1572872 | tf_op jit(solution)/shard_map/ppermute | solution.py:916
  741.5 42.0 %collective-permute-start.24 = (bf16[1,4,16,512]{3,2,1,0:T(8,128)(2,1)S(1)}, bf16[1,4,16,512]{3,2,1,0:T(8,128)(2,1)S(1)}, u32[]{:S(2)}, u32[]{:S(2)}) collective-permute-start(bf16[1,4,16,512]{3,2,1,0:T(8,128)(2,1)S(1)} %fusion.106), channel_id=1, source_target_pairs={{0,8},{2,10},{4,12},{6,14},{8,0},{10,2},{12,4},{14,6},{16,24},{18,... | collective-permute-start | bytes 196616 | tf_op jit(solution)/shard_map/ppermute | solution.py:916
  742.7 23.9 %collective-permute-start.36 = (bf16[4,2,4,16,512]{4,3,2,1,0:T(8,128)(2,1)S(1)}, bf16[4,2,4,16,512]{4,3,2,1,0:T(8,128)(2,1)S(1)}, u32[]{:S(2)}, u32[]{:S(2)}) collective-permute-start(bf16[4,2,4,16,512]{4,3,2,1,0:T(8,128)(2,1)S(1)} %fusion.39), channel_id=1, source_target_pairs={{0,1},{1,0},{2,3},{3,2},{4,5},{5,4},{6,7},{7,6},{8,9},{9,8},{10,11... | collective-permute-start | bytes 1572872 | tf_op jit(solution)/shard_map/ppermute | solution.py:914
  755.3 12.2 %collective-permute-start.34 = (bf16[4,2,4,16,512]{4,3,2,1,0:T(8,128)(2,1)S(1)}, bf16[4,2,4,16,512]{4,3,2,1,0:T(8,128)(2,1)S(1)}, u32[]{:S(2)}, u32[]{:S(2)}) collective-permute-start(bf16[4,2,4,16,512]{4,3,2,1,0:T(8,128)(2,1)S(1)} %fusion.42), channel_id=1, source_target_pairs={{0,4},{2,6},{4,0},{6,2},{8,12},{10,14},{12,8},{14,10},{16,20},{18,... | collective-permute-start | bytes 1572872 | tf_op jit(solution)/shard_map/ppermute | solution.py:916
  756.1 27.2 %collective-permute-start.30 = (bf16[4,4,2,16,512]{4,3,1,0,2:T(8,128)(2,1)S(1)}, bf16[4,4,2,16,512]{4,3,1,0,2:T(8,128)(2,1)S(1)}, u32[]{:S(2)}, u32[]{:S(2)}) collective-permute-start(bf16[4,4,2,16,512]{4,3,1,0,2:T(8,128)(2,1)S(1)} %copy_bitcast_fusion.5), channel_id=1, source_target_pairs={{0,16},{2,18},{4,20},{6,22},{8,24},{10,26},{12,28},{14,30},{16,0},... | collective-permute-start | bytes 1572872 | tf_op jit(solution)/shard_map/ppermute | solution.py:916
  767.9 26.8 %collective-permute-start.37 = (bf16[4,4,2,16,512]{4,3,1,0,2:T(8,128)(2,1)S(1)}, bf16[4,4,2,16,512]{4,3,1,0,2:T(8,128)(2,1)S(1)}, u32[]{:S(2)}, u32[]{:S(2)}) collective-permute-start(bf16[4,4,2,16,512]{4,3,1,0,2:T(8,128)(2,1)S(1)} %copy_bitcast_fusion.4), channel_id=1, source_target_pairs={{0,16},{2,18},{4,20},{6,22},{8,24},{10,26},{12,28},{14,30},{16,0},... | collective-permute-start | bytes 1572872 | tf_op jit(solution)/shard_map/ppermute | solution.py:916
  783.5 11.4 %collective-permute-start.31 = (bf16[4,4,16,512]{3,2,1,0:T(8,128)(2,1)S(1)}, bf16[4,4,16,512]{3,2,1,0:T(8,128)(2,1)S(1)}, u32[]{:S(2)}, u32[]{:S(2)}) collective-permute-start(bf16[4,4,16,512]{3,2,1,0:T(8,128)(2,1)S(1)} %fusion.66), channel_id=1, source_target_pairs={{0,8},{2,10},{4,12},{6,14},{8,0},{10,2},{12,4},{14,6},{16,24},{18,... | collective-permute-start | bytes 786440 | tf_op jit(solution)/shard_map/ppermute | solution.py:916
  794.8 8.2 collective-permute-start.38
  805.3 57.5 %all-to-all-start = ((bf16[16,6,16,512]{3,2,1,0:T(8,128)(2,1)}), bf16[16,6,16,512]{3,2,1,0:T(8,128)(2,1)S(1)}, u32[]{:S(2)}, u32[]{:S(2)}) async-start(bf16[16,6,16,512]{3,2,1,0:T(8,128)(2,1)} %broadcast_select_fusion.1), calls=%async_computation | async-start | bytes 3145728 | tf_op jit(solution)/shard_map/all_to_all | solution.py:1123
  833.1 26.7 %collective-permute-start.3 = (bf16[400,1024]{1,0:T(8,128)(2,1)S(1)}, bf16[400,1024]{1,0:T(8,128)(2,1)S(1)}, u32[]{:S(2)}, u32[]{:S(2)}) collective-permute-start(bf16[400,1024]{1,0:T(8,128)(2,1)S(1)} %dynamic-slice_convert_fusion), channel_id=1, source_target_pairs={{0,1},{1,0},{2,3},{3,2},{4,5},{5,4},{6,7},{7,6},{8,9},{9,8},{10,11... | collective-permute-start | bytes 2457608 | tf_op jit(solution)/shard_map/ppermute | solution.py:1082
  835.1 11.7 %collective-permute-start.47 = (f32[10,1024]{1,0:T(8,128)S(1)}, f32[10,1024]{1,0:T(8,128)S(1)}, u32[]{:S(2)}, u32[]{:S(2)}) collective-permute-start(f32[10,1024]{1,0:T(8,128)S(1)} %add.975), channel_id=1, source_target_pairs={{0,8},{2,10},{4,12},{6,14},{8,0},{10,2},{12,4},{14,6},{16,24},{18,... | collective-permute-start | bytes 122888 | tf_op jit(solution)/shard_map/ppermute | solution.py:916
  835.9 12.2 %collective-permute-start.40 = (f32[2,1024]{1,0:T(2,128)S(1)}, f32[2,1024]{1,0:T(2,128)S(1)}, u32[]{:S(2)}, u32[]{:S(2)}) collective-permute-start(f32[2,1024]{1,0:T(2,128)S(1)} %fusion.145), channel_id=1, source_target_pairs={{0,4},{2,6},{4,0},{6,2},{8,12},{10,14},{12,8},{14,10},{16,20},{18,... | collective-permute-start | bytes 24584 | tf_op jit(solution)/shard_map/ppermute | solution.py:916
  846.8 10.7 %collective-permute-start.48 = (f32[10,1024]{1,0:T(8,128)S(1)}, f32[10,1024]{1,0:T(8,128)S(1)}, u32[]{:S(2)}, u32[]{:S(2)}) collective-permute-start(f32[10,1024]{1,0:T(8,128)S(1)} %add.976), channel_id=1, source_target_pairs={{0,16},{2,18},{4,20},{6,22},{8,24},{10,26},{12,28},{14,30},{16,0},... | collective-permute-start | bytes 122888 | tf_op jit(solution)/shard_map/ppermute | solution.py:916
  848.1 4.8 collective-permute-start.41
  855.6 3.4 collective-permute-start.43
  (52 other events, 848.8 us)

commit v3 on v2

--- a/solution.py
+++ b/solution.py
@@ -335,7 +335,7 @@
 DOC_MAX = 800
 EXT_PAD = 512
 ABLK = 256
-HPG = 4
+HPG = 8
 AUG = 16
 neg_big = -1000000000.0
 NN = (((1,), (0,)), ((), ()))
@@ -375,16 +375,20 @@
 
             def key_block(kb, _):
                 ks = pl.ds(pl.multiple_of(kb * ABLK, ABLK), ABLK)
+                heads = [slice(h * HD, (h + 1) * HD) for h in range(HPG)]
+                scores = [
+                    mm(kn_ref[h, ks, :], jnp.concatenate([q_ref[heads[h], qs], qaug_ref[:, qs]], axis=0), NN)
+                    for h in range(HPG)
+                ]
+                olds = [m_ref[h] for h in range(HPG)]
+                news = [
+                    jnp.maximum(olds[h], jnp.max(scores[h], axis=0, keepdims=True)) for h in range(HPG)
+                ]
+                raised = [jnp.exp(scores[h] - news[h]).astype(jnp.bfloat16) for h in range(HPG)]
                 for h in range(HPG):
-                    rows = slice(h * HD, (h + 1) * HD)
-                    qa = jnp.concatenate([q_ref[rows, qs], qaug_ref[:, qs]], axis=0)
-                    s = mm(kn_ref[h, ks, :], qa, NN)
-                    old = m_ref[h]
-                    new = jnp.maximum(old, jnp.max(s, axis=0, keepdims=True))
-                    m_ref[h] = new
-                    p = jnp.exp(s - new).astype(jnp.bfloat16)
-                    va = jnp.concatenate([v_ref[rows, ks], ones], axis=0)
-                    acc_ref[h] = acc_ref[h] * jnp.exp(old - new) + mm(va, p, NN)
+                    m_ref[h] = news[h]
+                    va = jnp.concatenate([v_ref[heads[h], ks], ones], axis=0)
+                    acc_ref[h] = acc_ref[h] * jnp.exp(olds[h] - news[h]) + mm(va, raised[h], NN)
                 return 0
 
             lax.fori_loop(lo, hi, key_block, 0)
@@ -446,19 +450,27 @@
 
             def key_block(kb, _):
                 ks = pl.ds(pl.multiple_of(kb * ABLK, ABLK), ABLK)
-                for h in range(HPG):
-                    rows = slice(h * HD, (h + 1) * HD)
-                    q = q_ref[rows, qs]
-                    g = g_ref[rows, qs]
-                    qa = jnp.concatenate([q, qaug_ref[:, qs]], axis=0)
-                    s = mm(kn_ref[h, ks, :], qa, NN)
-                    p = jnp.exp(s - logs[h])
-                    dp = mm(vn_ref[h, ks, :], g, NN)
-                    ds = (p * (dp - deltas[h])).astype(jnp.bfloat16)
-                    pb = p.astype(jnp.bfloat16)
-                    dv_acc[rows, ks] += mm(g, pb, NT)
-                    dk_acc[rows, ks] += mm(q, ds, NT)
-                    acc_ref[h] += mm(k_ref[rows, ks], ds, NN)
+                heads = [slice(h * HD, (h + 1) * HD) for h in range(HPG)]
+                every = range(HPG)
+                qs_h = [q_ref[heads[h], qs] for h in every]
+                gs_h = [g_ref[heads[h], qs] for h in every]
+                scores = [
+                    mm(kn_ref[h, ks, :], jnp.concatenate([qs_h[h], qaug_ref[:, qs]], axis=0), NN)
+                    for h in every
+                ]
+                grads = [mm(vn_ref[h, ks, :], gs_h[h], NN) for h in every]
+                weights = [jnp.exp(scores[h] - logs[h]) for h in every]
+                low = [weights[h].astype(jnp.bfloat16) for h in every]
+                back = [
+                    (weights[h] * (grads[h] - deltas[h])).astype(jnp.bfloat16) for h in every
+                ]
+                v_new = [mm(gs_h[h], low[h], NT) for h in every]
+                k_new = [mm(qs_h[h], back[h], NT) for h in every]
+                q_new = [mm(k_ref[heads[h], ks], back[h], NN) for h in every]
+                for h in every:
+                    dv_acc[heads[h], ks] += v_new[h]
+                    dk_acc[heads[h], ks] += k_new[h]
+                    acc_ref[h] += q_new[h]
                 return 0
 
             lax.fori_loop(lo, hi, key_block, 0)
@@ -898,6 +910,344 @@
     )(slots, low)
 
 
+BLOCKS = 12
+
+
+def reduce_kernel(
+    piece_ref, vec_ref, far_qkv, far_out, far_up, far_down, near_qkv, near_out, near_up, near_down,
+    out_ref, sum_ref,
+    near_buf, core_in, x_in, y_in, x2_in, y2_in, line, up_in, down_in, done, parcel, vec_in, vec_out,
+    near_sem, local_sem, post, mail, send, recv, vec_send, vec_recv,
+):
+    z, y, core, x = coordinates()
+    near = neighbours(z, y, core, x)
+    me = lax.axis_index("dp")
+    n_dp = parcel.shape[0]
+    width = D // 2
+    greet_all(near, me, n_dp)
+
+    def from_hbm(refs, i, body):
+        for ref, first, count in zip(refs, (0, 3, 4, 8), (3, 1, 4, 4)):
+
+            @pl.when((i >= first) & (i < first + count))
+            def _here():
+                body(ref.at[i - first])
+
+    def remote(kind, i, link, src, dst):
+        return pltpu.make_async_remote_copy(
+            src_ref=src,
+            dst_ref=dst,
+            send_sem=send.at[kind, i],
+            recv_sem=recv.at[kind, i],
+            device_id=near[link],
+            device_id_type=MESH,
+        )
+
+    def core_copy(i, src):
+        return remote(0, i, "core", src, core_in.at[i])
+
+    def near_copy(i, src):
+        return pltpu.make_async_copy(src, near_buf.at[i], near_sem.at[i])
+
+    def x1(i):
+        return remote(1, i, "x", core_in.at[i, 1 - x, pl.ds(0, 2)], x_in.at[i])
+
+    def y1(i):
+        return remote(2, i, "y", core_in.at[i, :, pl.ds(2, 2), :, 1 - y], y_in.at[i])
+
+    def y2(i):
+        return remote(3, i, "y", x_in.at[i, :, :, 1 - y], y2_in.at[i])
+
+    def x2(i):
+        return remote(4, i, "x", y_in.at[i, 1 - x], x2_in.at[i])
+
+    def up(i, zz):
+        return remote(4 + zz, i, "up", up_in.at[i, zz], up_in.at[i, zz])
+
+    def down(i, zz):
+        return remote(8 + zz, i, "down", down_in.at[i, zz], down_in.at[i, zz])
+
+    def load(i):
+        from_hbm((far_qkv, far_out, far_up, far_down), i, lambda src: core_copy(i, src).start())
+        from_hbm((near_qkv, near_out, near_up, near_down), i, lambda src: near_copy(i, src).start())
+
+    def stage_one(i):
+        near_copy(i, near_buf.at[i]).wait()
+        core_copy(i, core_in.at[i]).wait_recv()
+
+        def add(j, _):
+            t, p = j // 4, j % 4
+            core_in[i, t, p] = core_in[i, t, p] + near_buf[i, t, p]
+            return 0
+
+        lax.fori_loop(0, 8, add, 0)
+        x1(i).start()
+        y1(i).start()
+
+    def stage_two(i):
+        x1(i).wait_recv()
+        y1(i).wait_recv()
+        for p in range(2):
+            x_in[i, p] = x_in[i, p] + core_in[i, x, p]
+        for t in range(2):
+            for p in range(2):
+                y_in[i, t, p] = y_in[i, t, p] + core_in[i, t, 2 + p, :, y]
+        y2(i).start()
+        x2(i).start()
+
+    def stage_three(i):
+        y2(i).wait_recv()
+        x2(i).wait_recv()
+        for p in range(2):
+            line[i, :, p] = x_in[i, p, :, y] + y2_in[i, p]
+            line[i, :, 2 + p] = y_in[i, x, p] + x2_in[i, p]
+
+    def stage_up(i):
+        for zz in range(1, 4):
+
+            @pl.when((z > 0) & (zz >= z))
+            def _arrived():
+                up(i, zz).wait_recv()
+
+            @pl.when((z > 0) & (zz > z))
+            def _add():
+                up_in[i, zz] = up_in[i, zz] + line[i, zz]
+
+            @pl.when(z == 0)
+            def _first():
+                up_in[i, zz] = line[i, zz]
+
+            @pl.when(zz > z)
+            def _on():
+                up(i, zz).start()
+
+    def stage_down(i):
+        for zz in range(3):
+
+            @pl.when((z < 3) & (zz <= z))
+            def _arrived():
+                down(i, zz).wait_recv()
+
+            @pl.when((z < 3) & (zz < z))
+            def _add():
+                down_in[i, zz] = down_in[i, zz] + line[i, zz]
+
+            @pl.when(z == 3)
+            def _first():
+                down_in[i, zz] = line[i, zz]
+
+            @pl.when(zz < z)
+            def _on():
+                down(i, zz).start()
+
+    def stage_last(i):
+        mine = pl.ds(i * 4, 4)
+
+        @pl.when(z == 0)
+        def _bottom():
+            done[mine] = line[i, 0] + down_in[i, 0]
+
+        @pl.when((z > 0) & (z < 3))
+        def _middle():
+            total = line[i, z].astype(jnp.float32) + up_in[i, z].astype(jnp.float32)
+            done[mine] = (total + down_in[i, z].astype(jnp.float32)).astype(jnp.bfloat16)
+
+        @pl.when(z == 3)
+        def _top():
+            done[mine] = line[i, 3] + up_in[i, 3]
+
+    def ended(i):
+        core_copy(i, core_in.at[i]).wait_send()
+        x1(i).wait_send()
+        y1(i).wait_send()
+        y2(i).wait_send()
+        x2(i).wait_send()
+        for zz in range(1, 4):
+
+            @pl.when(zz > z)
+            def _up():
+                up(i, zz).wait_send()
+
+        for zz in range(3):
+
+            @pl.when(zz < z)
+            def _down():
+                down(i, zz).wait_send()
+
+    z_one = z + 1 - 2 * lax.rem(z, 2)
+    z_two = lax.rem(z + 2, 4)
+    partners = [
+        near["core"],
+        near["y"],
+        near["x"],
+        {"dp": (z_one * 2 + y) * 2 + core, "tensor": x},
+        {"dp": (z_two * 2 + y) * 2 + core, "tensor": x},
+    ]
+
+    def swap(n):
+        return pltpu.make_async_remote_copy(
+            src_ref=vec_out.at[n],
+            dst_ref=vec_in.at[n],
+            send_sem=vec_send.at[n],
+            recv_sem=vec_recv.at[n],
+            device_id=partners[n],
+            device_id_type=MESH,
+        )
+
+    vec_out[0] = vec_ref[...]
+    for i in range(3):
+        load(i)
+
+    def step(s, _):
+        @pl.when(s + 3 < BLOCKS)
+        def _load():
+            load(s + 3)
+
+        @pl.when(s < BLOCKS)
+        def _one():
+            stage_one(s)
+
+        @pl.when((s >= 1) & (s < BLOCKS + 1))
+        def _two():
+            stage_two(s - 1)
+
+        @pl.when((s >= 2) & (s < BLOCKS + 2))
+        def _three():
+            stage_three(s - 2)
+
+        @pl.when((s - 3 - z >= 0) & (s - 3 - z < BLOCKS))
+        def _up():
+            stage_up(s - 3 - z)
+
+        @pl.when((s - 6 + z >= 0) & (s - 6 + z < BLOCKS))
+        def _down():
+            stage_down(s - 6 + z)
+
+        @pl.when(s >= 7)
+        def _last():
+            stage_last(s - 7)
+
+        for n in range(5):
+
+            @pl.when(s == n)
+            def _begin():
+                swap(n).start()
+
+            @pl.when(s == n + 1)
+            def _end():
+                swap(n).wait()
+                if n < 4:
+                    vec_out[n + 1] = vec_out[n] + vec_in[n]
+                else:
+                    sum_ref[...] = vec_out[n] + vec_in[n]
+
+        return 0
+
+    lax.fori_loop(0, BLOCKS + 7, step, 0)
+
+    def finish(i, _):
+        ended(i)
+        return 0
+
+    lax.fori_loop(0, BLOCKS, finish, 0)
+
+    done[BLOCKS * 4] = jnp.zeros((16, width), done.dtype)
+
+    def pack(n, _):
+        parcel[n // CAP, n % CAP] = done[piece_ref[n]]
+        return 0
+
+    lax.fori_loop(0, n_dp * CAP, pack, 0)
+
+    def place(of):
+        return out_ref.at[
+            :,
+            pl.ds(pl.multiple_of((of // 2) * 16, 16), 16),
+            pl.ds(pl.multiple_of((of % 2) * width, width), width),
+        ]
+
+    def letter(to):
+        return pltpu.make_async_remote_copy(
+            src_ref=parcel.at[to],
+            dst_ref=place(me),
+            send_sem=post.at[to],
+            recv_sem=mail.at[me],
+            device_id={"dp": to, "tensor": x},
+            device_id_type=MESH,
+        )
+
+    def answer(of):
+        return pltpu.make_async_remote_copy(
+            src_ref=parcel.at[of],
+            dst_ref=place(of),
+            send_sem=post.at[of],
+            recv_sem=mail.at[of],
+            device_id={"dp": of, "tensor": x},
+            device_id_type=MESH,
+        )
+
+    def post_one(i, _):
+        letter(lax.rem(me + i, n_dp)).start()
+        return 0
+
+    lax.fori_loop(1, n_dp, post_one, 0)
+    own = pltpu.make_async_copy(parcel.at[me], place(me), local_sem)
+    own.start()
+
+    def mail_one(i, _):
+        answer(lax.rem(me + i, n_dp)).wait_recv()
+        letter(lax.rem(me + i, n_dp)).wait_send()
+        return 0
+
+    lax.fori_loop(1, n_dp, mail_one, 0)
+    own.wait()
+
+
+def reduce_grads(piece_of, vec, far, near):
+    n_dp = piece_of.shape[0] // CAP
+    low = jnp.bfloat16
+    width = D // 2
+    anywhere = pl.BlockSpec(memory_space=pl.ANY)
+    vmem = pl.BlockSpec(memory_space=pltpu.VMEM)
+    return pl.pallas_call(
+        reduce_kernel,
+        out_shape=(
+            jax.ShapeDtypeStruct((CAP, 128, D), low),
+            jax.ShapeDtypeStruct(vec.shape, jnp.float32),
+        ),
+        in_specs=[pl.BlockSpec(memory_space=pltpu.SMEM), vmem] + [anywhere] * 8,
+        out_specs=(anywhere, vmem),
+        scratch_shapes=[
+            pltpu.VMEM((BLOCKS, 2, 4, 4, 2, 16, width), low),
+            pltpu.VMEM((BLOCKS, 2, 4, 4, 2, 16, width), low),
+            pltpu.VMEM((BLOCKS, 2, 4, 2, 16, width), low),
+            pltpu.VMEM((BLOCKS, 2, 2, 4, 16, width), low),
+            pltpu.VMEM((BLOCKS, 2, 4, 16, width), low),
+            pltpu.VMEM((BLOCKS, 2, 4, 16, width), low),
+            pltpu.VMEM((BLOCKS, 4, 4, 16, width), low),
+            pltpu.VMEM((BLOCKS, 4, 4, 16, width), low),
+            pltpu.VMEM((BLOCKS, 4, 4, 16, width), low),
+            pltpu.VMEM((BLOCKS * 4 + 1, 16, width), low),
+            pltpu.VMEM((n_dp, CAP, 16, width), low),
+            pltpu.VMEM((5,) + vec.shape, jnp.float32),
+            pltpu.VMEM((5,) + vec.shape, jnp.float32),
+            pltpu.SemaphoreType.DMA((BLOCKS,)),
+            pltpu.SemaphoreType.DMA,
+            pltpu.SemaphoreType.DMA((n_dp,)),
+            pltpu.SemaphoreType.DMA((n_dp,)),
+            pltpu.SemaphoreType.DMA((11, BLOCKS)),
+            pltpu.SemaphoreType.DMA((11, BLOCKS)),
+            pltpu.SemaphoreType.DMA((5,)),
+            pltpu.SemaphoreType.DMA((5,)),
+        ],
+        compiler_params=pltpu.CompilerParams(
+            collective_id=2, has_side_effects=True, vmem_limit_bytes=60 * 2**20
+        ),
+        cost_estimate=pl.CostEstimate(flops=0, bytes_accessed=50 * 10**6, transcendentals=0),
+        name="reduce_grads",
+    )(piece_of, vec, *far, *near)
+
+
 def gelu_pair(values):
     cdf = 0.5 * lax.erfc(values * (-(0.5**0.5)))
     density = jnp.exp(values * values * -0.5) * (0.5 / jnp.pi) ** 0.5
@@ -920,42 +1270,15 @@
     return lax.dynamic_index_in_dim(values, index, axis, keepdims=False)
 
 
-def add_low(one, two):
-    return (one.astype(jnp.float32) + two.astype(jnp.float32)).astype(jnp.bfloat16)
-
-
-def sum_all(values):
-    for axis in ("core", "y", "x", "z_near", "z_far"):
-        values = values + exchange(values, axis)
-    return values
-
-
-def halve(values, index, axis, link):
-    other = exchange(pick(values, 1 - index, axis), link)
-    return pick(values, index, axis), other
-
-
-def scatter_rows(lhs, rhs, dims, shape):
-    z, y, core, x = coordinates()
+def products(lhs, rhs, dims):
+    core = lax.axis_index("dp") % 2
     width = D // 2
-    far = lax.dynamic_slice_in_dim(rhs, (1 - core) * width, width, 1)
-    near = lax.dynamic_slice_in_dim(rhs, core * width, width, 1)
-    arrived = exchange(mm(lhs, far, dims).astype(jnp.bfloat16), "core")
-    product = (mm(lhs, near, dims) + arrived.astype(jnp.float32)).astype(jnp.bfloat16)
-    product = product.reshape(shape + (width,))
-    middle = shape[2] // 2
-    one, one_in = halve(product[:, :, :middle], x, 1, "x")
-    two, two_in = halve(product[:, :, middle:], y, 4, "y")
-    one_send = exchange(add_low(pick(one, 1 - y, 3), pick(one_in, 1 - y, 3)), "y")
-    two_send = exchange(add_low(pick(two, 1 - x, 1), pick(two_in, 1 - x, 1)), "x")
-    one = pick(one, y, 3).astype(jnp.float32) + pick(one_in, y, 3).astype(jnp.float32) + one_send.astype(jnp.float32)
-    two = pick(two, x, 1).astype(jnp.float32) + pick(two_in, x, 1).astype(jnp.float32) + two_send.astype(jnp.float32)
-    line = jnp.concatenate([one, two], axis=1).astype(jnp.bfloat16)
-    line = line.reshape(shape[0], shape[2], 2, 2, 16, width)
-    line, line_in = halve(line, z // 2, 2, "z_far")
-    last_in = exchange(add_low(pick(line, 1 - z % 2, 2), pick(line_in, 1 - z % 2, 2)), "z_near")
-    last = pick(line, z % 2, 2).astype(jnp.float32) + pick(line_in, z % 2, 2).astype(jnp.float32)
-    return (last + last_in.astype(jnp.float32)).astype(jnp.bfloat16).reshape(-1, 16, width)
+
+    def half(which):
+        columns = lax.dynamic_slice_in_dim(rhs, which * width, width, 1)
+        return mm(lhs, columns, dims).astype(jnp.bfloat16).reshape(-1, 2, 4, 4, 2, 16, width)
+
+    return half(1 - core), half(core)
 
 
 def on_device_rows(
@@ -1042,11 +1365,8 @@
     grad_two = norm_back(grad_out, normal_two, inverse_two, vectors[10])
     grad_two_low = grad_two.astype(jnp.bfloat16)
 
-    wide = (4, n_tensor, up_pieces // 4, 4, 2, 16)
-    grad_w_down = scatter_rows(hidden, grad_two_low, TN, wide)
     grad_pre32 = mm(grad_two_low, w_down, NT) * slope.astype(jnp.float32)
     grad_pre = grad_pre32.astype(jnp.bfloat16)
-    grad_w_up = scatter_rows(grad_pre, normed_low, TN, wide)
     grad_norm = grad_two + mm(grad_pre, w_up, NN)
     grad_one = norm_back(grad_norm, normal_one, inverse_one, vectors[8])
     grad_one_low = grad_one.astype(jnp.bfloat16)
@@ -1056,27 +1376,9 @@
     )
     grad_ext = jnp.where(handled[:, None], extend(grad_one_low, halo_grad), 0)
     grad_context = mm(w_out, grad_ext, NT).astype(jnp.bfloat16)
-    grad_w_out = scatter_rows(context, grad_ext, NN, (1, n_tensor, per, 4, 2, 16))
-    half_heads = (3, n_tensor, per // 2, 4, 2, 16)
-    parts = []
-    grad_w_qkv = []
-    for first in range(2):
-        part = attend_back(
-            lo, hi, qkv, grad_context, context, logs, qaug, kaug, hidden_keys, first, 2
-        )
-        parts.append(part)
-        grad_w_qkv.append(
-            scatter_rows(jnp.concatenate(part, axis=0), tokens_ext, NN, half_heads)
-        )
-    grad_w_qkv = jnp.concatenate(
-        [g.reshape(3, per // 2, 16, D // 2) for g in grad_w_qkv], axis=1
-    ).reshape(3 * per, 16, D // 2)
-
-    def whole(index):
-        pair = [part[index].reshape(n_tensor, -1, ext) for part in parts]
-        return jnp.concatenate(pair, axis=1).reshape(D, ext)
-
-    grad_q, grad_k, grad_v = whole(0), whole(1), whole(2)
+    grad_q, grad_k, grad_v = attend_back(
+        lo, hi, qkv, grad_context, context, logs, qaug, kaug, hidden_keys, 0, 1
+    )
     grad_qkv = jnp.concatenate([grad_q, grad_k, grad_v], axis=0)
     input_ext = mm(grad_qkv, w_qkv, TN)
     halo_input = lax.ppermute(halo_part(input_ext).astype(jnp.bfloat16), "tensor", swap)
@@ -1087,8 +1389,14 @@
         jnp.bfloat16
     )
 
-    early_terms = jnp.concatenate(
+    vector_terms = jnp.concatenate(
         [
+            jnp.stack(
+                [
+                    jnp.sum(grad_q.astype(jnp.float32), axis=1),
+                    jnp.sum(grad_v.astype(jnp.float32), axis=1),
+                ]
+            ),
             jnp.sum(grad_pre.astype(jnp.float32), axis=0)
             .reshape(4, n_tensor, -1)
             .transpose(1, 0, 2)
@@ -1106,23 +1414,22 @@
         ],
         axis=0,
     )
-    late_terms = jnp.stack(
-        [
-            jnp.sum(grad_q.astype(jnp.float32), axis=1),
-            jnp.sum(grad_v.astype(jnp.float32), axis=1),
-        ]
-    )
-    vector_grads = jnp.concatenate([sum_all(late_terms), sum_all(early_terms)], axis=0)
-
-    grad_chunks = jnp.concatenate([grad_w_qkv, grad_w_out, grad_w_up, grad_w_down], axis=0)
+    pairs = (
+        products(grad_qkv, tokens_ext, NN),
+        products(context, grad_ext, NN),
+        products(grad_pre, normed_low, TN),
+        products(hidden, grad_two_low, TN),
+    )
     piece_of = jnp.full((n_dp * CAP,), pieces, jnp.int32).at[slots].set(
         jnp.arange(pieces, dtype=jnp.int32)
     )
-    padded = jnp.concatenate([grad_chunks, jnp.zeros((1, 16, D // 2), jnp.bfloat16)], axis=0)
-    outgoing = jnp.take(padded, piece_of, axis=0).reshape(n_dp, CAP, 16, D // 2)
-    incoming = lax.all_to_all(outgoing, "dp", 0, 0, tiled=False)
-    own_grads = incoming.reshape(8, 2, CAP, 16, D // 2).transpose(2, 0, 3, 1, 4)
-    own_grads = own_grads.reshape(CAP, piece_rows, D).astype(jnp.float32)
+    own_grads, vector_grads = reduce_grads(
+        piece_of,
+        vector_terms,
+        [pair[0] for pair in pairs],
+        [pair[1] for pair in pairs],
+    )
+    own_grads = own_grads.astype(jnp.float32)
     slot_new, slot_first_new, slot_second_new = adam_update(
         master_slots[0], slot_first[0], slot_second[0], own_grads, rate_matrix, weight_decay
     )

time: 876 us -> 743 us (0.85); the launches traced: 879 us -> 729 us
  starting transfers between devices: 213 us -> 1.22 us
  Pallas kernels: 256 us -> 444 us
  waiting for transfers between devices: 131 us -> 23.9 us
  other arithmetic: 48.6 us -> 38.2 us
    pallas_call x0 -> x1, Pallas kernels: none -> 189 us  [reduce_grads(): pl.pallas_call(reduce_kernel, out_shape=(jax.ShapeDtypeStruct((CAP, 128,...]
    ppermute x45 -> x0, starting transfers between devices: 153 us -> none  [the longest x33 144 us: exchange(): lax.ppermute(values, 'dp', [(i, i ^ flip) for i in range(lax.axis_size('d...]
    ppermute x45 -> x0, waiting for transfers between devices: 124 us -> none  [the longest x33 93.2 us: exchange(): lax.ppermute(values, 'dp', [(i, i ^ flip) for i in range(lax.axis_size('d...]
    ppermute x1, starting transfers between devices: 43.3 us -> 0.01 us  [on_device_rows(): halo_attn = lax.ppermute(halo_part(attn_ext), 'tensor', swap)]
    pallas_call x1, Pallas kernels: 51.2 us -> 36.2 us  [attend(): pl.pallas_call(attn_fwd_kernel, out_shape=(jax.ShapeDtypeStruct((D, ext),...]
    pallas_call x2 -> x1, Pallas kernels: 57.9 us -> 72 us  [attend_back(): pl.pallas_call(attn_bwd_kernel, out_shape=(out, out, out), grid_spec=pltp...]
    all_to_all x1 -> x0, starting transfers between devices: 13.5 us -> none  [on_device_rows(): incoming = lax.all_to_all(outgoing, 'dp', 0, 0, tiled=False)]
    broadcast_in_dim x0 -> x1, other arithmetic: none -> 9.68 us  [on_device_rows(): slot_second_new[None]]
  transfers between devices with their start and end apart: 50 -> 4, of which waited for: 26 -> 2; matrix products, arithmetic and copies ran while one was open for 13% -> 6% of each run, Pallas kernels for 23% -> 46%
where the time goes in v3:
time: 743 us; the launch traced here: 729 us
  Pallas kernels  444 us (60%)
  matrix products  179 us (24%)
  local copies, waits for them, and re-layouts  39.5 us (5%)
  other arithmetic  38.2 us (5%)
  waiting for transfers between devices  23.9 us (3%)
    pallas_call x1, Pallas kernels, reduce_grads(): pl.pallas_call(reduce_kernel, out_shape=(jax.ShapeDtypeStruct((CAP, 128,...  189 us
    dot_general x16, matrix products, mm(): return lax.dot_general(a, b, dims, preferred_element_type=jnp.float32)  179 us
    pallas_call x1, Pallas kernels, gather_weights(): pl.pallas_call(gather_kernel, out_shape=(stack,) * 3, in_specs=[pl.BlockS...  147 us
    pallas_call x1, Pallas kernels, attend_back(): pl.pallas_call(attn_bwd_kernel, out_shape=(out, out, out), grid_spec=pltp...  72 us
    pallas_call x1, Pallas kernels, attend(): pl.pallas_call(attn_fwd_kernel, out_shape=(jax.ShapeDtypeStruct((D, ext),...  36.2 us
    unnamed x115, local copies, waits for them, and re-layouts  19.3 us
    ppermute x1, waiting for transfers between devices, on_device_rows(): halo_attn = lax.ppermute(halo_part(attn_ext), 'tensor', swap)  15.2 us
  transfers between devices with their start and end apart: 4, of which 2 were waited for; matrix products, arithmetic and copies ran while one was open for 6% of the time, Pallas kernels for 46%

profile of v3, /device:TPU:13, one launch (start us, length us, event | category | flops | bytes accessed | tf_op | source)
XLA Modules:
  0.0 729.0 jit_solution(2290271153384998327)
XLA Ops:
  0.6 2.1 constant_dynamic-slice_fusion.3
  2.7 1.2 collective-permute-start
  8.5 1.6 fusion.64
  12.6 2.1 convert_element_type.122
  14.8 1.2 convert_element_type.123
  16.3 146.6 %gather_weights.1 = (bf16[4,2,4,128,1024]{4,3,2,1,0:T(8,128)(2,1)S(1)}, bf16[4,2,4,128,1024]{4,3,2,1,0:T(8,128)(2,1)S(1)}, bf16[4,2,4,128,1024]{4,3,2,1,0:T(8,128)(2,1)}) custom-call(s32[48]{0:T(128)S(1)} %multiply_add_fusion.3.slots_ref, bf16[16,6,16,512]{3,2,1,0:T(8,128)(2,1)S(1)} %bitcast.102), custom_call_target="tpu_custom_call" | custom-call | bytes 50000000 | tf_op jit(solution)/shard_map/gather_weights/pallas_call | solution.py:887
  162.9 3.3 copy-done.6
  166.2 3.5 slice.35
  169.7 1.5 slice.38
  171.9 1.4 constant_dynamic-update-slice_fusion.8
  173.6 1.7 copy-done.23
  175.3 11.8 %multiply_convert_fusion.q_ref.k_ref.v_ref = bf16[3072,1536]{1,0:T(8,128)(2,1)S(1)} fusion(bf16[3072,1024]{1,0:T(8,128)(2,1)S(1)} %bitcast.107, bf16[1536,1024]{1,0:T(8,128)(2,1)} %copy-done.23, f32[3072]{0:T(1024)S(1)} %copy-done.45, f32[3072]{0:T(1024)S(1)} %pad_maximum_fusion), kind=kOutput, calls=%fused_computation.2 | convolution fusion | flops 9677832192 | bytes 18898944 | tf_op jit(solution)/shard_map/dot_general | solution.py:347
  187.1 36.2 %attend.1 = (bf16[1024,1536]{1,0:T(8,128)(2,1)S(1)}, f32[2,8,1536]{2,1,0:T(8,128)S(1)}) custom-call(s32[6]{0:T(128)S(1)} %get-tuple-element.73.lo_ref, s32[6]{0:T(128)S(1)} %get-tuple-element.72.hi_ref, bf16[3072,1536]{1,0:T(8,128)(2,1)S(1)} %multiply_convert_fusion.q_ref.k_ref.v_ref, bf16[3072,1536]{1,0:T(8,128)(2,1)S(1)} %multiply_convert_fusion.q_ref.k_ref.v_ref, ...), custom_call_target="tpu_custom_call" | custom-call | flops 20000000000 | bytes 14000000 | tf_op jit(solution)/shard_map/attend/pallas_call | solution.py:504
  223.3 4.0 convolution_convert_fusion.7
  227.3 1.1 constant_dynamic-slice_fusion.1
  230.1 1.3 scatter_custom_fusion.piece_ref
  231.4 15.2 %collective-permute-done.1 = bf16[400,1024]{1,0:T(8,128)(2,1)S(1)} collective-permute-done((bf16[400,1024]{1,0:T(8,128)(2,1)}, bf16[400,1024]{1,0:T(8,128)(2,1)S(1)}, u32[]{:S(2)}, u32[]{:S(2)}) %collective-permute-start.1) | collective-permute-done | bytes 819232 | tf_op jit(solution)/shard_map/ppermute | solution.py:1348
  247.0 1.7 fusion.16
  249.9 1.5 fusion.15
  251.8 46.7 %multiply_convert_fusion.2 = (bf16[1024,4096]{1,0:T(8,128)(2,1)S(1)}, f32[1024,4096]{1,0:T(8,128)}, f32[1024,4096]{1,0:T(8,128)}) fusion(f32[4096]{0:T(1024)S(1)} %bitcast.145, bf16[1024,1024]{1,0:T(8,128)(2,1)S(1)} %fusion.15, bf16[4096,1024]{1,0:T(8,128)(2,1)S(1)} %bitcast.106), kind=kOutput, calls=%fused_computation.8 | convolution fusion | flops 8862564352 | bytes 52445184 | tf_op jit(solution)/shard_map/dot_general | solution.py:347
  298.6 9.4 %fusion.65 = (f32[1024]{0:T(1024)S(1)}, f32[1024,1024]{1,0:T(8,128)S(1)}) fusion(f32[1024]{0:T(1024)S(1)} %bitcast.153, bf16[1024,4096]{1,0:T(8,128)(2,1)S(1)} %get-tuple-element.49, bf16[4096,1024]{1,0:T(8,128)(2,1)S(1)} %bitcast.159, f32[1024]{0:T(1024)S(1)} %bitcast.150, f32[1024]{0:T(1024)S(1)} %bitcast.135, f32[1024]{0:T(1024)S(1)} %add_rsqrt_fusion.1, ...), kind=kOutput, calls=%fused_computation.165 | convolution fusion | flops 8601467904 | bytes 25194496 | tf_op jit(solution)/shard_map/dot_general | solution.py:347
  309.6 2.8 fusion.14
  312.5 3.6 fusion.59
  316.1 2.0 copy-done.16
  318.4 6.3 convolution_convert_fusion.2
  324.7 22.8 %convert_reduce_fusion = (f32[4096]{0:T(1024)S(1)}, bf16[1024,4096]{1,0:T(8,128)(2,1)}) fusion(f32[1024,4096]{1,0:T(8,128)} %get-tuple-element.50, f32[1024,4096]{1,0:T(8,128)} %get-tuple-element.74, f32[4096]{0:T(1024)S(1)} %bitcast.146, bf16[1024,1024]{1,0:T(8,128)(2,1)} %copy-done.27, bf16[4096,1024]{1,0:T(8,128)(2,1)} %bitcast.156), kind=kOutput, calls=%fused_computation.5 | convolution fusion | flops 8640262144 | bytes 52461568 | tf_op jit(solution)/shard_map/dot_general | solution.py:347
  347.5 17.9 %multiply_reduce_fusion = (f32[1024]{0:T(1024)S(1)}, f32[1024]{0:T(1024)S(1)}, f32[1024]{0:T(1024)S(1)}, f32[1024]{0:T(1024)S(1)}, f32[1024,1024]{1,0:T(8,128)S(1)}) fusion(f32[1024]{0:T(1024)S(1)} %add_rsqrt_fusion.1, f32[1024]{0:T(1024)S(1)} %broadcast_multiply_fusion.5, f32[1024]{0:T(1024)S(1)} %bitcast.127, bf16[1024,1024]{1,0:T(8,128)(2,1)} %copy-done.14, ...), kind=kOutput, calls=%fused_computation.42 | convolution fusion | flops 8604610560 | bytes 29392896 | tf_op jit(solution)/shard_map/dot_general | solution.py:347
  365.5 10.0 %convolution_convert_fusion.3 = bf16[4096,512]{1,0:T(8,128)(2,1)} fusion(bf16[1024,4096]{1,0:T(8,128)(2,1)} %get-tuple-element.79, bf16[1024,1024]{1,0:T(8,128)(2,1)S(1)} %copy-done.32, s32[]{:T(128)S(6)} %select_n.145), kind=kOutput, calls=%fused_computation.30 | convolution fusion | flops 4297064448 | bytes 13631492 | tf_op jit(solution)/shard_map/dot_general | solution.py:347
  375.4 6.6 convolution_convert_fusion
  382.0 2.1 fusion.61
  384.1 2.1 copy-done.10
  387.6 9.7 %convolution_convert_fusion.1 = bf16[4096,512]{1,0:T(8,128)(2,1)} fusion(bf16[1024,4096]{1,0:T(8,128)(2,1)} %get-tuple-element.79, bf16[1024,1024]{1,0:T(8,128)(2,1)S(1)} %copy-done.33, s32[]{:T(128)S(6)} %select_n.146), kind=kOutput, calls=%fused_computation.28 | convolution fusion | flops 4297064448 | bytes 13631492 | tf_op jit(solution)/shard_map/dot_general | solution.py:347
  397.3 8.6 %collective-permute-done.2 = bf16[400,1024]{1,0:T(8,128)(2,1)S(1)} collective-permute-done((bf16[400,1024]{1,0:T(8,128)(2,1)}, bf16[400,1024]{1,0:T(8,128)(2,1)S(1)}, u32[]{:S(2)}, u32[]{:S(2)}) %collective-permute-start.2) | collective-permute-done | bytes 819232 | tf_op jit(solution)/shard_map/ppermute | solution.py:1374
  408.9 2.8 fusion.32
  411.7 2.8 fusion.29
  414.5 4.8 convolution_convert_fusion.6.g_ref
  419.3 72.0 %attend_back.1 = (bf16[1024,1536]{1,0:T(8,128)(2,1)S(1)}, bf16[1024,1536]{1,0:T(8,128)(2,1)}, bf16[1024,1536]{1,0:T(8,128)(2,1)}) custom-call(s32[6]{0:T(128)S(1)} %get-tuple-element.73.lo_ref, s32[6]{0:T(128)S(1)} %get-tuple-element.72.hi_ref, bf16[3072,1536]{1,0:T(8,128)(2,1)} %copy-done.9, bf16[3072,1536]{1,0:T(8,128)(2,1)} %copy-done.9, ...), custom_call_target="tpu_custom_call" | custom-call | flops 49999998976 | bytes 30000000 | tf_op jit(solution)/shard_map/attend_back/pallas_call | solution.py:547
  491.5 1.7 copy-done.22
  494.4 1.1 copy-done.24
  495.5 6.4 convolution_convert_fusion.5
  501.9 6.6 convolution_convert_fusion.4
  509.5 10.5 %fusion.66 = f32[1536,1024]{1,0:T(8,128)S(1)} fusion(bf16[3072,1536]{1,0:T(8,128)(2,1)S(1)} %constant_dynamic-update-slice_fusion, bf16[3072,1024]{1,0:T(8,128)(2,1)S(1)} %bitcast.110), kind=kOutput, calls=%fused_computation.166 | convolution fusion | flops 9663676416 | bytes 22020096 | tf_op jit(solution)/shard_map/dot_general | solution.py:347
  520.0 2.7 copy-done.21
  523.7 1.3 concatenate.19.vec_ref
  525.0 189.3 %reduce_grads.1 = (bf16[6,128,1024]{2,1,0:T(8,128)(2,1)}, f32[12,1024]{1,0:T(8,128)}) custom-call(s32[96]{0:T(128)} %scatter_custom_fusion.piece_ref, f32[12,1024]{1,0:T(8,128)} %concatenate.19.vec_ref, bf16[3,2,4,4,2,16,512]{6,5,4,3,2,1,0:T(8,128)(2,1)} %bitcast.117, bf16[1,2,4,4,2,16,512]{6,5,4,3,2,1,0:T(8,128)(2,1)} %bitcast.122, ...), custom_call_target="tpu_custom_call" | custom-call | bytes 50000000 | tf_op jit(solution)/shard_map/reduce_grads/pallas_call | solution.py:1212
  714.4 1.6 multiply_subtract_fusion
  715.9 9.7 %fusion.22 = (f32[1,6,128,1024]{3,2,1,0:T(8,128)}, f32[1,6,128,1024]{3,2,1,0:T(8,128)}, f32[1,6,128,1024]{3,2,1,0:T(8,128)}) fusion(bf16[6,128,1024]{2,1,0:T(8,128)(2,1)} %get-tuple-element.26, f32[1,6,128,1024]{3,2,1,0:T(8,128)} %param.17, f32[1,6,128,1024]{3,2,1,0:T(8,128)} %param.16, f32[1,6,128,1024]{3,2,1,0:T(8,128)S(1)} %copy-done.17), kind=kLoop, calls=%fused_computation.70 | loop fusion | flops 11796480 | bytes 20447232 | tf_op jit(solution)/shard_map/broadcast_in_dim | solution.py:1444
  726.0 2.7 add_convert_fusion.1
  (177 shorter events, 20.6 us)
Async XLA Ops:
  2.7 168.7 %collective-permute-start = (bf16[400,1024]{1,0:T(8,128)(2,1)}, bf16[400,1024]{1,0:T(8,128)(2,1)}, u32[]{:S(2)}, u32[]{:S(2)}) collective-permute-start(bf16[400,1024]{1,0:T(8,128)(2,1)} %constant_dynamic-slice_fusion.3), channel_id=1, source_target_pairs={{0,1},{1,0},{2,3},{3,2},{4,5},{5,4},{6,7},{7,6},{8,9},{9,8},{10,11... | collective-permute-start | bytes 2457608 | tf_op jit(solution)/shard_map/ppermute | solution.py:1323
  8.4 4.2 copy-start.37
  162.9 3.3 copy-start.6
  169.7 3.6 copy-start.13
  171.4 15.7 %copy-start.2 = (bf16[16,1536]{1,0:T(8,128)(2,1)}, bf16[16,1536]{1,0:T(8,128)(2,1)S(1)}, u32[]{:S(2)}) copy-start(bf16[16,1536]{1,0:T(8,128)(2,1)S(1)} %get-tuple-element.70.kaug_ref) | copy-start | bytes 147460
  171.4 15.7 %copy-start.4 = (bf16[16,1536]{1,0:T(8,128)(2,1)}, bf16[16,1536]{1,0:T(8,128)(2,1)S(1)}, u32[]{:S(2)}) copy-start(bf16[16,1536]{1,0:T(8,128)(2,1)S(1)} %get-tuple-element.71.qaug_ref) | copy-start | bytes 147460
  171.5 3.8 copy-start.20
  171.5 3.8 copy-start.45
  187.1 36.2 %copy-start.9 = (bf16[3072,1536]{1,0:T(8,128)(2,1)}, bf16[3072,1536]{1,0:T(8,128)(2,1)S(1)}, u32[]{:S(2)}) copy-start(bf16[3072,1536]{1,0:T(8,128)(2,1)S(1)} %multiply_convert_fusion.q_ref.k_ref.v_ref) | copy-start | bytes 28311556
  187.1 36.2 %copy-start = (f32[8,1536]{1,0:T(8,128)}, f32[8,1536]{1,0:T(8,128)S(1)}, u32[]{:S(2)}) copy-start(f32[8,1536]{1,0:T(8,128)S(1)} %broadcast_in_dim.141.hid_ref) | copy-start | bytes 147460
  187.1 36.2 %copy-start.29 = (bf16[1,2,4,128,1024]{4,3,2,1,0:T(8,128)(2,1)S(1)}, bf16[1,2,4,128,1024]{4,3,2,1,0:T(8,128)(2,1)}, u32[]{:S(2)}) copy-start(bf16[1,2,4,128,1024]{4,3,2,1,0:T(8,128)(2,1)} %slice.38) | copy-start | bytes 6291460
  223.3 4.0 copy-start.7
  223.3 6.8 copy-start.44
  229.3 17.4 %collective-permute-start.1 = (bf16[400,1024]{1,0:T(8,128)(2,1)}, bf16[400,1024]{1,0:T(8,128)(2,1)S(1)}, u32[]{:S(2)}, u32[]{:S(2)}) collective-permute-start(bf16[400,1024]{1,0:T(8,128)(2,1)} %constant_dynamic-slice_fusion.1), channel_id=1, source_target_pairs={{0,1},{1,0},{2,3},{3,2},{4,5},{5,4},{6,7},{7,6},{8,9},{9,8},{10,11... | collective-permute-start | bytes 2457608 | tf_op jit(solution)/shard_map/ppermute | solution.py:1348
  231.4 15.6 %copy-start.26 = (bf16[1536,1024]{1,0:T(8,128)(2,1)S(1)}, bf16[1536,1024]{1,0:T(8,128)(2,1)}, u32[]{:S(2)}) copy-start(bf16[1536,1024]{1,0:T(8,128)(2,1)} %copy-done.25) | copy-start | bytes 9437188
  247.0 4.4 slice-start
  248.8 49.8 %copy-start.14 = (bf16[1024,1024]{1,0:T(8,128)(2,1)}, bf16[1024,1024]{1,0:T(8,128)(2,1)S(1)}, u32[]{:S(2)}) copy-start(bf16[1024,1024]{1,0:T(8,128)(2,1)S(1)} %get-tuple-element.52) | copy-start | bytes 6291460
  248.8 3.0 slice-start.1
  249.9 48.7 %slice-start.6 = ((s8[8388608]{0:T(1024)(128)(4,1)}), s8[4194304]{0:T(1024)(128)(4,1)S(1)}, s32[]{:S(2)}) async-start(s8[8388608]{0:T(1024)(128)(4,1)} %bitcast.157), calls=%async_computation.6 | async-start | bytes 8388608
  251.4 47.1 %copy-start.31 = (bf16[1024,1024]{1,0:T(8,128)(2,1)}, bf16[1024,1024]{1,0:T(8,128)(2,1)S(1)}, u32[]{:S(2)}) copy-start(bf16[1024,1024]{1,0:T(8,128)(2,1)S(1)} %fusion.15) | copy-start | bytes 6291460
  251.8 46.7 %copy-start.43 = (f32[1,1024]{1,0:T(1,128)S(1)}, f32[1,1024]{1,0:T(1,128)}, u32[]{:S(2)}) copy-start(f32[1,1024]{1,0:T(1,128)} %get-tuple-element.61) | copy-start | bytes 12292
  251.8 46.7 %slice-start.7 = ((s8[8388608]{0:T(1024)(128)(4,1)}), s8[4194304]{0:T(1024)(128)(4,1)S(1)}, s32[]{:S(2)}) async-start(s8[8388608]{0:T(1024)(128)(4,1)} %bitcast.157), calls=%async_computation.7 | async-start | bytes 8388608
  298.5 19.8 %copy-start.46 = (bf16[1024,4096]{1,0:T(8,128)(2,1)}, bf16[1024,4096]{1,0:T(8,128)(2,1)S(1)}, u32[]{:S(2)}) copy-start(bf16[1024,4096]{1,0:T(8,128)(2,1)S(1)} %get-tuple-element.49) | copy-start | bytes 25165828
  308.6 3.8 copy-start.39
  318.4 6.3 copy-start.27
  347.5 17.9 %copy-start.32 = (bf16[1024,1024]{1,0:T(8,128)(2,1)S(1)}, bf16[1024,1024]{1,0:T(8,128)(2,1)}, u32[]{:S(2)}) copy-start(bf16[1024,1024]{1,0:T(8,128)(2,1)} %copy-done.31) | copy-start | bytes 6291460
  365.4 10.0 %copy-start.28 = (bf16[1024,1024]{1,0:T(8,128)(2,1)S(1)}, bf16[1024,1024]{1,0:T(8,128)(2,1)}, u32[]{:S(2)}) copy-start(bf16[1024,1024]{1,0:T(8,128)(2,1)} %copy-done.27) | copy-start | bytes 6291460
  365.5 10.0 %copy-start.47 = (bf16[1024,4096]{1,0:T(8,128)(2,1)S(1)}, bf16[1024,4096]{1,0:T(8,128)(2,1)}, u32[]{:S(2)}) copy-start(bf16[1024,4096]{1,0:T(8,128)(2,1)} %copy-done.46) | copy-start | bytes 25165828
  375.4 6.6 copy-start.15
  384.1 3.5 copy-start.33
  387.5 18.4 %collective-permute-start.2 = (bf16[400,1024]{1,0:T(8,128)(2,1)}, bf16[400,1024]{1,0:T(8,128)(2,1)S(1)}, u32[]{:S(2)}, u32[]{:S(2)}) collective-permute-start(bf16[400,1024]{1,0:T(8,128)(2,1)} %constant_dynamic-slice_fusion), channel_id=1, source_target_pairs={{0,1},{1,0},{2,3},{3,2},{4,5},{5,4},{6,7},{7,6},{8,9},{9,8},{10,11... | collective-permute-start | bytes 2457608 | tf_op jit(solution)/shard_map/ppermute | solution.py:1374
  397.3 9.1 %copy-start.11 = (f32[1024,1024]{1,0:T(8,128)S(1)}, f32[1024,1024]{1,0:T(8,128)}, u32[]{:S(2)}) copy-start(f32[1024,1024]{1,0:T(8,128)} %copy-done.10) | copy-start | bytes 12582916
  411.7 2.8 copy-start.30
  414.5 4.9 copy-start.1
  414.5 4.9 copy-start.3
  414.5 4.9 copy-start.5
  495.5 14.0 %slice-start.2 = ((s8[6291456]{0:T(1024)(128)(4,1)}), s8[4194304]{0:T(1024)(128)(4,1)S(1)}, s32[]{:S(2)}) async-start(s8[6291456]{0:T(1024)(128)(4,1)} %bitcast.108), calls=%async_computation.2 | async-start | bytes 8388608
  501.9 7.6 %slice-start.3 = ((s8[6291456]{0:T(1024)(128)(4,1)}), s8[2097152]{0:T(1024)(128)(4,1)S(1)}, s32[]{:S(2)}) async-start(s8[6291456]{0:T(1024)(128)(4,1)} %bitcast.108), calls=%async_computation.3 | async-start | bytes 4194304
  509.5 14.2 %copy-start.40 = (f32[1024]{0:T(1024)S(1)}, f32[1024]{0:T(1024)}, u32[]{:S(2)}) copy-start(f32[1024]{0:T(1024)} %get-tuple-element.45) | copy-start | bytes 12292
  509.5 14.2 %copy-start.41 = (f32[1024]{0:T(1024)S(1)}, f32[1024]{0:T(1024)}, u32[]{:S(2)}) copy-start(f32[1024]{0:T(1024)} %get-tuple-element.30) | copy-start | bytes 12292
  509.5 14.2 %copy-start.42 = (f32[1024]{0:T(1024)S(1)}, f32[1024]{0:T(1024)}, u32[]{:S(2)}) copy-start(f32[1024]{0:T(1024)} %get-tuple-element.35) | copy-start | bytes 12292
  523.7 201.9 %collective-permute-start.3 = (bf16[400,1024]{1,0:T(8,128)(2,1)}, bf16[400,1024]{1,0:T(8,128)(2,1)S(1)}, u32[]{:S(2)}, u32[]{:S(2)}) collective-permute-start(bf16[400,1024]{1,0:T(8,128)(2,1)} %dynamic-slice_convert_fusion), channel_id=1, source_target_pairs={{0,1},{1,0},{2,3},{3,2},{4,5},{5,4},{6,7},{7,6},{8,9},{9,8},{10,11... | collective-permute-start | bytes 2457608 | tf_op jit(solution)/shard_map/ppermute | solution.py:1384
  525.0 189.3 %copy-start.34 = (f32[12,1024]{1,0:T(8,128)S(1)}, f32[12,1024]{1,0:T(8,128)}, u32[]{:S(2)}) copy-start(f32[12,1024]{1,0:T(8,128)} %param.18) | copy-start | bytes 147460
  525.0 189.3 %copy-start.35 = (f32[12,1024]{1,0:T(8,128)S(1)}, f32[12,1024]{1,0:T(8,128)}, u32[]{:S(2)}) copy-start(f32[12,1024]{1,0:T(8,128)} %param.19) | copy-start | bytes 147460
  525.0 190.9 %copy-start.17 = (f32[1,6,128,1024]{3,2,1,0:T(8,128)S(1)}, f32[1,6,128,1024]{3,2,1,0:T(8,128)}, u32[]{:S(2)}) copy-start(f32[1,6,128,1024]{3,2,1,0:T(8,128)} %param.15) | copy-start | bytes 9437188
  715.9 10.0 %slice-start.4 = ((s8[6291456]{0:T(1024)(128)(4,1)}), s8[4194304]{0:T(1024)(128)(4,1)S(1)}, s32[]{:S(2)}) async-start(s8[6291456]{0:T(1024)(128)(4,1)} %bitcast.115), calls=%async_computation.4 | async-start | bytes 8388608
  715.9 10.0 %copy-start.12 = (f32[1024,1024]{1,0:T(8,128)S(1)}, f32[1024,1024]{1,0:T(8,128)}, u32[]{:S(2)}) copy-start(f32[1024,1024]{1,0:T(8,128)} %copy-done.10) | copy-start | bytes 12582916
  715.9 10.1 %slice-start.5 = ((s8[6291456]{0:T(1024)(128)(4,1)}), s8[2097152]{0:T(1024)(128)(4,1)S(1)}, s32[]{:S(2)}) async-start(s8[6291456]{0:T(1024)(128)(4,1)} %bitcast.115), calls=%async_computation.5 | async-start | bytes 4194304
  (12 other events, 22.8 us)
